TPU v7x, 256 devices: a whole 4x4x8 slice. The times are simulated.
256 devices in a mesh: dp: 16 (over y, z_lo, core), tensor: 16 (over x, z_hi).
Axes of the slice: x: 4, y: 4, z: 8 (z_hi: 4, z_lo: 2; z = z_hi * 2 + z_lo), core: 2. Of those that a mesh axis runs over, the one named last changes fastest.
Arguments:
- ssm_input: bfloat16 [128, 64, 8192], P('dp', None, 'tensor'), may hold values from -6 to 6
- gate_input: bfloat16 [128, 64, 8192], P('dp', None, 'tensor'), may hold values from -6 to 6
- write_basis: bfloat16 [128, 64, 4, 128], P('dp'), may hold values from -4 to 4
- read_basis: bfloat16 [128, 64, 4, 128], P('dp'), may hold values from -4 to 4
- step_raw: float32 [128, 128, 64], P('dp', 'tensor'), may hold values from -4 to 4
- step_bias: float32 [128], P('tensor'), may hold values from -1 to 1
- decay_rate: float32 [128], P('tensor'), may hold values from 0.003 to 0.12
- skip_gain: float32 [128], P('tensor'), may hold values from 0.5 to 1.5
- norm_gain: float32 [8192], P('tensor'), may hold values from 0.1 to 1.9
- out_weight: bfloat16 [8192, 8192], P('tensor'), may hold values from -0.09375 to 0.09375
- ssm_states: bfloat16 [128, 128, 64, 128], P('dp', 'tensor'), may hold values from -6 to 6
- anchor: int32 [128], replicated, may hold values from 0 to 127, as said below
- tool_length: int32 [128], P('dp'), may hold values from 1 to 64, 4096 in all
Outputs:
- layer_out: bfloat16 [128, 64, 8192], P('dp', None, 'tensor')
- new_states: bfloat16 [128, 128, 64, 128], P('dp', 'tensor')
Inputs may be any that keep to these rules, and one draw needn't show every extreme that they name: anchor is a permutation of 0 .. 127; row i lies in group i // 8 and takes over row anchor[i] of group anchor[i] // 8. From one group to another different group at most 2 rows move, and at most 4 rows leave one group; both bounds are reached in every draw.
All inputs are finite; a program needn't handle non-finite values. No bound on the sum of `tool_length` on one device may be relied on, other than what follows from the above.
Results may differ from a plain program's by a relative error of at most 0.0049.
Values may be sent and summed in bfloat16 or wider, within the bound.
No kernel may reach another device: no remote copies, remote signals or barrier semaphores. Data moves between devices by JAX's collectives and lax.ppermute only.
A program may use at most 128 MiB of HBM per device.

v0:
```python
import jax
import jax.numpy as jnp
from jax import lax
from jax.sharding import PartitionSpec as P

HEADS = 128
NGROUPS = 4


def route_tables(anchor, row_count):
    row_total = anchor.shape[0]
    global_ids = jnp.arange(row_total, dtype=jnp.int32)
    dest_group = global_ids // row_count
    source_group = anchor // row_count
    source_row = anchor % row_count
    moving = source_group != dest_group
    earlier = global_ids[None, :] < global_ids[:, None]
    return (dest_group, source_group, source_row, moving, earlier)


def gather_rows(states_here, wanted, source_row):
    picked = jnp.sum(jnp.where(wanted, source_row[None, :], 0), axis=1)
    filled = jnp.any(wanted, axis=1)
    rows_out = states_here[picked]
    return jnp.where(filled[:, None, None, None], rows_out, jnp.zeros((), states_here.dtype))


def local(
    ssm_input,
    gate_input,
    write_basis,
    read_basis,
    step_raw,
    step_bias,
    decay_rate,
    skip_gain,
    norm_gain,
    out_weight,
    ssm_states,
    anchor,
    tool_length,
):
    row_count, new_len, inner_dev = ssm_input.shape
    heads_dev = step_raw.shape[1]
    head_dim = ssm_states.shape[2]
    my_group = lax.axis_index("dp")
    dest_group, source_group, source_row, moving, earlier = route_tables(anchor, row_count)
    same_source = moving[None, :] & (source_group[None, :] == source_group[:, None]) & earlier
    outgoing = moving & (source_group == my_group)
    my_start = my_group * row_count
    mine_source = lax.dynamic_slice_in_dim(source_group, my_start, row_count)
    mine_row = lax.dynamic_slice_in_dim(source_row, my_start, row_count)
    mine_moving = lax.dynamic_slice_in_dim(moving, my_start, row_count)
    staying = ssm_states[mine_row]
    send_cap = row_count // 2
    send_order = jnp.sum(same_source.astype(jnp.int32), axis=1)
    slot_ids = jnp.arange(send_cap, dtype=jnp.int32)
    wanted = outgoing[None, :] & (send_order[None, :] == slot_ids[:, None])
    outbound = gather_rows(ssm_states, wanted, source_row)
    arrived = lax.all_gather(outbound, "dp", axis=0, tiled=True)
    arrive_index = mine_source * send_cap + lax.dynamic_slice_in_dim(
        send_order, my_start, row_count
    )
    start_state = jnp.where(mine_moving[:, None, None, None], arrived[arrive_index], staying)
    tensor_rank = lax.axis_index("tensor")
    group_heads = HEADS // NGROUPS
    head_group = tensor_rank * heads_dev // group_heads
    write_mine = lax.dynamic_index_in_dim(write_basis, head_group, 2, keepdims=False)
    read_mine = lax.dynamic_index_in_dim(read_basis, head_group, 2, keepdims=False)
    positions = jnp.arange(new_len, dtype=jnp.int32)
    live_mask = (positions[None, :] < tool_length[:, None]).astype(jnp.float32)
    step_size = jax.nn.softplus(step_raw + step_bias[None, :, None]) * live_mask[:, None, :]
    decay_sum = jnp.cumsum(-decay_rate[None, :, None] * step_size, axis=2)
    causal = positions[None, :] <= positions[:, None]
    spread = decay_sum[:, :, :, None] - decay_sum[:, :, None, :]
    segment = jnp.where(causal, jnp.exp(jnp.where(causal, spread, 0.0)), 0.0)
    affinity = jnp.einsum("rtn,rsn->rts", read_mine, write_mine, preferred_element_type=jnp.float32)
    mixing = affinity[:, None] * segment * step_size[:, :, None, :]
    input_heads = ssm_input.reshape(row_count, new_len, heads_dev, head_dim).astype(jnp.float32)
    within_block = jnp.einsum(
        "rhts,rshp->rthp", mixing, input_heads, precision=lax.Precision.HIGHEST
    )
    start_float = start_state.astype(jnp.float32)
    read_float = read_mine.astype(jnp.float32)
    carried = jnp.einsum("rhpn,rtn->rthp", start_float, read_float, precision=lax.Precision.HIGHEST)
    carried = carried * jnp.exp(decay_sum).transpose(0, 2, 1)[..., None]
    outputs = (within_block + carried + skip_gain[None, None, :, None] * input_heads) * live_mask[
        :, :, None, None
    ]
    tail_weight = jnp.exp(decay_sum[:, :, -1:] - decay_sum) * step_size
    weighted_input = input_heads * tail_weight.transpose(0, 2, 1)[..., None]
    final_state = jnp.exp(decay_sum[:, :, -1])[:, :, None, None] * start_float + jnp.einsum(
        "rshp,rsn->rhpn",
        weighted_input,
        write_mine.astype(jnp.float32),
        precision=lax.Precision.HIGHEST,
    )
    gate_heads = gate_input.reshape(row_count, new_len, heads_dev, head_dim).astype(jnp.float32)
    gated = outputs * jax.nn.silu(gate_heads)
    local_square = jnp.sum(gated * gated, axis=(2, 3))
    selector = (jnp.arange(NGROUPS, dtype=jnp.int32) == head_group).astype(jnp.float32)
    summed = lax.psum(local_square[:, :, None] * selector, "tensor")
    square_sum = lax.dynamic_index_in_dim(summed, head_group, 2, keepdims=False)
    mean_square = square_sum / (group_heads * head_dim)
    scale_rows = lax.rsqrt(mean_square + 1e-05)[:, :, None, None]
    normed = (gated * scale_rows * norm_gain.reshape(heads_dev, head_dim)).astype(jnp.bfloat16)
    flat_normed = normed.reshape(row_count * new_len, inner_dev)
    partial_value = jnp.dot(flat_normed, out_weight, preferred_element_type=jnp.float32)
    reduced = lax.psum_scatter(partial_value, "tensor", scatter_dimension=1, tiled=True)
    layer_out = reduced.astype(jnp.bfloat16).reshape(row_count, new_len, -1)
    return (layer_out, final_state.astype(jnp.bfloat16))


def solution(mesh):
    placed = (
        P("dp", None, "tensor"),
        P("dp", None, "tensor"),
        P("dp", None, None, None),
        P("dp", None, None, None),
        P("dp", "tensor", None),
        P("tensor"),
        P("tensor"),
        P("tensor"),
        P("tensor"),
        P("tensor", None),
        P("dp", "tensor", None, None),
        P(),
        P("dp"),
    )
    return jax.shard_map(
        local,
        mesh=mesh,
        in_specs=placed,
        out_specs=(P("dp", None, "tensor"), P("dp", "tensor", None, None)),
        check_vma=False,
    )
```

profile of v0, /device:TPU:12, one launch (start us, length us, event | category | flops | bytes accessed | tf_op | source)
XLA Modules:
  0.0 385.6 jit_solution(9477484666739780135)
XLA Ops:
  7.2 0.0 copy-start
  7.2 0.0 copy-start.10
  7.2 0.0 copy-start.6
  7.2 0.0 all-gather.2.cloned.1.call-start
  7.3 0.7 and_select_fusion
  8.0 0.7 compare_and_fusion
  8.7 0.2 convert_reduce_fusion
  8.8 0.1 fusion.31
  9.0 0.1 select_reduce_fusion
  9.1 0.6 gather_fusion
  9.8 0.0 copy-start.4
  9.8 0.9 broadcast_select_fusion.1
  10.7 0.0 all-gather.2.cloned.1.call-update
  10.7 0.0 reduce-scatter.2.cloned.1.call-start
  10.8 0.6 dynamic_slice.25
  11.4 0.0 copy-done.6
  11.4 0.1 mul.150
  11.5 0.1 compare_select_fusion.1
  11.6 1.7 gather_fusion.2
  13.3 1.3 copy.29
  14.6 1.4 copy.30
  16.0 0.1 fusion.29
  16.1 0.1 broadcast_multiply_fusion
  16.2 1.8 reduce_window_sum.11
  18.0 0.6 compare_convert_fusion
  18.6 0.1 compare_select_fusion.2
  18.7 0.2 slice_reduce_fusion
  18.8 1.8 constant_dynamic-slice_fusion
  20.7 0.1 multiply_bitcast_fusion
  20.7 0.6 copy-done.3
  21.4 0.2 fusion.20
  21.6 5.1 %fusion.4 = f32[8,8,64,64]{2,3,1,0:T(8,128)} fusion(bf16[8,64,8,64]{1,3,2,0:T(8,128)(2,1)} %bitcast.41, f32[8,8,64]{2,1,0:T(8,128)S(1)} %get-tuple-element.6, f32[8,8,64]{2,1,0:T(8,128)S(1)} %reduce_window_sum.11, f32[8,64,64]{2,1,0:T(8,128)S(1)} %fusion.20, pred[64,64]{1,0:T(8,128)(4,1)S(1)} %iota_compare_fusion.1), kind=kOutput, calls=%fused_computation.13 | convolution fusion | flops 202637312 | bytes 1740800 | tf_op jit(solution)/shard_map/rhts,rshp->rthp/dot_general | solution.py:80
  26.7 41.6 %all-gather.2.cloned.1.call-done = bf16[64,8,64,128]{3,2,1,0:T(8,128)(2,1)} async-done(((bf16[4,8,64,128]{3,2,1,0:T(8,128)(2,1)}), bf16[64,8,64,128]{3,2,1,0:T(8,128)(2,1)}) %all-gather.2.cloned.1.call-update) | async-done | bytes 8388624 | tf_op jit(solution)/shard_map/all_gather | solution.py:60
  68.3 5.0 %gather_fusion.1 = bf16[8,8,64,128]{3,2,1,0:T(8,128)(2,1)} fusion(bf16[64,8,64,128]{3,2,1,0:T(8,128)(2,1)} %all-gather.2.cloned.1.call-done, s32[1024]{0:T(1024)S(1)} %pad_clamp_fusion.1), kind=kCustom, calls=%fused_computation.1 | custom fusion | bytes 2097184 | tf_op jit(solution)/shard_map/gather | solution.py:64
  73.3 0.0 copy-done.11
  73.3 5.4 %multiply_reduce_fusion = (f32[8,64]{1,0:T(8,128)S(1)}, f32[8,64,8,64]{1,3,2,0:T(8,128)}) fusion(f32[8,64,8,64]{1,3,2,0:T(8,128)S(1)} %bitcast.40, f32[8,64]{1,0:T(8,128)S(1)} %fusion.29, bf16[8,64,8,64]{1,3,2,0:T(8,128)(2,1)} %bitcast.42, f32[8]{0:T(128)S(1)} %copy-done.11, f32[8,64,8]{1,2,0:T(8,128)S(1)} %get-tuple-element.8, ...), kind=kOutput, calls=%fused_computation.12 | convolution fusion | flops 71040512 | bytes 5918760 | tf_op jit(solution)/shard_map/rhpn,rtn->rthp/dot_general | solution.py:85
  78.7 0.1 broadcast_multiply_fusion.1
  78.8 72.0 %psum.7 = f32[8,64,4]{1,0,2:T(8,128)S(1)} all-reduce(f32[8,64,4]{1,0,2:T(8,128)S(1)} %broadcast_multiply_fusion.1), channel_id=1, replica_groups=mesh['dp'=16,'tensor'=16] {'tensor'}, use_global_device_ids=true, to_apply=%region_5.6 | all-reduce | flops 2048 | bytes 16384 | tf_op jit(solution)/shard_map/psum | solution.py:102
  150.8 2.0 multiply_convert_fusion
  152.8 0.7 copy.31
  153.6 0.6 reshape.110
  154.2 11.5 %fusion.37 = f32[512,8192]{1,0:T(8,128)} fusion(bf16[512,512]{1,0:T(8,128)(2,1)S(1)} %reshape.110, bf16[512,8192]{1,0:T(8,128)(2,1)} %param.22), kind=kOutput, calls=%fused_computation.78 | convolution fusion | flops 4294967296 | bytes 25690112 | tf_op jit(solution)/shard_map/dot_general | solution.py:108
  165.6 0.0 reduce-scatter.2.cloned.1.call-update
  165.7 1.2 copy-done.1
  166.9 0.3 copy-done.2
  167.2 3.7 add_convert_fusion
  170.9 205.8 %reduce-scatter.2.cloned.1.call-done = f32[512,512]{1,0:T(8,128)} async-done(((f32[512,8192]{1,0:T(8,128)}), f32[512,512]{1,0:T(8,128)}) %reduce-scatter.2.cloned.1.call-update) | async-done | bytes 1048592 | tf_op jit(solution)/shard_map/reduce_scatter | solution.py:109
  376.6 2.1 convert_element_type.51
  (25 shorter events, 0.1 us)
Async XLA Ops:
  7.2 1.9 copy-start
  7.2 3.6 copy-start.10
  7.2 4.2 %copy-start.6 = (f32[512]{0:T(512)S(1)}, f32[512]{0:T(512)}, u32[]{:S(2)}) copy-start(f32[512]{0:T(512)} %param.21) | copy-start | bytes 6148
  7.2 61.1 %all-gather.2.cloned.1.call-start = ((), (), s32[]{:S(2)}) async-start(), calls=%async_computation.1 | async-start | bytes 8912896 | tf_op jit(solution)/shard_map/all_gather | solution.py:60
  9.8 3.5 copy-start.4
  10.7 365.9 %reduce-scatter.2.cloned.1.call-start = ((), (), s32[]{:S(2)}) async-start(), calls=%async_computation.2 | async-start | bytes 17825792 | tf_op jit(solution)/shard_map/reduce_scatter | solution.py:109
  13.3 2.7 copy-start.8
  13.3 2.8 copy-start.5
  13.3 2.8 copy-start.7
  20.6 0.7 copy-start.3
  26.7 46.6 %copy-start.11 = (f32[8]{0:T(128)S(1)}, f32[8]{0:T(128)}, u32[]{:S(2)}) copy-start(f32[8]{0:T(128)} %param.20) | copy-start | bytes 100
  26.7 46.6 %copy-start.12 = (pred[8]{0:T(512)(128)(4,1)S(1)}, pred[8]{0:T(512)(128)(4,1)}, u32[]{:S(2)}) copy-start(pred[8]{0:T(512)(128)(4,1)} %dynamic_slice.25) | copy-start | bytes 28
  73.3 5.4 %copy-start.9 = (f32[4]{0:T(128)S(1)}, f32[4]{0:T(128)}, u32[]{:S(2)}) copy-start(f32[4]{0:T(128)} %compare_convert_fusion) | copy-start | bytes 52
  165.6 1.2 copy-start.1
  165.6 1.5 copy-start.2
Sparse Core Ops, SparseCore 0:
  10.8 57.4 all-gather.1
  165.8 210.8 reduce-scatter.1
where the time goes:
time: 387 us; the launch traced here: 386 us
  waiting for transfers between devices  247 us (64%)
  blocking collectives  72 us (19%)
  matrix products  25.9 us (7%)
  local copies, waits for them, and re-layouts  16.3 us (4%)
  between operations  14.3 us (4%)
  other arithmetic  9.68 us (3%)
    reduce_scatter x1, waiting for transfers between devices, local(): lax.psum_scatter(partial_value, 'tensor', scatter_dimension=1, tiled=True)  206 us
    psum x1, blocking collectives, local(): summed = lax.psum(local_square[:, :, None] * selector, 'tensor')  72 us
    all_gather x1, waiting for transfers between devices, local(): arrived = lax.all_gather(outbound, 'dp', axis=0, tiled=True)  41.6 us
    dot_general x1, matrix products, local(): jnp.dot(flat_normed, out_weight, preferred_element_type=jnp.float32)  11.5 us
  transfers between devices with their start and end apart: 2, of which 2 were waited for; matrix products, arithmetic and copies ran while one was open for 5% of the time, Pallas kernels for 0%

commit v1 on v0

v1 whole, which is shorter than its diff:
```python
import functools
import jax
import jax.numpy as jnp
import numpy as np
from jax import lax
from jax.experimental import pallas as pl
from jax.experimental.pallas import tpu as pltpu
from jax.sharding import Mesh, PartitionSpec as P

F32 = jnp.float32
BF16 = jnp.bfloat16
HIGH = lax.Precision.HIGHEST
SIZES = {"y": 4, "zl": 2, "c": 2, "x": 4, "zh": 4}
ROWS = 8
HALF = 4
NEW = 64
NT = (((1,), (1,)), ((), ()))
TN = (((0,), (0,)), ((), ()))


def shift(value, axis, step):
    size = SIZES[axis]
    return lax.ppermute(value, axis, [(i, (i + step) % size) for i in range(size)])


def ssm_kernel(source_count, has_alias, sc, x_ref, g_ref, b_ref, c_ref, dt_ref, par_ref, *refs):
    sources = refs[:source_count]
    refs = refs[source_count + int(has_alias) :]
    gated_ref, sq_ref, new_ref, held = refs
    r = pl.program_id(0)
    length = sc[HALF + r]
    code = sc[2 * HALF + r]
    for which, source in enumerate(sources):

        @pl.when(code == which)
        def _():
            held[...] = source[0]

    lane = lax.broadcasted_iota(jnp.int32, (NEW, 128), 1)
    sub = lax.broadcasted_iota(jnp.int32, (NEW, 128), 0)
    within = lane & 63
    causal = within <= sub
    eye = within == sub
    first_half = lane < 64
    live = sub < length
    rows = lax.broadcasted_iota(jnp.int32, (128, 128), 0)
    cols = lax.broadcasted_iota(jnp.int32, (128, 128), 1)
    same = (rows >> 6) == (cols >> 6)
    same_head = jnp.where(same, 1.0, 0.0).astype(F32)
    upper = jnp.where(same & (rows <= cols), 1.0, 0.0).astype(F32)
    bias4, rate4, skip4 = par_ref[0], par_ref[1], par_ref[2]
    raw = dt_ref[0] + bias4
    soft = jnp.maximum(raw, 0.0) + jnp.log1p(jnp.exp(-jnp.abs(raw)))
    lane4 = lax.broadcasted_iota(jnp.int32, (4, 128), 1) & 63
    dt4 = jnp.where(lane4 < length, soft, 0.0)
    a4 = -rate4 * dt4
    pieces = [jnp.where(causal, a4[p : p + 1], 0.0) for p in range(4)]
    pieces += [jnp.where(eye, dt4[p : p + 1], 0.0) for p in range(4)]
    spread = jnp.dot(
        jnp.concatenate(pieces, axis=0), same_head, precision=HIGH, preferred_element_type=F32
    )
    ds4 = jnp.dot(a4, upper, precision=HIGH, preferred_element_type=F32)
    tot4 = jnp.dot(a4, same_head, precision=HIGH, preferred_element_type=F32)
    c_val = c_ref[0]
    b_val = b_ref[0]
    bb = jnp.concatenate([b_val, b_val], axis=0)
    affinity = lax.dot_general(c_val, bb, NT, preferred_element_type=F32)
    affinity = jnp.where(causal, affinity, 0.0)
    squares = jnp.zeros((NEW, 128), F32)
    for p in range(4):
        ds_t = spread[p * NEW : (p + 1) * NEW]
        dt_t = spread[(4 + p) * NEW : (5 + p) * NEW]
        mix = affinity * jnp.exp(ds_t - ds4[p : p + 1]) * dt4[p : p + 1]
        hi = mix.astype(BF16)
        lo = (mix - hi.astype(F32)).astype(BF16)
        xf = x_ref[0, :, p * 128 : (p + 1) * 128].astype(F32)
        blocks = jnp.concatenate(
            [jnp.where(first_half, xf, 0.0), jnp.where(first_half, 0.0, xf)], axis=0
        ).astype(BF16)
        inner = jnp.dot(hi, blocks, preferred_element_type=F32) + jnp.dot(
            lo, blocks, preferred_element_type=F32
        )
        state = held[2 * p : 2 * p + 2].reshape(128, 128)
        carried = lax.dot_general(c_val, state, NT, preferred_element_type=F32)
        out = inner + carried * jnp.exp(ds_t) + skip4[p : p + 1] * xf
        gf = g_ref[0, :, p * 128 : (p + 1) * 128].astype(F32)
        gated = jnp.where(live, out * (gf / (1.0 + jnp.exp(-gf))), 0.0)
        gated_ref[0, :, p * 128 : (p + 1) * 128] = gated
        squares = squares + gated * gated
        weighted = xf * (jnp.exp(tot4[p : p + 1] - ds_t) * dt_t)
        w_hi = weighted.astype(BF16)
        w_lo = (weighted - w_hi.astype(F32)).astype(BF16)
        both = jnp.concatenate([w_hi, w_lo], axis=0)
        update = lax.dot_general(both, bb, TN, preferred_element_type=F32)
        e_tot = jnp.exp(tot4[p : p + 1])
        for k in range(2):
            kept = state[k * 64 : (k + 1) * 64].astype(F32) * e_tot[:, k * 64 : k * 64 + 1]
            new_ref[0, 2 * p + k] = (kept + update[k * 64 : (k + 1) * 64]).astype(BF16)
    ones = jnp.ones((8, 128), F32)
    sq = lax.dot_general(ones, squares, NT, precision=HIGH, preferred_element_type=F32)
    sq_ref[0] = sq[0:1]


def run_ssm(table, x, gate, b, c, dt, par, sources, alias):
    count = len(sources)
    row3 = lambda r, sc: (sc[r], 0, 0)
    in_specs = [
        pl.BlockSpec((1, NEW, 512), row3),
        pl.BlockSpec((1, NEW, 512), row3),
        pl.BlockSpec((1, NEW, 128), row3),
        pl.BlockSpec((1, NEW, 128), row3),
        pl.BlockSpec((1, 4, 128), row3),
        pl.BlockSpec((3, 4, 128), lambda r, sc: (0, 0, 0)),
    ]
    for k in range(count):
        in_specs.append(
            pl.BlockSpec(
                (1, 8, 64, 128), lambda r, sc, k=k: (sc[(3 + k) * HALF + r], 0, 0, 0)
            )
        )
    operands = [table, x, gate, b, c, dt, par, *sources]
    aliases = {}
    if alias is not None:
        in_specs.append(pl.BlockSpec(memory_space=pl.ANY))
        aliases = {len(operands): 2}
        operands.append(alias)
    return pl.pallas_call(
        functools.partial(ssm_kernel, count, alias is not None),
        grid_spec=pltpu.PrefetchScalarGridSpec(
            num_scalar_prefetch=1,
            grid=(HALF,),
            in_specs=in_specs,
            out_specs=[
                pl.BlockSpec((1, NEW, 512), lambda r, sc: (r, 0, 0)),
                pl.BlockSpec((1, 1, NEW), lambda r, sc: (r, 0, 0)),
                pl.BlockSpec((1, 8, 64, 128), lambda r, sc: (sc[r], 0, 0, 0)),
            ],
            scratch_shapes=[pltpu.VMEM((8, 64, 128), BF16)],
        ),
        out_shape=[
            jax.ShapeDtypeStruct((HALF, NEW, 512), F32),
            jax.ShapeDtypeStruct((HALF, 1, NEW), F32),
            jax.ShapeDtypeStruct((ROWS, 8, 64, 128), BF16),
        ],
        input_output_aliases=aliases,
        compiler_params=pltpu.CompilerParams(vmem_limit_bytes=32 << 20),
        cost_estimate=pl.CostEstimate(flops=300_000_000, bytes_accessed=4 << 20, transcendentals=0),
        name="ssm",
    )(*operands)


def normalise(gated, sums, gain, held):
    rows = lax.broadcasted_iota(jnp.int32, (NEW, NEW), 0)
    cols = lax.broadcasted_iota(jnp.int32, (NEW, NEW), 1)
    for r in range(HALF):
        total = sums[0][r] + sums[1][r] + sums[2][r] + sums[3][r]
        scale = lax.rsqrt(total / 2048.0 + 1e-05)
        column = jnp.sum(jnp.where(rows == cols, scale, 0.0), axis=1, keepdims=True)
        held[r * NEW : (r + 1) * NEW] = (gated[r] * column * gain[...]).astype(BF16)


def project_kernel(sc, gated, s0, s1, s2, s3, gain, w, out, held):
    @pl.when(pl.program_id(0) == 0)
    def _():
        normalise(gated, (s0, s1, s2, s3), gain, held)

    out[...] = jnp.dot(held[...], w[...], preferred_element_type=F32).astype(BF16)


def norm_specs():
    return [
        pl.BlockSpec((HALF, NEW, 512), lambda j, sc: (0, 0, 0)),
        *[pl.BlockSpec((HALF, 1, NEW), lambda j, sc: (0, 0, 0)) for _ in range(4)],
        pl.BlockSpec((1, 512), lambda j, sc: (0, 0)),
    ]


def project(place, step, gated, sums, gain, w):
    rows = HALF * NEW
    return pl.pallas_call(
        project_kernel,
        grid_spec=pltpu.PrefetchScalarGridSpec(
            num_scalar_prefetch=1,
            grid=(2,),
            in_specs=[
                *norm_specs(),
                pl.BlockSpec((512, 1024), lambda j, sc: (0, ((sc[0] + step) % 4) * 2 + j)),
            ],
            out_specs=pl.BlockSpec((rows, 1024), lambda j, sc: (0, j)),
            scratch_shapes=[pltpu.VMEM((rows, 512), BF16)],
        ),
        out_shape=jax.ShapeDtypeStruct((rows, 2048), BF16),
        compiler_params=pltpu.CompilerParams(vmem_limit_bytes=32 << 20),
        cost_estimate=pl.CostEstimate(
            flops=2 * rows * 512 * 2048, bytes_accessed=4 << 20, transcendentals=0
        ),
        name="project",
    )(place, gated, *sums, gain, w)


def own_kernel(sc, gated, s0, s1, s2, s3, gain, w, r1, r2, r3, z0, z1, z2, z3, held):
    j = pl.program_id(0)

    @pl.when(j == 0)
    def _():
        normalise(gated, (s0, s1, s2, s3), gain, held)

    value = jnp.dot(held[...], w[...], preferred_element_type=F32)
    value = value + r1[...].astype(F32) + r2[...].astype(F32) + r3[...].astype(F32)

    @pl.when(j == 0)
    def _():
        z0[...] = value

    for k, ref in ((1, z1), (2, z2), (3, z3)):

        @pl.when(j == k)
        def _():
            ref[...] = value.astype(BF16)


def own_project(place, gated, sums, gain, w, received):
    rows = HALF * NEW
    whole = pl.BlockSpec((rows, 512), lambda j, sc: (0, 0))
    return pl.pallas_call(
        own_kernel,
        grid_spec=pltpu.PrefetchScalarGridSpec(
            num_scalar_prefetch=1,
            grid=(4,),
            in_specs=[
                *norm_specs(),
                pl.BlockSpec((512, 512), lambda j, sc: (0, sc[0] * 4 + (sc[1] + j) % 4)),
                *[
                    pl.BlockSpec((rows, 512), lambda j, sc: (0, (sc[1] + j) % 4))
                    for _ in range(3)
                ],
            ],
            out_specs=[whole] * 4,
            scratch_shapes=[pltpu.VMEM((rows, 512), BF16)],
        ),
        out_shape=[
            jax.ShapeDtypeStruct((rows, 512), F32),
            *[jax.ShapeDtypeStruct((rows, 512), BF16) for _ in range(3)],
        ],
        compiler_params=pltpu.CompilerParams(vmem_limit_bytes=32 << 20),
        cost_estimate=pl.CostEstimate(
            flops=2 * rows * 512 * 2048, bytes_accessed=7 << 20, transcendentals=0
        ),
        name="own_project",
    )(place, gated, *sums, gain, w, *received)


def finish_kernel(sc, z0, r1, r2, r3, *refs):
    out = refs[-1]
    value = z0[...] + r1[...].astype(F32) + r2[...].astype(F32) + r3[...].astype(F32)
    out[0] = value.astype(BF16)


def finish(table, parts, alias):
    block = pl.BlockSpec((NEW, 512), lambda r, sc: (r, 0))
    in_specs = [block] * 4
    operands = [table, *parts]
    aliases = {}
    if alias is not None:
        in_specs.append(pl.BlockSpec(memory_space=pl.ANY))
        aliases = {len(operands): 0}
        operands.append(alias)
    return pl.pallas_call(
        finish_kernel,
        grid_spec=pltpu.PrefetchScalarGridSpec(
            num_scalar_prefetch=1,
            grid=(HALF,),
            in_specs=in_specs,
            out_specs=pl.BlockSpec((1, NEW, 512), lambda r, sc: (sc[r], 0, 0)),
        ),
        out_shape=jax.ShapeDtypeStruct((ROWS, NEW, 512), BF16),
        input_output_aliases=aliases,
        cost_estimate=pl.CostEstimate(flops=1_000_000, bytes_accessed=2 << 20, transcendentals=0),
        name="finish",
    )(*operands)


def pick_kernel(count, sc, *refs):
    sources, outs = refs[: count * 3], refs[count * 3 :]
    q = pl.program_id(0)
    for k in range(3):
        code = sc[k * HALF + q]
        for which in range(count):

            @pl.when(code == which)
            def _():
                outs[k][...] = sources[k * count + which][...]


def pick(table, sources):
    count = len(sources)
    block = (1, 8, 64, 128)
    in_specs = [
        pl.BlockSpec(block, lambda q, sc, k=k: (sc[3 * HALF + k * HALF + q], 0, 0, 0))
        for k in range(3)
        for _ in range(count)
    ]
    return pl.pallas_call(
        functools.partial(pick_kernel, count),
        grid_spec=pltpu.PrefetchScalarGridSpec(
            num_scalar_prefetch=1,
            grid=(HALF,),
            in_specs=in_specs,
            out_specs=[pl.BlockSpec(block, lambda q, sc: (q, 0, 0, 0))] * 3,
        ),
        out_shape=[jax.ShapeDtypeStruct((HALF, 8, 64, 128), BF16)] * 3,
        compiler_params=pltpu.CompilerParams(vmem_limit_bytes=32 << 20),
        cost_estimate=pl.CostEstimate(flops=1, bytes_accessed=8 << 20, transcendentals=0),
        name="pick",
    )(table, *(list(sources) * 3))


def copy_kernel(sc, source, out):
    out[...] = source[...]


def take_rows(table, states):
    block = (1, 8, 64, 128)
    return pl.pallas_call(
        copy_kernel,
        grid_spec=pltpu.PrefetchScalarGridSpec(
            num_scalar_prefetch=1,
            grid=(HALF,),
            in_specs=[pl.BlockSpec(block, lambda q, sc: (sc[q], 0, 0, 0))],
            out_specs=pl.BlockSpec(block, lambda q, sc: (q, 0, 0, 0)),
        ),
        out_shape=jax.ShapeDtypeStruct((HALF, 8, 64, 128), BF16),
        cost_estimate=pl.CostEstimate(flops=1, bytes_accessed=1 << 20, transcendentals=0),
        name="take_rows",
    )(table, states)


def chosen(mask, values):
    return jnp.sum(jnp.where(mask, values, 0), axis=-1, dtype=jnp.int32)


def local(
    ssm_input,
    gate_input,
    write_basis,
    read_basis,
    step_raw,
    step_bias,
    decay_rate,
    skip_gain,
    norm_gain,
    out_weight,
    ssm_states,
    anchor,
    tool_length,
):
    y, zl, c = lax.axis_index("y"), lax.axis_index("zl"), lax.axis_index("c")
    x, zh = lax.axis_index("x"), lax.axis_index("zh")
    me = (y * 2 + zl) * 2 + c
    ids = jnp.arange(ROWS * 16, dtype=jnp.int32)
    dest = ids // ROWS
    source, source_row = anchor // ROWS, anchor % ROWS
    moving = source != dest
    earlier = ids[None, :] < ids[:, None]

    same_source = moving[None, :] & (source[None, :] == source[:, None]) & earlier
    leave_slot = jnp.sum(same_source, axis=1, dtype=jnp.int32)
    slots = jnp.arange(HALF, dtype=jnp.int32)
    leaving = (moving & (source == me))[None, :] & (leave_slot[None, :] == slots[:, None])
    buf = take_rows(chosen(leaving, source_row[None, :]), ssm_states)
    across = shift(buf, "zl", 1)
    beside = shift(buf, "c", 1)

    lo = me * ROWS
    mine_source = lax.dynamic_slice_in_dim(source, lo, ROWS)
    mine_row = lax.dynamic_slice_in_dim(source_row, lo, ROWS)
    mine_moving = mine_source != me
    local_ids = jnp.arange(ROWS, dtype=jnp.int32)
    before = (mine_moving[None, :] == mine_moving[:, None]) & (
        local_ids[None, :] < local_ids[:, None]
    )
    rank = jnp.sum(before, axis=1, dtype=jnp.int32) + jnp.where(
        mine_moving, ROWS - jnp.sum(mine_moving, dtype=jnp.int32), 0
    )
    at = rank[None, :] == local_ids[:, None]
    order = chosen(at, local_ids[None, :])
    length = chosen(at, tool_length[None, :])
    row_of = chosen(at, mine_row[None, :])

    place = jnp.stack([x, zh]).astype(jnp.int32)
    b = lax.dynamic_index_in_dim(write_basis, x, 2, keepdims=False)
    cc = lax.dynamic_index_in_dim(read_basis, x, 2, keepdims=False)
    dt = step_raw.reshape(ROWS, 4, 128)
    par = jnp.repeat(jnp.stack([step_bias, decay_rate, skip_gain]), 64, axis=1).reshape(3, 4, 128)
    gain = norm_gain.reshape(1, 512)

    def sums_of(sq):
        return (sq, shift(sq, "zh", 1), shift(sq, "zh", 2), shift(sq, "zh", 3))

    def reduce_over(gated, sums):
        received = []
        for step in (2, 1, 3):
            part = project(place, step, gated, sums, gain, out_weight)
            received.append(shift(part, "x", step))
        zs = own_project(place, gated, sums, gain, out_weight, received)
        return [zs[0]] + [shift(zs[k], "zh", k) for k in (1, 2, 3)]

    table1 = jnp.concatenate(
        [order[:HALF], length[:HALF], jnp.zeros((HALF,), jnp.int32), row_of[:HALF]]
    )
    gated1, sq1, states1 = run_ssm(
        table1, ssm_input, gate_input, b, cc, dt, par, [ssm_states], None
    )
    sums1 = sums_of(sq1)
    parts1 = reduce_over(gated1, sums1)

    beside_across = shift(across, "c", 1)
    plane = [buf, across, beside, beside_across]
    plane_of = source // 4
    spot = ((source // 2) % 2 ^ zl) + 2 * ((source % 2) ^ c)
    same_plane = (
        moving[None, :]
        & (dest[None, :] == dest[:, None])
        & (plane_of[None, :] == plane_of[:, None])
        & earlier
    )
    plane_slot = jnp.sum(same_plane, axis=1, dtype=jnp.int32)
    steps = jnp.arange(1, 4, dtype=jnp.int32)
    targets = (((y + steps) % 4) * 2 + zl) * 2 + c
    going = moving & (plane_of == y)
    wanted = (
        going[None, None, :]
        & (dest[None, None, :] == targets[:, None, None])
        & (plane_slot[None, None, :] == slots[None, :, None])
    )
    pick_table = jnp.concatenate(
        [
            chosen(wanted, spot[None, None, :]).reshape(-1),
            chosen(wanted, leave_slot[None, None, :]).reshape(-1),
        ]
    )
    sends = pick(pick_table, plane)
    arrived = [shift(sends[k], "y", k + 1) for k in range(3)]

    mine = lambda v: lax.dynamic_slice_in_dim(v, lo, ROWS)
    hops = (y - mine(plane_of)) % 4
    code = jnp.where(
        mine_moving, jnp.where(hops == 0, 1 + mine(spot), 4 + hops), 0
    )
    index = jnp.where(
        mine_moving, jnp.where(hops == 0, mine(leave_slot), mine(plane_slot)), mine_row
    )
    code2 = chosen(at, code[None, :])[HALF:]
    index2 = chosen(at, index[None, :])[HALF:]
    per_source = jnp.where(
        jnp.arange(8, dtype=jnp.int32)[:, None] == code2[None, :], index2[None, :], 0
    )
    table2 = jnp.concatenate([order[HALF:], length[HALF:], code2, per_source.reshape(-1)])
    gated2, sq2, new_states = run_ssm(
        table2,
        ssm_input,
        gate_input,
        b,
        cc,
        dt,
        par,
        [ssm_states, *plane, *arrived],
        states1,
    )
    sums2 = sums_of(sq2)
    parts2 = reduce_over(gated2, sums2)
    half_out = finish(order[:HALF], parts1, None)
    layer_out = finish(order[HALF:], parts2, half_out)
    return layer_out, new_states


def solution(mesh):
    fine = Mesh(mesh.devices.reshape(4, 2, 2, 4, 4), ("y", "zl", "c", "x", "zh"))
    dp, tp = ("y", "zl", "c"), ("x", "zh")
    placed = (
        P(dp, None, tp),
        P(dp, None, tp),
        P(dp, None, None, None),
        P(dp, None, None, None),
        P(dp, tp, None),
        P(tp),
        P(tp),
        P(tp),
        P(tp),
        P(tp, None),
        P(dp, tp, None, None),
        P(),
        P(dp),
    )
    return jax.shard_map(
        local,
        mesh=fine,
        in_specs=placed,
        out_specs=(P(dp, None, tp), P(dp, tp, None, None)),
        check_vma=False,
    )
```

time: 387 us -> 177 us (0.46)
  waiting for transfers between devices: 247 us -> 59.8 us
  blocking collectives: 72 us -> 0 us
  starting transfers between devices: 0.08 us -> 47.1 us
  Pallas kernels: 0 us -> 44.7 us
  matrix products: 25.9 us -> 0 us
  between operations: 14.3 us -> 1.53 us
  other arithmetic: 9.68 us -> 5.32 us
    reduce_scatter x1 -> x0, waiting for transfers between devices: 206 us -> none  [local(): lax.psum_scatter(partial_value, 'tensor', scatter_dimension=1, tiled=True)]
    psum x1 -> x0, blocking collectives: 72 us -> none  [local(): summed = lax.psum(local_square[:, :, None] * selector, 'tensor')]
    ppermute x0 -> x24, waiting for transfers between devices: none -> 59.8 us  [shift(): lax.ppermute(value, axis, [(i, (i + step) % size) for i in range(size)])]
    ppermute x0 -> x24, starting transfers between devices: none -> 47.1 us  [shift(): lax.ppermute(value, axis, [(i, (i + step) % size) for i in range(size)])]
    pallas_call x0 -> x14, Pallas kernels: none -> 44.7 us  [the longest x2 11.8 us: run_ssm(): pl.pallas_call(functools.partial(ssm_kernel, count, alias is not None), g...]
    all_gather x1 -> x0, waiting for transfers between devices: 41.6 us -> none  [local(): arrived = lax.all_gather(outbound, 'dp', axis=0, tiled=True)]
    dot_general x5 -> x0, matrix products: 25.9 us -> none  [the longest x1 11.5 us: local(): jnp.dot(flat_normed, out_weight, preferred_element_type=jnp.float32)]
    unnamed x27 -> x48, local copies, waits for them, and re-layouts: 3.53 us -> 13.1 us
  transfers between devices with their start and end apart: 2 -> 24, of which waited for: 2 -> 12; matrix products, arithmetic and copies ran while one was open for 5% -> 4% of each run, Pallas kernels for 0% -> 21%
where the time goes in v1:
time: 177 us; the launch traced here: 175 us
  waiting for transfers between devices  59.8 us (34%)
  starting transfers between devices  47.1 us (27%)
  Pallas kernels  44.7 us (25%)
  local copies, waits for them, and re-layouts  16.5 us (9%)
  other arithmetic  5.32 us (3%)
    ppermute x24, waiting for transfers between devices, shift(): lax.ppermute(value, axis, [(i, (i + step) % size) for i in range(size)])  59.8 us
    ppermute x24, starting transfers between devices, shift(): lax.ppermute(value, axis, [(i, (i + step) % size) for i in range(size)])  47.1 us
    unnamed x48, local copies, waits for them, and re-layouts  13.1 us
    pallas_call x2, Pallas kernels, run_ssm(): pl.pallas_call(functools.partial(ssm_kernel, count, alias is not None), g...  11.8 us
    pallas_call x6, Pallas kernels, project(): pl.pallas_call(project_kernel, grid_spec=pltpu.PrefetchScalarGridSpec(num...  11.8 us
    pallas_call x2, Pallas kernels, finish(): pl.pallas_call(finish_kernel, grid_spec=pltpu.PrefetchScalarGridSpec(num_...  7.91 us
    pallas_call x2, Pallas kernels, own_project(): pl.pallas_call(own_kernel, grid_spec=pltpu.PrefetchScalarGridSpec(num_sca...  7.02 us
    pallas_call x1, Pallas kernels, take_rows(): pl.pallas_call(copy_kernel, grid_spec=pltpu.PrefetchScalarGridSpec(num_sc...  3.83 us
  transfers between devices with their start and end apart: 24, of which 12 were waited for; matrix products, arithmetic and copies ran while one was open for 4% of the time, Pallas kernels for 21%

profile of v1, /device:TPU:12, one launch (start us, length us, event | category | flops | bytes accessed | tf_op | source)
XLA Modules:
  0.0 174.9 jit_solution(4081423624842652601)
XLA Ops:
  2.8 3.8 %take_rows.1.refs_0_.refs_4_.refs_8_.refs_1_ = bf16[4,8,64,128]{3,2,1,0:T(8,128)(2,1)} custom-call(s32[4]{0:T(128)} %select_reduce_fusion.5.sc, bf16[8,8,64,128]{3,2,1,0:T(8,128)(2,1)} %refs_0_.3), custom_call_target="tpu_custom_call" | custom-call | flops 1 | bytes 1048576 | tf_op jit(solution)/shard_map/take_rows/pallas_call | solution.py:324
  6.7 1.9 %collective-permute-start = (bf16[4,8,64,128]{3,2,1,0:T(8,128)(2,1)}, bf16[4,8,64,128]{3,2,1,0:T(8,128)(2,1)S(1)}, u32[]{:S(2)}, u32[]{:S(2)}) collective-permute-start(bf16[4,8,64,128]{3,2,1,0:T(8,128)(2,1)} %take_rows.1.refs_0_.refs_4_.refs_8_.refs_1_), channel_id=1, source_target_pairs={{0,32},{32,0},{1,33},{33,1},{2,34},{34,2},{3,35},{35,3},{4,36},{36... | collective-permute-start | bytes 1572872 | tf_op jit(solution)/shard_map/ppermute | solution.py:23
  11.2 1.8 %constant_dynamic-slice_fusion = (bf16[8,64,1,128]{3,2,1,0:T(2,128)(2,1)S(1)}, bf16[8,64,1,128]{3,2,1,0:T(2,128)(2,1)S(1)}) fusion(bf16[8,64,4,128]{3,2,1,0:T(4,128)(2,1)} %param.16, s32[]{:T(128)S(6)} %select_n.147, bf16[8,64,4,128]{3,2,1,0:T(4,128)(2,1)} %param.15), kind=kLoop, calls=%fused_computation.78 | loop fusion | bytes 524292 | tf_op jit(solution)/shard_map/jit(dynamic_index_in_dim)/dynamic_slice | solution.py:392
  14.9 1.2 copy-done.3
  16.1 1.0 copy-done.5
  17.2 1.0 copy-done.7
  18.2 5.4 %ssm.2 = (f32[4,64,512]{2,1,0:T(8,128)S(1)}, f32[4,1,64]{2,1,0:T(1,128)S(1)}, bf16[8,8,64,128]{3,2,1,0:T(8,128)(2,1)}) custom-call(s32[16]{0:T(128)S(1)} %pad_add_fusion.3.sc, bf16[8,64,512]{2,1,0:T(8,128)(2,1)S(1)} %copy-done.5, bf16[8,64,512]{2,1,0:T(8,128)(2,1)S(1)} %copy-done.7, bf16[8,64,128]{2,1,0:T(8,128)(2,1)S(1)} %bitcast.17, ...), custom_call_target="tpu_custom_call" | custom-call | flops 300000000 | bytes 4194304 | tf_op jit(solution)/shard_map/ssm/pallas_call | solution.py:127
  23.6 3.3 %collective-permute-start.15 = (f32[4,1,64]{2,1,0:T(1,128)S(1)}, f32[4,1,64]{2,1,0:T(1,128)S(1)}, u32[]{:S(2)}, u32[]{:S(2)}) collective-permute-start(f32[4,1,64]{2,1,0:T(1,128)S(1)} %get-tuple-element.30.s0), channel_id=1, source_target_pairs={{0,1},{1,2},{2,3},{3,0},{4,5},{5,6},{6,7},{7,4},{8,9},{9,10},{10,1... | collective-permute-start | bytes 3080 | tf_op jit(solution)/shard_map/ppermute | solution.py:23
  26.9 4.5 %collective-permute-start.16 = (f32[4,1,64]{2,1,0:T(1,128)S(1)}, f32[4,1,64]{2,1,0:T(1,128)S(1)}, u32[]{:S(2)}, u32[]{:S(2)}) collective-permute-start(f32[4,1,64]{2,1,0:T(1,128)S(1)} %get-tuple-element.30.s0), channel_id=1, source_target_pairs={{0,2},{1,3},{2,0},{3,1},{4,6},{5,7},{6,4},{7,5},{8,10},{9,11},{10,... | collective-permute-start | bytes 3080 | tf_op jit(solution)/shard_map/ppermute | solution.py:23
  31.4 2.7 %collective-permute-start.17 = (f32[4,1,64]{2,1,0:T(1,128)S(1)}, f32[4,1,64]{2,1,0:T(1,128)S(1)}, u32[]{:S(2)}, u32[]{:S(2)}) collective-permute-start(f32[4,1,64]{2,1,0:T(1,128)S(1)} %get-tuple-element.30.s0), channel_id=1, source_target_pairs={{0,3},{1,0},{2,1},{3,2},{4,7},{5,4},{6,5},{7,6},{8,11},{9,8},{10,9... | collective-permute-start | bytes 3080 | tf_op jit(solution)/shard_map/ppermute | solution.py:23
  34.8 1.1 collective-permute-done.17.s3
  35.9 3.4 %copy-done = bf16[512,8192]{1,0:T(8,128)(2,1)S(1)} copy-done((bf16[512,8192]{1,0:T(8,128)(2,1)S(1)}, bf16[512,8192]{1,0:T(8,128)(2,1)}, u32[]{:S(2)}) %copy-start) | copy-done | bytes 8388632
  39.9 2.6 %project.9 = bf16[256,2048]{1,0:T(8,128)(2,1)} custom-call(s32[2]{0:T(128)S(1)} %pad_add_fusion.sc, f32[4,64,512]{2,1,0:T(8,128)S(1)} %get-tuple-element.29.gated, f32[4,1,64]{2,1,0:T(1,128)S(1)} %get-tuple-element.30.s0, f32[4,1,64]{2,1,0:T(1,128)S(1)} %collective-permute-done.15.s1, f32[4,1,64]{2,1,0:T(1,128)S(1)} %collective-permute-done.16.s2, ...), custom_call_target="tpu_custom_call" | custom-call | flops 536870912 | bytes 4194304 | tf_op jit(solution)/shard_map/project/pallas_call | solution.py:180
  43.5 2.4 %pick.1 = (bf16[4,8,64,128]{3,2,1,0:T(8,128)(2,1)}, bf16[4,8,64,128]{3,2,1,0:T(8,128)(2,1)}, bf16[4,8,64,128]{3,2,1,0:T(8,128)(2,1)}) custom-call(s32[24]{0:T(128)S(1)} %pad_add_fusion.2.sc, bf16[4,8,64,128]{3,2,1,0:T(8,128)(2,1)S(1)} %copy-done.2, bf16[4,8,64,128]{3,2,1,0:T(8,128)(2,1)S(1)} %collective-permute-done.refs_1_.refs_5_.refs_9_.refs_2_, ...), custom_call_target="tpu_custom_call" | custom-call | flops 1 | bytes 8388608 | tf_op jit(solution)/shard_map/pick/pallas_call | solution.py:303
  45.8 1.6 collective-permute-start.3
  48.4 2.4 %collective-permute-start.5 = (bf16[4,8,64,128]{3,2,1,0:T(8,128)(2,1)}, bf16[4,8,64,128]{3,2,1,0:T(8,128)(2,1)}, u32[]{:S(2)}, u32[]{:S(2)}) collective-permute-start(bf16[4,8,64,128]{3,2,1,0:T(8,128)(2,1)} %get-tuple-element.21), channel_id=1, source_target_pairs={{0,192},{64,0},{128,64},{192,128},{1,193},{65,1},{129,65},{193,129... | collective-permute-start | bytes 1572872 | tf_op jit(solution)/shard_map/ppermute | solution.py:23
  51.0 3.4 %copy-done.1 = bf16[512,8192]{1,0:T(8,128)(2,1)S(1)} copy-done((bf16[512,8192]{1,0:T(8,128)(2,1)S(1)}, bf16[512,8192]{1,0:T(8,128)(2,1)}, u32[]{:S(2)}) %copy-start.1) | copy-done | bytes 8388632
  54.4 1.8 %project.10 = bf16[256,2048]{1,0:T(8,128)(2,1)S(1)} custom-call(s32[2]{0:T(128)S(1)} %pad_add_fusion.sc, f32[4,64,512]{2,1,0:T(8,128)S(1)} %get-tuple-element.29.gated, f32[4,1,64]{2,1,0:T(1,128)S(1)} %get-tuple-element.30.s0, f32[4,1,64]{2,1,0:T(1,128)S(1)} %collective-permute-done.15.s1, f32[4,1,64]{2,1,0:T(1,128)S(1)} %collective-permute-done.16.s2, ...), custom_call_target="tpu_custom_call" | custom-call | flops 536870912 | bytes 4194304 | tf_op jit(solution)/shard_map/project/pallas_call | solution.py:180
  56.3 2.2 %collective-permute-start.19 = (bf16[256,2048]{1,0:T(8,128)(2,1)S(1)}, bf16[256,2048]{1,0:T(8,128)(2,1)S(1)}, u32[]{:S(2)}, u32[]{:S(2)}) collective-permute-start(bf16[256,2048]{1,0:T(8,128)(2,1)S(1)} %project.10), channel_id=1, source_target_pairs={{0,4},{4,8},{8,12},{12,0},{1,5},{5,9},{9,13},{13,1},{2,6},{6,10},{... | collective-permute-start | bytes 3145736 | tf_op jit(solution)/shard_map/ppermute | solution.py:23
  58.4 1.8 %project.11 = bf16[256,2048]{1,0:T(8,128)(2,1)S(1)} custom-call(s32[2]{0:T(128)S(1)} %pad_add_fusion.sc, f32[4,64,512]{2,1,0:T(8,128)S(1)} %get-tuple-element.29.gated, f32[4,1,64]{2,1,0:T(1,128)S(1)} %get-tuple-element.30.s0, f32[4,1,64]{2,1,0:T(1,128)S(1)} %collective-permute-done.15.s1, f32[4,1,64]{2,1,0:T(1,128)S(1)} %collective-permute-done.16.s2, ...), custom_call_target="tpu_custom_call" | custom-call | flops 536870912 | bytes 4194304 | tf_op jit(solution)/shard_map/project/pallas_call | solution.py:180
  60.9 2.2 %collective-permute-start.20 = (bf16[256,2048]{1,0:T(8,128)(2,1)S(1)}, bf16[256,2048]{1,0:T(8,128)(2,1)S(1)}, u32[]{:S(2)}, u32[]{:S(2)}) collective-permute-start(bf16[256,2048]{1,0:T(8,128)(2,1)S(1)} %project.11), channel_id=1, source_target_pairs={{0,12},{4,0},{8,4},{12,8},{1,13},{5,1},{9,5},{13,9},{2,14},{6,2},{... | collective-permute-start | bytes 3145736 | tf_op jit(solution)/shard_map/ppermute | solution.py:23
  63.2 1.0 collective-permute-done.4.refs_6_
  64.1 7.9 %collective-permute-done.5.refs_7_ = bf16[4,8,64,128]{3,2,1,0:T(8,128)(2,1)} collective-permute-done((bf16[4,8,64,128]{3,2,1,0:T(8,128)(2,1)}, bf16[4,8,64,128]{3,2,1,0:T(8,128)(2,1)}, u32[]{:S(2)}, u32[]{:S(2)}) %collective-permute-start.5) | collective-permute-done | bytes 524320 | tf_op jit(solution)/shard_map/ppermute | solution.py:23
  72.0 6.4 %ssm.3 = (f32[4,64,512]{2,1,0:T(8,128)S(1)}, f32[4,1,64]{2,1,0:T(1,128)S(1)}, bf16[8,8,64,128]{3,2,1,0:T(8,128)(2,1)}) custom-call(s32[44]{0:T(128)S(1)} %pad_add_fusion.1.sc, bf16[8,64,512]{2,1,0:T(8,128)(2,1)S(1)} %copy-done.6, bf16[8,64,512]{2,1,0:T(8,128)(2,1)S(1)} %copy-done.8, ...), custom_call_target="tpu_custom_call", output_to_operand_aliasing={{2}: (15, {})} | custom-call | flops 300000000 | bytes 4194304 | tf_op jit(solution)/shard_map/ssm/pallas_call | solution.py:127
  78.4 1.3 collective-permute-start.6
  79.7 3.9 %collective-permute-start.7 = (f32[4,1,64]{2,1,0:T(1,128)S(1)}, f32[4,1,64]{2,1,0:T(1,128)S(1)}, u32[]{:S(2)}, u32[]{:S(2)}) collective-permute-start(f32[4,1,64]{2,1,0:T(1,128)S(1)} %get-tuple-element.24.s0), channel_id=1, source_target_pairs={{0,2},{1,3},{2,0},{3,1},{4,6},{5,7},{6,4},{7,5},{8,10},{9,11},{10,... | collective-permute-start | bytes 3080 | tf_op jit(solution)/shard_map/ppermute | solution.py:23
  84.1 1.6 collective-permute-start.8
  85.7 1.5 collective-permute-done.7.s2
  87.2 1.4 collective-permute-done.8.s3
  88.6 1.8 %project.8 = bf16[256,2048]{1,0:T(8,128)(2,1)S(1)} custom-call(s32[2]{0:T(128)S(1)} %pad_add_fusion.sc, f32[4,64,512]{2,1,0:T(8,128)S(1)} %get-tuple-element.23.gated, f32[4,1,64]{2,1,0:T(1,128)S(1)} %get-tuple-element.24.s0, f32[4,1,64]{2,1,0:T(1,128)S(1)} %collective-permute-done.6.s1, f32[4,1,64]{2,1,0:T(1,128)S(1)} %collective-permute-done.7.s2, ...), custom_call_target="tpu_custom_call" | custom-call | flops 536870912 | bytes 4194304 | tf_op jit(solution)/shard_map/project/pallas_call | solution.py:180
  90.4 2.2 %collective-permute-start.11 = (bf16[256,2048]{1,0:T(8,128)(2,1)S(1)}, bf16[256,2048]{1,0:T(8,128)(2,1)S(1)}, u32[]{:S(2)}, u32[]{:S(2)}) collective-permute-start(bf16[256,2048]{1,0:T(8,128)(2,1)S(1)} %project.8), channel_id=1, source_target_pairs={{0,12},{4,0},{8,4},{12,8},{1,13},{5,1},{9,5},{13,9},{2,14},{6,2},{... | collective-permute-start | bytes 3145736 | tf_op jit(solution)/shard_map/ppermute | solution.py:23
  92.6 1.8 %project.7 = bf16[256,2048]{1,0:T(8,128)(2,1)S(1)} custom-call(s32[2]{0:T(128)S(1)} %pad_add_fusion.sc, f32[4,64,512]{2,1,0:T(8,128)S(1)} %get-tuple-element.23.gated, f32[4,1,64]{2,1,0:T(1,128)S(1)} %get-tuple-element.24.s0, f32[4,1,64]{2,1,0:T(1,128)S(1)} %collective-permute-done.6.s1, f32[4,1,64]{2,1,0:T(1,128)S(1)} %collective-permute-done.7.s2, ...), custom_call_target="tpu_custom_call" | custom-call | flops 536870912 | bytes 4194304 | tf_op jit(solution)/shard_map/project/pallas_call | solution.py:180
  94.6 1.8 %project.6 = bf16[256,2048]{1,0:T(8,128)(2,1)S(1)} custom-call(s32[2]{0:T(128)S(1)} %pad_add_fusion.sc, f32[4,64,512]{2,1,0:T(8,128)S(1)} %get-tuple-element.23.gated, f32[4,1,64]{2,1,0:T(1,128)S(1)} %get-tuple-element.24.s0, f32[4,1,64]{2,1,0:T(1,128)S(1)} %collective-permute-done.6.s1, f32[4,1,64]{2,1,0:T(1,128)S(1)} %collective-permute-done.7.s2, ...), custom_call_target="tpu_custom_call" | custom-call | flops 536870912 | bytes 4194304 | tf_op jit(solution)/shard_map/project/pallas_call | solution.py:180
  96.4 3.0 %collective-permute-start.9 = (bf16[256,2048]{1,0:T(8,128)(2,1)S(1)}, bf16[256,2048]{1,0:T(8,128)(2,1)S(1)}, u32[]{:S(2)}, u32[]{:S(2)}) collective-permute-start(bf16[256,2048]{1,0:T(8,128)(2,1)S(1)} %project.6), channel_id=1, source_target_pairs={{0,8},{4,12},{8,0},{12,4},{1,9},{5,13},{9,1},{13,5},{2,10},{6,14},... | collective-permute-start | bytes 3145736 | tf_op jit(solution)/shard_map/ppermute | solution.py:23
  99.4 4.1 %own_project.3 = (f32[256,512]{1,0:T(8,128)S(1)}, bf16[256,512]{1,0:T(8,128)(2,1)S(1)}, bf16[256,512]{1,0:T(8,128)(2,1)S(1)}, bf16[256,512]{1,0:T(8,128)(2,1)S(1)}) custom-call(s32[2]{0:T(128)S(1)} %pad_add_fusion.sc, f32[4,64,512]{2,1,0:T(8,128)S(1)} %get-tuple-element.29.gated, f32[4,1,64]{2,1,0:T(1,128)S(1)} %get-tuple-element.30.s0, ...), custom_call_target="tpu_custom_call" | custom-call | flops 536870912 | bytes 7340032 | tf_op jit(solution)/shard_map/own_project/pallas_call | solution.py:225
  103.5 2.1 %collective-permute-start.21 = (bf16[256,512]{1,0:T(8,128)(2,1)S(1)}, bf16[256,512]{1,0:T(8,128)(2,1)S(1)}, u32[]{:S(2)}, u32[]{:S(2)}) collective-permute-start(bf16[256,512]{1,0:T(8,128)(2,1)S(1)} %get-tuple-element.32), channel_id=1, source_target_pairs={{0,1},{1,2},{2,3},{3,0},{4,5},{5,6},{6,7},{7,4},{8,9},{9,10},{10,1... | collective-permute-start | bytes 786440 | tf_op jit(solution)/shard_map/ppermute | solution.py:23
  105.6 3.1 %collective-permute-start.22 = (bf16[256,512]{1,0:T(8,128)(2,1)S(1)}, bf16[256,512]{1,0:T(8,128)(2,1)S(1)}, u32[]{:S(2)}, u32[]{:S(2)}) collective-permute-start(bf16[256,512]{1,0:T(8,128)(2,1)S(1)} %get-tuple-element.33), channel_id=1, source_target_pairs={{0,2},{1,3},{2,0},{3,1},{4,6},{5,7},{6,4},{7,5},{8,10},{9,11},{10,... | collective-permute-start | bytes 786440 | tf_op jit(solution)/shard_map/ppermute | solution.py:23
  108.8 26.3 %collective-permute-done.11.r3 = bf16[256,2048]{1,0:T(8,128)(2,1)S(1)} collective-permute-done((bf16[256,2048]{1,0:T(8,128)(2,1)S(1)}, bf16[256,2048]{1,0:T(8,128)(2,1)S(1)}, u32[]{:S(2)}, u32[]{:S(2)}) %collective-permute-start.11) | collective-permute-done | bytes 1048608 | tf_op jit(solution)/shard_map/ppermute | solution.py:23
  135.0 5.0 %collective-permute-done.9.r1 = bf16[256,2048]{1,0:T(8,128)(2,1)S(1)} collective-permute-done((bf16[256,2048]{1,0:T(8,128)(2,1)S(1)}, bf16[256,2048]{1,0:T(8,128)(2,1)S(1)}, u32[]{:S(2)}, u32[]{:S(2)}) %collective-permute-start.9) | collective-permute-done | bytes 1048608 | tf_op jit(solution)/shard_map/ppermute | solution.py:23
  140.0 2.9 %own_project.2 = (f32[256,512]{1,0:T(8,128)S(1)}, bf16[256,512]{1,0:T(8,128)(2,1)S(1)}, bf16[256,512]{1,0:T(8,128)(2,1)S(1)}, bf16[256,512]{1,0:T(8,128)(2,1)S(1)}) custom-call(s32[2]{0:T(128)S(1)} %pad_add_fusion.sc, f32[4,64,512]{2,1,0:T(8,128)S(1)} %get-tuple-element.23.gated, f32[4,1,64]{2,1,0:T(1,128)S(1)} %get-tuple-element.24.s0, ...), custom_call_target="tpu_custom_call" | custom-call | flops 536870912 | bytes 7340032 | tf_op jit(solution)/shard_map/own_project/pallas_call | solution.py:225
  143.7 2.5 %collective-permute-start.12 = (bf16[256,512]{1,0:T(8,128)(2,1)S(1)}, bf16[256,512]{1,0:T(8,128)(2,1)S(1)}, u32[]{:S(2)}, u32[]{:S(2)}) collective-permute-start(bf16[256,512]{1,0:T(8,128)(2,1)S(1)} %get-tuple-element.26), channel_id=1, source_target_pairs={{0,1},{1,2},{2,3},{3,0},{4,5},{5,6},{6,7},{7,4},{8,9},{9,10},{10,1... | collective-permute-start | bytes 786440 | tf_op jit(solution)/shard_map/ppermute | solution.py:23
  146.3 2.6 %collective-permute-start.13 = (bf16[256,512]{1,0:T(8,128)(2,1)S(1)}, bf16[256,512]{1,0:T(8,128)(2,1)S(1)}, u32[]{:S(2)}, u32[]{:S(2)}) collective-permute-start(bf16[256,512]{1,0:T(8,128)(2,1)S(1)} %get-tuple-element.27), channel_id=1, source_target_pairs={{0,2},{1,3},{2,0},{3,1},{4,6},{5,7},{6,4},{7,5},{8,10},{9,11},{10,... | collective-permute-start | bytes 786440 | tf_op jit(solution)/shard_map/ppermute | solution.py:23
  148.9 2.0 %collective-permute-start.14 = (bf16[256,512]{1,0:T(8,128)(2,1)S(1)}, bf16[256,512]{1,0:T(8,128)(2,1)S(1)}, u32[]{:S(2)}, u32[]{:S(2)}) collective-permute-start(bf16[256,512]{1,0:T(8,128)(2,1)S(1)} %get-tuple-element.28), channel_id=1, source_target_pairs={{0,3},{1,0},{2,1},{3,2},{4,7},{5,4},{6,5},{7,6},{8,11},{9,8},{10,9... | collective-permute-start | bytes 786440 | tf_op jit(solution)/shard_map/ppermute | solution.py:23
  151.7 4.0 %finish.2.refs_0_ = bf16[8,64,512]{2,1,0:T(8,128)(2,1)} custom-call(s32[4]{0:T(128)} %copy-done.20, f32[256,512]{1,0:T(8,128)} %copy-done.10, bf16[256,512]{1,0:T(8,128)(2,1)} %copy-done.16, bf16[256,512]{1,0:T(8,128)(2,1)} %copy-done.17, bf16[256,512]{1,0:T(8,128)(2,1)} %copy-done.18), custom_call_target="tpu_custom_call" | custom-call | flops 1000000 | bytes 2097152 | tf_op jit(solution)/shard_map/finish/pallas_call | solution.py:268
  155.7 5.7 %collective-permute-done.12.r1 = bf16[256,512]{1,0:T(8,128)(2,1)S(1)} collective-permute-done((bf16[256,512]{1,0:T(8,128)(2,1)S(1)}, bf16[256,512]{1,0:T(8,128)(2,1)S(1)}, u32[]{:S(2)}, u32[]{:S(2)}) %collective-permute-start.12) | collective-permute-done | bytes 262176 | tf_op jit(solution)/shard_map/ppermute | solution.py:23
  161.4 5.8 %collective-permute-done.13.r2 = bf16[256,512]{1,0:T(8,128)(2,1)S(1)} collective-permute-done((bf16[256,512]{1,0:T(8,128)(2,1)S(1)}, bf16[256,512]{1,0:T(8,128)(2,1)S(1)}, u32[]{:S(2)}, u32[]{:S(2)}) %collective-permute-start.13) | collective-permute-done | bytes 262176 | tf_op jit(solution)/shard_map/ppermute | solution.py:23
  167.2 3.0 %collective-permute-done.14.r3 = bf16[256,512]{1,0:T(8,128)(2,1)S(1)} collective-permute-done((bf16[256,512]{1,0:T(8,128)(2,1)S(1)}, bf16[256,512]{1,0:T(8,128)(2,1)S(1)}, u32[]{:S(2)}, u32[]{:S(2)}) %collective-permute-start.14) | collective-permute-done | bytes 262176 | tf_op jit(solution)/shard_map/ppermute | solution.py:23
  170.9 4.0 %finish.3 = bf16[8,64,512]{2,1,0:T(8,128)(2,1)} custom-call(s32[4]{0:T(128)} %copy-done.19, f32[256,512]{1,0:T(8,128)} %copy-done.9, bf16[256,512]{1,0:T(8,128)(2,1)} %copy-done.13, bf16[256,512]{1,0:T(8,128)(2,1)} %copy-done.14, bf16[256,512]{1,0:T(8,128)(2,1)} %copy-done.15, bf16[8,64,512]{2,1,0:T(8,128)(2,1)} %finish.2.refs_0_), custom_call_target="tpu_custom_call", output_to_operand_aliasing={{}: (5, {})} | custom-call | flops 1000000 | bytes 2097152 | tf_op jit(solution)/shard_map/finish/pallas_call | solution.py:268
  (96 shorter events, 13.2 us)
Async XLA Ops:
  6.7 36.8 %copy-start.2 = (bf16[4,8,64,128]{3,2,1,0:T(8,128)(2,1)S(1)}, bf16[4,8,64,128]{3,2,1,0:T(8,128)(2,1)}, u32[]{:S(2)}) copy-start(bf16[4,8,64,128]{3,2,1,0:T(8,128)(2,1)} %take_rows.1.refs_0_.refs_4_.refs_8_.refs_1_) | copy-start | bytes 1572868
  6.7 27.5 %collective-permute-start = (bf16[4,8,64,128]{3,2,1,0:T(8,128)(2,1)}, bf16[4,8,64,128]{3,2,1,0:T(8,128)(2,1)S(1)}, u32[]{:S(2)}, u32[]{:S(2)}) collective-permute-start(bf16[4,8,64,128]{3,2,1,0:T(8,128)(2,1)} %take_rows.1.refs_0_.refs_4_.refs_8_.refs_1_), channel_id=1, source_target_pairs={{0,32},{32,0},{1,33},{33,1},{2,34},{34,2},{3,35},{35,3},{4,36},{36... | collective-permute-start | bytes 1572872 | tf_op jit(solution)/shard_map/ppermute | solution.py:23
  11.2 34.7 %copy-start.20 = (s32[4]{0:T(128)}, s32[4]{0:T(128)S(1)}, u32[]{:S(2)}) copy-start(s32[4]{0:T(128)S(1)} %get-tuple-element.53.sc) | copy-start | bytes 52
  11.2 51.9 %copy-start.19 = (s32[4]{0:T(128)}, s32[4]{0:T(128)S(1)}, u32[]{:S(2)}) copy-start(s32[4]{0:T(128)S(1)} %get-tuple-element.54.sc) | copy-start | bytes 52
  14.9 1.2 copy-start.3
  16.1 1.0 copy-start.5
  17.2 1.0 copy-start.7
  23.6 27.4 %copy-start.12 = (f32[512]{0:T(512)S(1)}, f32[512]{0:T(512)}, u32[]{:S(2)}) copy-start(f32[512]{0:T(512)} %param.21) | copy-start | bytes 6148
  23.6 11.1 %collective-permute-start.15 = (f32[4,1,64]{2,1,0:T(1,128)S(1)}, f32[4,1,64]{2,1,0:T(1,128)S(1)}, u32[]{:S(2)}, u32[]{:S(2)}) collective-permute-start(f32[4,1,64]{2,1,0:T(1,128)S(1)} %get-tuple-element.30.s0), channel_id=1, source_target_pairs={{0,1},{1,2},{2,3},{3,0},{4,5},{5,6},{6,7},{7,4},{8,9},{9,10},{10,1... | collective-permute-start | bytes 3080 | tf_op jit(solution)/shard_map/ppermute | solution.py:23
  26.9 7.9 %collective-permute-start.16 = (f32[4,1,64]{2,1,0:T(1,128)S(1)}, f32[4,1,64]{2,1,0:T(1,128)S(1)}, u32[]{:S(2)}, u32[]{:S(2)}) collective-permute-start(f32[4,1,64]{2,1,0:T(1,128)S(1)} %get-tuple-element.30.s0), channel_id=1, source_target_pairs={{0,2},{1,3},{2,0},{3,1},{4,6},{5,7},{6,4},{7,5},{8,10},{9,11},{10,... | collective-permute-start | bytes 3080 | tf_op jit(solution)/shard_map/ppermute | solution.py:23
  31.4 4.5 %collective-permute-start.17 = (f32[4,1,64]{2,1,0:T(1,128)S(1)}, f32[4,1,64]{2,1,0:T(1,128)S(1)}, u32[]{:S(2)}, u32[]{:S(2)}) collective-permute-start(f32[4,1,64]{2,1,0:T(1,128)S(1)} %get-tuple-element.30.s0), channel_id=1, source_target_pairs={{0,3},{1,0},{2,1},{3,2},{4,7},{5,4},{6,5},{7,6},{8,11},{9,8},{10,9... | collective-permute-start | bytes 3080 | tf_op jit(solution)/shard_map/ppermute | solution.py:23
  34.0 9.4 %collective-permute-start.1 = (bf16[4,8,64,128]{3,2,1,0:T(8,128)(2,1)}, bf16[4,8,64,128]{3,2,1,0:T(8,128)(2,1)S(1)}, u32[]{:S(2)}, u32[]{:S(2)}) collective-permute-start(bf16[4,8,64,128]{3,2,1,0:T(8,128)(2,1)} %take_rows.1.refs_0_.refs_4_.refs_8_.refs_1_), channel_id=1, source_target_pairs={{0,16},{16,0},{1,17},{17,1},{2,18},{18,2},{3,19},{19,3},{4,20},{20... | collective-permute-start | bytes 1572872 | tf_op jit(solution)/shard_map/ppermute | solution.py:23
  34.1 9.3 %collective-permute-start.2 = (bf16[4,8,64,128]{3,2,1,0:T(8,128)(2,1)S(1)}, bf16[4,8,64,128]{3,2,1,0:T(8,128)(2,1)S(1)}, u32[]{:S(2)}, u32[]{:S(2)}) collective-permute-start(bf16[4,8,64,128]{3,2,1,0:T(8,128)(2,1)S(1)} %collective-permute-done.refs_1_.refs_5_.refs_9_.refs_2_), channel_id=1, source_target_pairs={{0,16},{16,0},{1,17},{17,1},{2,18},{18,2},{3,19},{19,3},{4,20},{20... | collective-permute-start | bytes 1572872 | tf_op jit(solution)/shard_map/ppermute | solution.py:23
  35.9 3.4 %copy-start = (bf16[512,8192]{1,0:T(8,128)(2,1)S(1)}, bf16[512,8192]{1,0:T(8,128)(2,1)}, u32[]{:S(2)}) copy-start(bf16[512,8192]{1,0:T(8,128)(2,1)} %w.15) | copy-start | bytes 25165828
  39.2 0.7 copy-start.11
  42.5 53.9 %collective-permute-start.18 = (bf16[256,2048]{1,0:T(8,128)(2,1)}, bf16[256,2048]{1,0:T(8,128)(2,1)}, u32[]{:S(2)}, u32[]{:S(2)}) collective-permute-start(bf16[256,2048]{1,0:T(8,128)(2,1)} %project.9), channel_id=1, source_target_pairs={{0,8},{4,12},{8,0},{12,4},{1,9},{5,13},{9,1},{13,5},{2,10},{6,14},... | collective-permute-start | bytes 3145736 | tf_op jit(solution)/shard_map/ppermute | solution.py:23
  45.8 15.1 %collective-permute-start.3 = (bf16[4,8,64,128]{3,2,1,0:T(8,128)(2,1)}, bf16[4,8,64,128]{3,2,1,0:T(8,128)(2,1)S(1)}, u32[]{:S(2)}, u32[]{:S(2)}) collective-permute-start(bf16[4,8,64,128]{3,2,1,0:T(8,128)(2,1)} %get-tuple-element.19), channel_id=1, source_target_pairs={{0,64},{64,128},{128,192},{192,0},{1,65},{65,129},{129,193},{193,1... | collective-permute-start | bytes 1572872 | tf_op jit(solution)/shard_map/ppermute | solution.py:23
  47.4 16.7 %collective-permute-start.4 = (bf16[4,8,64,128]{3,2,1,0:T(8,128)(2,1)}, bf16[4,8,64,128]{3,2,1,0:T(8,128)(2,1)}, u32[]{:S(2)}, u32[]{:S(2)}) collective-permute-start(bf16[4,8,64,128]{3,2,1,0:T(8,128)(2,1)} %get-tuple-element.20), channel_id=1, source_target_pairs={{0,128},{64,192},{128,0},{192,64},{1,129},{65,193},{129,1},{193,65... | collective-permute-start | bytes 1572872 | tf_op jit(solution)/shard_map/ppermute | solution.py:23
  48.4 23.6 %collective-permute-start.5 = (bf16[4,8,64,128]{3,2,1,0:T(8,128)(2,1)}, bf16[4,8,64,128]{3,2,1,0:T(8,128)(2,1)}, u32[]{:S(2)}, u32[]{:S(2)}) collective-permute-start(bf16[4,8,64,128]{3,2,1,0:T(8,128)(2,1)} %get-tuple-element.21), channel_id=1, source_target_pairs={{0,192},{64,0},{128,64},{192,128},{1,193},{65,1},{129,65},{193,129... | collective-permute-start | bytes 1572872 | tf_op jit(solution)/shard_map/ppermute | solution.py:23
  51.0 3.4 %copy-start.1 = (bf16[512,8192]{1,0:T(8,128)(2,1)S(1)}, bf16[512,8192]{1,0:T(8,128)(2,1)}, u32[]{:S(2)}) copy-start(bf16[512,8192]{1,0:T(8,128)(2,1)} %w.15) | copy-start | bytes 25165828
  54.4 17.6 %copy-start.4 = (bf16[8,8,64,128]{3,2,1,0:T(8,128)(2,1)S(1)}, bf16[8,8,64,128]{3,2,1,0:T(8,128)(2,1)}, u32[]{:S(2)}) copy-start(bf16[8,8,64,128]{3,2,1,0:T(8,128)(2,1)} %refs_0_.3) | copy-start | bytes 3145732
  54.4 17.6 %copy-start.6 = (bf16[8,64,512]{2,1,0:T(8,128)(2,1)S(1)}, bf16[8,64,512]{2,1,0:T(8,128)(2,1)}, u32[]{:S(2)}) copy-start(bf16[8,64,512]{2,1,0:T(8,128)(2,1)} %x_ref.3) | copy-start | bytes 1572868
  54.4 17.6 %copy-start.8 = (bf16[8,64,512]{2,1,0:T(8,128)(2,1)S(1)}, bf16[8,64,512]{2,1,0:T(8,128)(2,1)}, u32[]{:S(2)}) copy-start(bf16[8,64,512]{2,1,0:T(8,128)(2,1)} %g_ref.3) | copy-start | bytes 1572868
  54.4 34.2 %slice-start = ((s8[8388608]{0:T(1024)(128)(4,1)}), s8[4194304]{0:T(1024)(128)(4,1)S(1)}, s32[]{:S(2)}) async-start(s8[8388608]{0:T(1024)(128)(4,1)} %bitcast.13), calls=%async_computation | async-start | bytes 8388608
  56.3 32.3 %slice-start.1 = ((s8[8388608]{0:T(1024)(128)(4,1)}), s8[4194304]{0:T(1024)(128)(4,1)S(1)}, s32[]{:S(2)}) async-start(s8[8388608]{0:T(1024)(128)(4,1)} %bitcast.13), calls=%async_computation.1 | async-start | bytes 8388608
  56.3 43.1 %collective-permute-start.19 = (bf16[256,2048]{1,0:T(8,128)(2,1)S(1)}, bf16[256,2048]{1,0:T(8,128)(2,1)S(1)}, u32[]{:S(2)}, u32[]{:S(2)}) collective-permute-start(bf16[256,2048]{1,0:T(8,128)(2,1)S(1)} %project.10), channel_id=1, source_target_pairs={{0,4},{4,8},{8,12},{12,0},{1,5},{5,9},{9,13},{13,1},{2,6},{6,10},{... | collective-permute-start | bytes 3145736 | tf_op jit(solution)/shard_map/ppermute | solution.py:23
  60.9 38.5 %collective-permute-start.20 = (bf16[256,2048]{1,0:T(8,128)(2,1)S(1)}, bf16[256,2048]{1,0:T(8,128)(2,1)S(1)}, u32[]{:S(2)}, u32[]{:S(2)}) collective-permute-start(bf16[256,2048]{1,0:T(8,128)(2,1)S(1)} %project.11), channel_id=1, source_target_pairs={{0,12},{4,0},{8,4},{12,8},{1,13},{5,1},{9,5},{13,9},{2,14},{6,2},{... | collective-permute-start | bytes 3145736 | tf_op jit(solution)/shard_map/ppermute | solution.py:23
  78.4 5.7 %collective-permute-start.6 = (f32[4,1,64]{2,1,0:T(1,128)S(1)}, f32[4,1,64]{2,1,0:T(1,128)S(1)}, u32[]{:S(2)}, u32[]{:S(2)}) collective-permute-start(f32[4,1,64]{2,1,0:T(1,128)S(1)} %get-tuple-element.24.s0), channel_id=1, source_target_pairs={{0,1},{1,2},{2,3},{3,0},{4,5},{5,6},{6,7},{7,4},{8,9},{9,10},{10,1... | collective-permute-start | bytes 3080 | tf_op jit(solution)/shard_map/ppermute | solution.py:23
  79.7 7.5 %collective-permute-start.7 = (f32[4,1,64]{2,1,0:T(1,128)S(1)}, f32[4,1,64]{2,1,0:T(1,128)S(1)}, u32[]{:S(2)}, u32[]{:S(2)}) collective-permute-start(f32[4,1,64]{2,1,0:T(1,128)S(1)} %get-tuple-element.24.s0), channel_id=1, source_target_pairs={{0,2},{1,3},{2,0},{3,1},{4,6},{5,7},{6,4},{7,5},{8,10},{9,11},{10,... | collective-permute-start | bytes 3080 | tf_op jit(solution)/shard_map/ppermute | solution.py:23
  84.1 4.5 %collective-permute-start.8 = (f32[4,1,64]{2,1,0:T(1,128)S(1)}, f32[4,1,64]{2,1,0:T(1,128)S(1)}, u32[]{:S(2)}, u32[]{:S(2)}) collective-permute-start(f32[4,1,64]{2,1,0:T(1,128)S(1)} %get-tuple-element.24.s0), channel_id=1, source_target_pairs={{0,3},{1,0},{2,1},{3,2},{4,7},{5,4},{6,5},{7,6},{8,11},{9,8},{10,9... | collective-permute-start | bytes 3080 | tf_op jit(solution)/shard_map/ppermute | solution.py:23
  90.4 44.6 %collective-permute-start.11 = (bf16[256,2048]{1,0:T(8,128)(2,1)S(1)}, bf16[256,2048]{1,0:T(8,128)(2,1)S(1)}, u32[]{:S(2)}, u32[]{:S(2)}) collective-permute-start(bf16[256,2048]{1,0:T(8,128)(2,1)S(1)} %project.8), channel_id=1, source_target_pairs={{0,12},{4,0},{8,4},{12,8},{1,13},{5,1},{9,5},{13,9},{2,14},{6,2},{... | collective-permute-start | bytes 3145736 | tf_op jit(solution)/shard_map/ppermute | solution.py:23
  94.5 40.5 %collective-permute-start.10 = (bf16[256,2048]{1,0:T(8,128)(2,1)S(1)}, bf16[256,2048]{1,0:T(8,128)(2,1)S(1)}, u32[]{:S(2)}, u32[]{:S(2)}) collective-permute-start(bf16[256,2048]{1,0:T(8,128)(2,1)S(1)} %project.7), channel_id=1, source_target_pairs={{0,4},{4,8},{8,12},{12,0},{1,5},{5,9},{9,13},{13,1},{2,6},{6,10},{... | collective-permute-start | bytes 3145736 | tf_op jit(solution)/shard_map/ppermute | solution.py:23
  96.4 43.5 %collective-permute-start.9 = (bf16[256,2048]{1,0:T(8,128)(2,1)S(1)}, bf16[256,2048]{1,0:T(8,128)(2,1)S(1)}, u32[]{:S(2)}, u32[]{:S(2)}) collective-permute-start(bf16[256,2048]{1,0:T(8,128)(2,1)S(1)} %project.6), channel_id=1, source_target_pairs={{0,8},{4,12},{8,0},{12,4},{1,9},{5,13},{9,1},{13,5},{2,10},{6,14},... | collective-permute-start | bytes 3145736 | tf_op jit(solution)/shard_map/ppermute | solution.py:23
  103.5 39.4 %copy-start.10 = (f32[256,512]{1,0:T(8,128)}, f32[256,512]{1,0:T(8,128)S(1)}, u32[]{:S(2)}) copy-start(f32[256,512]{1,0:T(8,128)S(1)} %get-tuple-element.31.z0) | copy-start | bytes 1572868
  103.5 45.3 %collective-permute-start.21 = (bf16[256,512]{1,0:T(8,128)(2,1)S(1)}, bf16[256,512]{1,0:T(8,128)(2,1)S(1)}, u32[]{:S(2)}, u32[]{:S(2)}) collective-permute-start(bf16[256,512]{1,0:T(8,128)(2,1)S(1)} %get-tuple-element.32), channel_id=1, source_target_pairs={{0,1},{1,2},{2,3},{3,0},{4,5},{5,6},{6,7},{7,4},{8,9},{9,10},{10,1... | collective-permute-start | bytes 786440 | tf_op jit(solution)/shard_map/ppermute | solution.py:23
  105.6 45.3 %collective-permute-start.22 = (bf16[256,512]{1,0:T(8,128)(2,1)S(1)}, bf16[256,512]{1,0:T(8,128)(2,1)S(1)}, u32[]{:S(2)}, u32[]{:S(2)}) collective-permute-start(bf16[256,512]{1,0:T(8,128)(2,1)S(1)} %get-tuple-element.33), channel_id=1, source_target_pairs={{0,2},{1,3},{2,0},{3,1},{4,6},{5,7},{6,4},{7,5},{8,10},{9,11},{10,... | collective-permute-start | bytes 786440 | tf_op jit(solution)/shard_map/ppermute | solution.py:23
  135.0 15.9 %collective-permute-start.23 = (bf16[256,512]{1,0:T(8,128)(2,1)S(1)}, bf16[256,512]{1,0:T(8,128)(2,1)S(1)}, u32[]{:S(2)}, u32[]{:S(2)}) collective-permute-start(bf16[256,512]{1,0:T(8,128)(2,1)S(1)} %get-tuple-element.34), channel_id=1, source_target_pairs={{0,3},{1,0},{2,1},{3,2},{4,7},{5,4},{6,5},{7,6},{8,11},{9,8},{10,9... | collective-permute-start | bytes 786440 | tf_op jit(solution)/shard_map/ppermute | solution.py:23
  142.9 0.8 copy-start.9
  143.7 17.7 %collective-permute-start.12 = (bf16[256,512]{1,0:T(8,128)(2,1)S(1)}, bf16[256,512]{1,0:T(8,128)(2,1)S(1)}, u32[]{:S(2)}, u32[]{:S(2)}) collective-permute-start(bf16[256,512]{1,0:T(8,128)(2,1)S(1)} %get-tuple-element.26), channel_id=1, source_target_pairs={{0,1},{1,2},{2,3},{3,0},{4,5},{5,6},{6,7},{7,4},{8,9},{9,10},{10,1... | collective-permute-start | bytes 786440 | tf_op jit(solution)/shard_map/ppermute | solution.py:23
  146.3 20.9 %collective-permute-start.13 = (bf16[256,512]{1,0:T(8,128)(2,1)S(1)}, bf16[256,512]{1,0:T(8,128)(2,1)S(1)}, u32[]{:S(2)}, u32[]{:S(2)}) collective-permute-start(bf16[256,512]{1,0:T(8,128)(2,1)S(1)} %get-tuple-element.27), channel_id=1, source_target_pairs={{0,2},{1,3},{2,0},{3,1},{4,6},{5,7},{6,4},{7,5},{8,10},{9,11},{10,... | collective-permute-start | bytes 786440 | tf_op jit(solution)/shard_map/ppermute | solution.py:23
  148.9 2.1 %copy-start.16 = (bf16[256,512]{1,0:T(8,128)(2,1)}, bf16[256,512]{1,0:T(8,128)(2,1)S(1)}, u32[]{:S(2)}) copy-start(bf16[256,512]{1,0:T(8,128)(2,1)S(1)} %collective-permute-done.21.r1) | copy-start | bytes 786436
  148.9 21.4 %collective-permute-start.14 = (bf16[256,512]{1,0:T(8,128)(2,1)S(1)}, bf16[256,512]{1,0:T(8,128)(2,1)S(1)}, u32[]{:S(2)}, u32[]{:S(2)}) collective-permute-start(bf16[256,512]{1,0:T(8,128)(2,1)S(1)} %get-tuple-element.28), channel_id=1, source_target_pairs={{0,3},{1,0},{2,1},{3,2},{4,7},{5,4},{6,5},{7,6},{8,11},{9,8},{10,9... | collective-permute-start | bytes 786440 | tf_op jit(solution)/shard_map/ppermute | solution.py:23
  150.9 0.7 copy-start.17
  150.9 0.8 copy-start.18
  161.4 8.8 %copy-start.13 = (bf16[256,512]{1,0:T(8,128)(2,1)}, bf16[256,512]{1,0:T(8,128)(2,1)S(1)}, u32[]{:S(2)}) copy-start(bf16[256,512]{1,0:T(8,128)(2,1)S(1)} %collective-permute-done.12.r1) | copy-start | bytes 786436
  167.2 3.0 %copy-start.14 = (bf16[256,512]{1,0:T(8,128)(2,1)}, bf16[256,512]{1,0:T(8,128)(2,1)S(1)}, u32[]{:S(2)}) copy-start(bf16[256,512]{1,0:T(8,128)(2,1)S(1)} %collective-permute-done.13.r2) | copy-start | bytes 786436
  170.2 0.7 copy-start.15

commit v2 on v1

v2 whole, which is shorter than its diff:
```python
import functools
import jax
import jax.numpy as jnp
import numpy as np
from jax import lax
from jax.experimental import pallas as pl
from jax.experimental.pallas import tpu as pltpu
from jax.sharding import Mesh, PartitionSpec as P

F32 = jnp.float32
BF16 = jnp.bfloat16
SIZES = {"y": 4, "zl": 2, "c": 2, "x": 4, "zh": 4}
ROWS = 8
HALF = 4
NEW = 64
NT = (((1,), (1,)), ((), ()))
TN = (((0,), (0,)), ((), ()))
LIMIT = pltpu.CompilerParams(vmem_limit_bytes=16 << 20)
WIDE = pltpu.CompilerParams(vmem_limit_bytes=57 << 20)
FREE = pl.CostEstimate(flops=0, bytes_accessed=0, transcendentals=0)
ANYWHERE = pl.BlockSpec(memory_space=pl.ANY)
STATE = (1, 8, 64, 128)

LEAVE, ORDER, LENGTH, CODE, INDEX = 0, 8, 16, 24, 32
BESIDE, BESIDE_ROW, ACROSS, ACROSS_ROW = 40, 48, 56, 64
X_AT, C_AT, ZH_AT = 72, 73, 74


def shift(value, axis, step):
    size = SIZES[axis]
    return lax.ppermute(value, axis, [(i, (i + step) % size) for i in range(size)])


def flip(value, mask):
    return lax.ppermute(value, "x", [(i, i ^ mask) for i in range(4)])


def route_kernel(place, lengths, anchor, out):
    y, zl, c, x, zh = (place[k] for k in range(5))
    me = (y * 2 + zl) * 2 + c
    lane = lax.broadcasted_iota(jnp.int32, (128, 128), 1)
    sub = lax.broadcasted_iota(jnp.int32, (128, 128), 0)
    here = jnp.broadcast_to(anchor[...].astype(F32), (128, 128))
    a_i = here.astype(jnp.int32)
    a_j = jnp.transpose(here).astype(jnp.int32)
    one = lambda mask: jnp.where(mask, 1, 0)
    earlier = one(sub < lane)
    same_dest = one((sub >> 3) == (lane >> 3))
    moves_i = one((a_i >> 3) != (lane >> 3))
    moves_j = one((a_j >> 3) != (sub >> 3))
    total = lambda m: jnp.sum(m.astype(F32), axis=0, keepdims=True).astype(jnp.int32)
    leave_slot = total(moves_j * one((a_j >> 3) == (a_i >> 3)) * earlier)
    before = moves_j * same_dest * earlier
    column_slot = total(before * one(((a_j >> 3) & 3) == ((a_i >> 3) & 3)))
    side_slot = total(before * one(((a_j >> 4) & 1) == ((a_i >> 4) & 1)))
    alike = one(moves_j == moves_i) * earlier
    rank = total(same_dest * (alike + moves_i * (1 - moves_j)))

    row = lambda v: jnp.broadcast_to(v, (8, 128))
    lane8 = lax.broadcasted_iota(jnp.int32, (8, 128), 1)
    q = lax.broadcasted_iota(jnp.int32, (8, 128), 0)
    a8 = row(a_i[0:1])
    leave8, column8, side8, rank8 = row(leave_slot), row(column_slot), row(side_slot), row(rank)
    source = a8 >> 3
    dest = lane8 >> 3
    moving = one(source != dest)
    source_row = a8 & 7
    hops = ((dest >> 2) - (source >> 2)) & 3
    same_zl = one(((source ^ dest) & 2) == 0)
    same_c = one(((source ^ dest) & 1) == 0)
    pick = lambda mask, yes, no: jnp.where(mask == 1, yes, no)
    code = moving * pick(same_zl, pick(same_c, 1 + hops, 5), 6)
    index = pick(
        moving, pick(same_zl, pick(same_c, leave8, column8), side8), source_row
    )
    length8 = jnp.zeros((8, 128), jnp.int32)
    for j in range(ROWS):
        length8 = jnp.where((lane8 & 7) == j, lengths[j], length8)
    take = lambda mask, value: jnp.sum((mask * value).astype(F32), axis=1, keepdims=True)
    leaving = moving * one(source == me) * one(leave8 == q)
    mine = one(dest == me) * one(rank8 == q)
    target = jnp.where(q < 4, (y * 2 + zl) * 2, (y * 2 + 1 - zl) * 2) + 1 - c
    beside = moving * one((source & 3) == zl * 2 + c) * one(dest == target)
    beside = beside * one(column8 == (q & 3))
    across = moving * one(((source >> 1) & 1) == zl) * one(dest == (y * 2 + 1 - zl) * 2 + c)
    across = across * one(side8 == q)
    own_column = one((source & 1) == c)
    parts = [
        take(leaving, source_row),
        take(mine, lane8 & 7),
        take(mine, length8),
        take(mine, code),
        take(mine, index),
        take(beside, hops),
        take(beside, leave8),
        take(across, pick(own_column, hops, 4)),
        take(across, pick(own_column, leave8, 4 + column8)),
    ]
    at = q[:, 0:1]
    tail = jnp.where(at == 0, x, jnp.where(at == 1, c, jnp.where(at == 2, zh, 0))).astype(F32)
    parts.append(tail)
    parts.append(jnp.zeros((128 - 8 * len(parts), 1), F32))
    column = jnp.concatenate(parts, axis=0)
    table = jnp.transpose(jnp.broadcast_to(column, (128, 128)))
    out[...] = table[0:1].astype(jnp.int32)


def route(place, tool_length, anchor):
    smem = pl.BlockSpec(memory_space=pltpu.SMEM)
    table = pl.pallas_call(
        route_kernel,
        in_specs=[smem, smem, pl.BlockSpec(memory_space=pltpu.VMEM)],
        out_specs=pl.BlockSpec(memory_space=pltpu.VMEM),
        out_shape=jax.ShapeDtypeStruct((1, 128), jnp.int32),
        compiler_params=LIMIT,
        cost_estimate=FREE,
        name="route",
    )(place, tool_length, anchor.reshape(1, 128))
    return table.reshape(128)


def per_head(ref):
    first = lax.broadcasted_iota(jnp.int32, (1, 128), 1) < 64
    return jnp.concatenate([jnp.where(first, ref[2 * p], ref[2 * p + 1]) for p in range(4)], axis=0)


def fly(value):
    near = lax.ppermute(value, "zh", [(i, i ^ 1) for i in range(4)])
    half = value + near
    return [half, lax.ppermute(half, "zh", [(i, i ^ 3) for i in range(4)])]


def product(left, right):
    return jnp.dot(left, right, preferred_element_type=F32)


def thirds(value):
    parts = []
    for _ in range(3):
        parts.append(value.astype(BF16))
        value = value - parts[-1].astype(F32)
    return parts


def ssm_kernel(start, count, unused, sc, x_ref, g_ref, b_ref, c_ref, dt_ref, bias, rate, skip, *refs):
    sources, refs = refs[:count], refs[count + unused :]
    gated_ref, sq_ref, new_ref, s_all, sems = refs
    r = pl.program_id(0)
    length = sc[LENGTH + start + r]

    @pl.when(r == 0)
    def _():
        for k in range(HALF):
            for which, source in enumerate(sources):

                @pl.when(sc[CODE + start + k] == which)
                def _():
                    pltpu.make_async_copy(
                        source.at[sc[INDEX + start + k]], s_all.at[k], sems.at[k]
                    ).start()

    pltpu.make_async_copy(sources[0].at[0], s_all.at[r], sems.at[r]).wait()
    held = s_all.at[r]
    lane = lax.broadcasted_iota(jnp.int32, (NEW, 128), 1)
    sub = lax.broadcasted_iota(jnp.int32, (NEW, 128), 0)
    within = lane & 63
    causal = within <= sub
    eye = within == sub
    first_half = lane < 64
    live = sub < length
    rows = lax.broadcasted_iota(jnp.int32, (128, 128), 0)
    cols = lax.broadcasted_iota(jnp.int32, (128, 128), 1)
    same = (rows >> 6) == (cols >> 6)
    same_head = jnp.where(same, 1.0, 0.0).astype(BF16)
    upper = jnp.where(same & (rows <= cols), 1.0, 0.0).astype(BF16)
    bias4, rate4, skip4 = per_head(bias), per_head(rate), per_head(skip)
    steps = dt_ref[0]
    raw = bias4 + jnp.concatenate(
        [
            jnp.concatenate([steps[2 * p : 2 * p + 1], steps[2 * p + 1 : 2 * p + 2]], axis=1)
            for p in range(4)
        ],
        axis=0,
    )
    soft = jnp.maximum(raw, 0.0) + jnp.log1p(jnp.exp(-jnp.abs(raw)))
    lane4 = lax.broadcasted_iota(jnp.int32, (4, 128), 1) & 63
    dt4 = jnp.where(lane4 < length, soft, 0.0)
    a4 = -rate4 * dt4
    pieces = [jnp.where(causal, a4[p : p + 1], 0.0) for p in range(4)]
    pieces += [jnp.where(eye, dt4[p : p + 1], 0.0) for p in range(4)]
    spread = sum(product(part, same_head) for part in thirds(jnp.concatenate(pieces, axis=0)))
    stacked = jnp.concatenate([part.astype(F32) for part in thirds(a4)] + [a4 * 0.0], axis=0)
    both = product(stacked.astype(BF16), jnp.concatenate([upper, same_head], axis=1))
    both = both[0:4] + both[4:8] + both[8:12]
    ds4, tot4 = both[:, :128], both[:, 128:]
    wide = lax.broadcasted_iota(jnp.int32, (NEW, 4 * NEW), 1)
    tall = lax.broadcasted_iota(jnp.int32, (NEW, 4 * NEW), 0)
    group = jnp.where(wide == 4 * tall + sc[X_AT], 1.0, 0.0).astype(BF16)
    c_val = jnp.dot(group, c_ref[0], preferred_element_type=F32).astype(BF16)
    b_val = jnp.dot(group, b_ref[0], preferred_element_type=F32).astype(BF16)
    bb = jnp.concatenate([b_val, b_val], axis=0)
    affinity = lax.dot_general(c_val, bb, NT, preferred_element_type=F32)
    affinity = jnp.where(causal, affinity, 0.0)
    squares = jnp.zeros((NEW, 128), F32)
    for p in range(4):
        ds_t = spread[p * NEW : (p + 1) * NEW]
        dt_t = spread[(4 + p) * NEW : (5 + p) * NEW]
        mix = affinity * jnp.exp(ds_t - ds4[p : p + 1]) * dt4[p : p + 1]
        hi = mix.astype(BF16)
        lo = (mix - hi.astype(F32)).astype(BF16)
        xf = x_ref[0, :, p * 128 : (p + 1) * 128].astype(F32)
        blocks = jnp.concatenate(
            [jnp.where(first_half, xf, 0.0), jnp.where(first_half, 0.0, xf)], axis=0
        ).astype(BF16)
        inner = jnp.dot(hi, blocks, preferred_element_type=F32) + jnp.dot(
            lo, blocks, preferred_element_type=F32
        )
        state = held[2 * p : 2 * p + 2].reshape(128, 128)
        carried = lax.dot_general(c_val, state, NT, preferred_element_type=F32)
        out = inner + carried * jnp.exp(ds_t) + skip4[p : p + 1] * xf
        gf = g_ref[0, :, p * 128 : (p + 1) * 128].astype(F32)
        gated = jnp.where(live, out * (gf / (1.0 + jnp.exp(-gf))), 0.0)
        gated_ref[0, :, p * 128 : (p + 1) * 128] = gated
        squares = squares + gated * gated
        weighted = xf * (jnp.exp(tot4[p : p + 1] - ds_t) * dt_t)
        w_hi = weighted.astype(BF16)
        w_lo = (weighted - w_hi.astype(F32)).astype(BF16)
        both = jnp.concatenate([w_hi, w_lo], axis=0)
        update = lax.dot_general(both, bb, TN, preferred_element_type=F32)
        e_tot = jnp.exp(tot4[p : p + 1])
        for k in range(2):
            kept = state[k * 64 : (k + 1) * 64].astype(F32) * e_tot[:, k * 64 : k * 64 + 1]
            new_ref[0, 2 * p + k] = (kept + update[k * 64 : (k + 1) * 64]).astype(BF16)
    ones = jnp.ones((8, 128), BF16)
    sq = sum(
        lax.dot_general(ones, part, NT, preferred_element_type=F32) for part in thirds(squares)[:2]
    )
    sq_ref[0] = sq[0:1]


def run_ssm(table, start, x, gate, b, c, dt, scalars, sources, alias, after=()):
    row3 = lambda r, sc: (sc[ORDER + start + r], 0, 0)
    smem = pl.BlockSpec(memory_space=pltpu.SMEM)
    in_specs = [
        pl.BlockSpec((1, NEW, 512), row3),
        pl.BlockSpec((1, NEW, 512), row3),
        pl.BlockSpec((1, 4 * NEW, 128), row3),
        pl.BlockSpec((1, 4 * NEW, 128), row3),
        pl.BlockSpec((1, 8, NEW), row3),
        *[smem] * 3,
        *[ANYWHERE] * (len(sources) + len(after)),
    ]
    operands = [table, x, gate, b, c, dt, *scalars, *sources, *after]
    unused = len(after)
    aliases = {}
    if alias is not None:
        in_specs.append(ANYWHERE)
        aliases = {len(operands): 2}
        operands.append(alias)
        unused += 1
    return pl.pallas_call(
        functools.partial(ssm_kernel, start, len(sources), unused),
        grid_spec=pltpu.PrefetchScalarGridSpec(
            num_scalar_prefetch=1,
            grid=(HALF,),
            in_specs=in_specs,
            out_specs=[
                pl.BlockSpec((1, NEW, 512), lambda r, sc: (r, 0, 0)),
                pl.BlockSpec((1, 1, NEW), lambda r, sc: (r, 0, 0)),
                pl.BlockSpec(STATE, lambda r, sc: (sc[ORDER + start + r], 0, 0, 0)),
            ],
            scratch_shapes=[
                pltpu.VMEM((HALF, 8, 64, 128), BF16),
                pltpu.SemaphoreType.DMA((HALF,)),
            ],
        ),
        out_shape=[
            jax.ShapeDtypeStruct((HALF, NEW, 512), F32),
            jax.ShapeDtypeStruct((HALF, 1, NEW), F32),
            jax.ShapeDtypeStruct((ROWS, 8, 64, 128), BF16),
        ],
        input_output_aliases=aliases,
        compiler_params=LIMIT,
        cost_estimate=FREE,
        name="ssm",
    )(*operands)


def normalise_kernel(count, gated, *refs):
    sums, (gain, after, out) = refs[:count], refs[count:]
    rows = lax.broadcasted_iota(jnp.int32, (NEW, NEW), 0)
    cols = lax.broadcasted_iota(jnp.int32, (NEW, NEW), 1)
    for r in range(HALF):
        total = sum(part[r] for part in sums)
        scale = lax.rsqrt(total / 2048.0 + 1e-05)
        column = jnp.sum(jnp.where(rows == cols, scale, 0.0), axis=1, keepdims=True)
        out[r * NEW : (r + 1) * NEW] = (gated[r] * column * gain[...]).astype(BF16)


def normalise(gated, sums, gain, after):
    whole = pl.BlockSpec(memory_space=pltpu.VMEM)
    return pl.pallas_call(
        functools.partial(normalise_kernel, len(sums)),
        in_specs=[whole] * (2 + len(sums)) + [ANYWHERE],
        out_specs=whole,
        out_shape=jax.ShapeDtypeStruct((HALF * NEW, 512), BF16),
        compiler_params=LIMIT,
        cost_estimate=FREE,
        name="normalise",
    )(gated, *sums, gain, after)


def project_kernel(sc, a, near0, near1, w0, w1, got, other, after, out0, out1):
    for side, near, w, out in ((0, near0, w0, out0), (1, near1, w1, out1)):

        @pl.when(sc[C_AT] == 1)
        def _():
            out[...] = (product(a[...], w[...]) + product(near[...], got[side])).astype(BF16)

        @pl.when(sc[C_AT] != 1)
        def _():
            out[...] = (product(a[...], w[...]) + product(near[...], other[side])).astype(BF16)


def project(table, a, nears, parts, weights, after):
    rows = HALF * NEW
    whole = pl.BlockSpec(memory_space=pltpu.VMEM)
    return pl.pallas_call(
        project_kernel,
        grid_spec=pltpu.PrefetchScalarGridSpec(
            num_scalar_prefetch=1,
            grid=(1,),
            in_specs=[whole] * 7 + [ANYWHERE],
            out_specs=[whole] * 2,
        ),
        out_shape=[jax.ShapeDtypeStruct((rows, 1024), BF16)] * 2,
        compiler_params=LIMIT,
        cost_estimate=FREE,
        name="project",
    )(table, a, *nears, *parts, *weights, after)


def base_kernel(sc, a, near0, near1, w, got, other, after, out):
    for side, near in ((0, near0), (1, near1)):
        columns = slice(side * 1024, (side + 1) * 1024)

        @pl.when(sc[C_AT] == 0)
        def _():
            out[:, columns] = product(a[...], w[:, columns]) + product(near[...], got[side])

        @pl.when(sc[C_AT] != 0)
        def _():
            out[:, columns] = product(a[...], w[:, columns]) + product(near[...], other[side])


def base_project(table, a, nears, own, weights, after):
    rows = HALF * NEW
    whole = pl.BlockSpec(memory_space=pltpu.VMEM)
    return pl.pallas_call(
        base_kernel,
        grid_spec=pltpu.PrefetchScalarGridSpec(
            num_scalar_prefetch=1,
            grid=(1,),
            in_specs=[whole] * 6 + [ANYWHERE],
            out_specs=whole,
        ),
        out_shape=jax.ShapeDtypeStruct((rows, 2048), F32),
        compiler_params=LIMIT,
        cost_estimate=FREE,
        name="base",
    )(table, a, *nears, own, *weights, after)


def combine_kernel(sc, base, e0, e1, after, z0, z1, z2, z3):
    j = pl.program_id(0)
    arrived = jnp.where((sc[ZH_AT] + j) % 4 < 2, e0[...].astype(F32), e1[...].astype(F32))
    value = base[...] + arrived

    @pl.when(j == 0)
    def _():
        z0[...] = value

    for k, ref in ((1, z1), (2, z2), (3, z3)):

        @pl.when(j == k)
        def _():
            ref[...] = value.astype(BF16)


def combine(table, base, e0, e1, after):
    rows = HALF * NEW
    whole = pl.BlockSpec((rows, 512), lambda j, sc: (0, 0))
    at = lambda j, sc: (sc[ZH_AT] + j) % 4
    return pl.pallas_call(
        combine_kernel,
        grid_spec=pltpu.PrefetchScalarGridSpec(
            num_scalar_prefetch=1,
            grid=(4,),
            in_specs=[
                pl.BlockSpec((rows, 512), lambda j, sc: (0, at(j, sc))),
                pl.BlockSpec((rows, 512), lambda j, sc: (0, jnp.minimum(at(j, sc), 1))),
                pl.BlockSpec((rows, 512), lambda j, sc: (0, jnp.maximum(at(j, sc) - 2, 0))),
                ANYWHERE,
            ],
            out_specs=[whole] * 4,
        ),
        out_shape=[
            jax.ShapeDtypeStruct((rows, 512), F32),
            *[jax.ShapeDtypeStruct((rows, 512), BF16) for _ in range(3)],
        ],
        compiler_params=LIMIT,
        cost_estimate=FREE,
        name="combine",
    )(table, base, e0, e1, after)


def slice_kernel(first, count, sc, *refs):
    w, outs, sems = refs[0], refs[2 : 2 + count], refs[-1]
    x, c = sc[X_AT], sc[C_AT]
    starts = [(x ^ 1 ^ (3 * c)) * 2, (x ^ 3 ^ c) * 2 + 1, (x ^ 3) * 2, (x ^ 1) * 2 + 1, x]
    copies = []
    for k, out in enumerate(outs):
        start = starts[first + k]
        width = out.shape[1]
        columns = pl.ds(pl.multiple_of(start * width, width), width)
        for part in range(4):
            rows = pl.ds(part * 128, 128)
            copies.append(
                pltpu.make_async_copy(w.at[rows, columns], out.at[rows], sems.at[k, part])
            )
            copies[-1].start()
    for copy in copies:
        copy.wait()


def slices(table, w, after, first, last):
    widths = [1024, 1024, 1024, 1024, 2048][first:last]
    return pl.pallas_call(
        functools.partial(slice_kernel, first, len(widths)),
        grid_spec=pltpu.PrefetchScalarGridSpec(
            num_scalar_prefetch=1,
            grid=(1,),
            in_specs=[ANYWHERE] * 2,
            out_specs=[pl.BlockSpec(memory_space=pltpu.VMEM)] * len(widths),
            scratch_shapes=[pltpu.SemaphoreType.DMA((len(widths), 4))],
        ),
        out_shape=[jax.ShapeDtypeStruct((512, width), BF16) for width in widths],
        compiler_params=WIDE,
        cost_estimate=FREE,
        name="slices",
    )(table, w, after)


def hold_kernel(value, after, out):
    pass


def hold(value, after):
    return pl.pallas_call(
        hold_kernel,
        in_specs=[ANYWHERE] * 2,
        out_specs=ANYWHERE,
        out_shape=jax.ShapeDtypeStruct(value.shape, value.dtype),
        input_output_aliases={0: 0},
        compiler_params=LIMIT,
        cost_estimate=FREE,
        name="hold",
    )(value, after)


def join_kernel(first, second, after, out, sems):
    copies = [
        pltpu.make_async_copy(ref, out.at[k], sems.at[k]) for k, ref in enumerate((first, second))
    ]
    for copy in copies:
        copy.start()
    for copy in copies:
        copy.wait()


def join(first, second, after):
    return pl.pallas_call(
        join_kernel,
        in_specs=[ANYWHERE] * 3,
        out_specs=pl.BlockSpec(memory_space=pltpu.VMEM),
        out_shape=jax.ShapeDtypeStruct((2, *first.shape), first.dtype),
        scratch_shapes=[pltpu.SemaphoreType.DMA((2,))],
        compiler_params=LIMIT,
        cost_estimate=FREE,
        name="join",
    )(first, second, after)


def gather_kernel(z0, r1, r3, out):
    out[...] = z0[...] + r1[...].astype(F32) + r3[...].astype(F32)


def gather_sum(z0, r1, r3):
    whole = pl.BlockSpec(memory_space=pltpu.VMEM)
    return pl.pallas_call(
        gather_kernel,
        in_specs=[whole] * 3,
        out_specs=whole,
        out_shape=jax.ShapeDtypeStruct(z0.shape, F32),
        compiler_params=LIMIT,
        cost_estimate=FREE,
        name="gather_sum",
    )(z0, r1, r3)


def finish_kernel(count, first, sc, *refs):
    parts = refs[:count]
    out, held, sem = refs[-3:]
    value = parts[0][...]
    for part in parts[1:]:
        value = value + part[...].astype(F32)
    held[...] = value.astype(BF16)
    copies = [
        pltpu.make_async_copy(
            held.at[pl.ds(r * NEW, NEW)], out.at[sc[ORDER + first + r]], sem.at[r]
        )
        for r in range(HALF)
    ]
    for copy in copies:
        copy.start()
    for copy in copies:
        copy.wait()


def finish(table, parts, first, alias):
    whole = pl.BlockSpec(memory_space=pltpu.VMEM)
    in_specs = [whole] * len(parts)
    operands = [table, *parts]
    aliases = {}
    if alias is not None:
        in_specs.append(ANYWHERE)
        aliases = {len(operands): 0}
        operands.append(alias)
    return pl.pallas_call(
        functools.partial(finish_kernel, len(parts), first),
        grid_spec=pltpu.PrefetchScalarGridSpec(
            num_scalar_prefetch=1,
            grid=(1,),
            in_specs=in_specs,
            out_specs=ANYWHERE,
            scratch_shapes=[
                pltpu.VMEM((HALF * NEW, 512), BF16),
                pltpu.SemaphoreType.DMA((HALF,)),
            ],
        ),
        out_shape=jax.ShapeDtypeStruct((ROWS, NEW, 512), BF16),
        input_output_aliases=aliases,
        compiler_params=LIMIT,
        cost_estimate=FREE,
        name="finish",
    )(*operands)


def copy_kernel(sc, source, out):
    out[...] = source[...]


def leave(table, states):
    return pl.pallas_call(
        copy_kernel,
        grid_spec=pltpu.PrefetchScalarGridSpec(
            num_scalar_prefetch=1,
            grid=(HALF,),
            in_specs=[pl.BlockSpec(STATE, lambda q, sc: (sc[LEAVE + q], 0, 0, 0))],
            out_specs=pl.BlockSpec(STATE, lambda q, sc: (q, 0, 0, 0)),
        ),
        out_shape=jax.ShapeDtypeStruct((HALF, 8, 64, 128), BF16),
        compiler_params=LIMIT,
        cost_estimate=FREE,
        name="leave",
    )(table, states)


def pick_kernel(count, start, start_row, sc, *refs):
    sources, out, sems = refs[:count], refs[-2], refs[-1]
    slots = out.shape[0]
    for q in range(slots):
        for which in range(count):

            @pl.when(sc[start + q] == which)
            def _():
                row = sc[start_row + q]
                pltpu.make_async_copy(sources[which].at[row], out.at[q], sems.at[q]).start()

    for q in range(slots):
        pltpu.make_async_copy(sources[0].at[0], out.at[q], sems.at[q]).wait()


def pick(table, sources, start, start_row, slots, after):
    return pl.pallas_call(
        functools.partial(pick_kernel, len(sources), start, start_row),
        grid_spec=pltpu.PrefetchScalarGridSpec(
            num_scalar_prefetch=1,
            grid=(1,),
            in_specs=[ANYWHERE] * (len(sources) + 1),
            out_specs=pl.BlockSpec(memory_space=pltpu.VMEM),
            scratch_shapes=[pltpu.SemaphoreType.DMA((slots,))],
        ),
        out_shape=jax.ShapeDtypeStruct((slots, 8, 64, 128), BF16),
        compiler_params=LIMIT,
        cost_estimate=FREE,
        name="pick",
    )(table, *sources, after)


def local(
    ssm_input,
    gate_input,
    write_basis,
    read_basis,
    step_raw,
    step_bias,
    decay_rate,
    skip_gain,
    norm_gain,
    out_weight,
    ssm_states,
    anchor,
    tool_length,
):
    place = jnp.stack([lax.axis_index(n) for n in ("y", "zl", "c", "x", "zh")]).astype(jnp.int32)
    table = route(place, tool_length, anchor)
    buf = leave(table, ssm_states)
    along = [buf] + [shift(buf, "y", k) for k in (1, 2, 3)]

    shares = slices(table, out_weight, buf, 0, 2)
    got = [flip(shares[0], 1), flip(shares[1], 3)]

    b = write_basis.reshape(ROWS, 4 * NEW, 128)
    c = read_basis.reshape(ROWS, 4 * NEW, 128)
    gain = norm_gain.reshape(1, 512)
    ssm = functools.partial(
        run_ssm,
        table,
        x=ssm_input,
        gate=gate_input,
        b=b,
        c=c,
        dt=step_raw,
        scalars=(step_bias, decay_rate, skip_gain),
    )

    def spread_rows(gated, sums, after):
        a = normalise(gated, sums, gain, after)
        return a, [flip(a, 1), flip(a, 3)]

    def reduce_rest(base, moved, after):
        zs = combine(table, base, *moved, after)
        return [zs[0]] + [shift(zs[k], "zh", k) for k in (1, 2, 3)]

    gated1, sq1, states1 = ssm(start=0, sources=[ssm_states], alias=None, after=[shares[0]])
    sums1 = lax.psum(sq1, "zh")

    part0, part1, own = slices(table, out_weight, sums1, 2, 5)
    chosen = pick(table, along, BESIDE, BESIDE_ROW, 8, own)
    beside = shift(chosen, "c", 1)
    near_weights = join(*got, chosen)
    a1, nears1 = spread_rows(gated1, [sums1], near_weights)
    picked = pick(table, [*along, beside], ACROSS, ACROSS_ROW, HALF, a1)
    across = shift(picked, "zl", 1)
    near_weights = hold(near_weights, picked)
    weights = [near_weights, shift(near_weights, "c", 1)]
    sent1 = project(table, a1, nears1, [part0, part1], weights, picked)
    moved1 = [flip(sent1[0], 3), flip(sent1[1], 1)]
    base1 = base_project(table, a1, nears1, own, weights, sent1[0])

    gated2, sq2, new_states = ssm(
        start=HALF, sources=[ssm_states, *along, beside, across], alias=states1, after=[sent1[0]]
    )
    sums2 = fly(sq2)
    z0, r1, r2, r3 = reduce_rest(base1, moved1, sq2)
    a2, nears2 = spread_rows(gated2, sums2, z0)
    gathered = gather_sum(z0, r1, r3)
    sent2 = project(table, a2, nears2, [part0, part1], weights, gathered)
    moved2 = [flip(sent2[0], 3), flip(sent2[1], 1)]
    base2 = base_project(table, a2, nears2, own, weights, sent2[0])
    half_out = finish(table, [gathered, r2], 0, None)
    done2 = reduce_rest(base2, moved2, half_out)
    return finish(table, done2, HALF, half_out), new_states


def solution(mesh):
    fine = Mesh(mesh.devices.reshape(4, 2, 2, 4, 4), ("y", "zl", "c", "x", "zh"))
    dp, tp = ("y", "zl", "c"), ("x", "zh")
    placed = (
        P(dp, None, tp),
        P(dp, None, tp),
        P(dp, None, None, None),
        P(dp, None, None, None),
        P(dp, tp, None),
        P(tp),
        P(tp),
        P(tp),
        P(tp),
        P(tp, None),
        P(dp, tp, None, None),
        P(),
        P(dp),
    )
    return jax.shard_map(
        local,
        mesh=fine,
        in_specs=placed,
        out_specs=(P(dp, None, tp), P(dp, tp, None, None)),
        check_vma=False,
    )
```

time: 177 us -> 156 us (0.88)
  blocking collectives: 0 us -> 15.5 us
  waiting for transfers between devices: 59.8 us -> 48.7 us
  starting transfers between devices: 47.1 us -> 38.4 us
  local copies, waits for them, and re-layouts: 16.5 us -> 8.07 us
  other arithmetic: 5.32 us -> 0.01 us
  Pallas kernels: 44.7 us -> 42.4 us
    ppermute x24 -> x12, waiting for transfers between devices: 59.8 us -> 38 us  [shift(): lax.ppermute(value, axis, [(i, (i + step) % size) for i in range(size)])]
    ppermute x24 -> x12, starting transfers between devices: 47.1 us -> 25.7 us  [shift(): lax.ppermute(value, axis, [(i, (i + step) % size) for i in range(size)])]
    psum x0 -> x1, blocking collectives: none -> 15.5 us  [local(): sums1 = lax.psum(sq1, 'zh')]
    ppermute x0 -> x12, starting transfers between devices: none -> 12.7 us  [the longest x10 10.8 us: flip(): return lax.ppermute(value, 'x', [(i, i ^ mask) for i in range(4)])]
    ppermute x0 -> x12, waiting for transfers between devices: none -> 10.7 us  [the longest x10 6.47 us: flip(): return lax.ppermute(value, 'x', [(i, i ^ mask) for i in range(4)])]
    pallas_call x6 -> x2, Pallas kernels: 11.8 us -> 4.01 us  [project(): pl.pallas_call(project_kernel, grid_spec=pltpu.PrefetchScalarGridSpec(num...]
    pallas_call x8 -> x19, Pallas kernels: 32.9 us -> 38.4 us  [the longest x2 12.7 us: run_ssm(): pl.pallas_call(functools.partial(ssm_kernel, start, len(sources), unused)...]
    unnamed x48 -> x62, local copies, waits for them, and re-layouts: 13.1 us -> 7.98 us
  transfers between devices with their start and end apart: 24 -> 24, of which waited for: 12 -> 11; matrix products, arithmetic and copies ran while one was open for 4% -> 0% of each run, Pallas kernels for 21% -> 22%
where the time goes in v2:
time: 156 us; the launch traced here: 155 us
  waiting for transfers between devices  48.7 us (31%)
  Pallas kernels  42.4 us (27%)
  starting transfers between devices  38.4 us (25%)
  blocking collectives  15.5 us (10%)
  local copies, waits for them, and re-layouts  8.07 us (5%)
    ppermute x12, waiting for transfers between devices, shift(): lax.ppermute(value, axis, [(i, (i + step) % size) for i in range(size)])  38 us
    ppermute x12, starting transfers between devices, shift(): lax.ppermute(value, axis, [(i, (i + step) % size) for i in range(size)])  25.7 us
    psum x1, blocking collectives, local(): sums1 = lax.psum(sq1, 'zh')  15.5 us
    pallas_call x2, Pallas kernels, run_ssm(): pl.pallas_call(functools.partial(ssm_kernel, start, len(sources), unused)...  12.7 us
    ppermute x10, starting transfers between devices, flip(): return lax.ppermute(value, 'x', [(i, i ^ mask) for i in range(4)])  10.8 us
    pallas_call x2, Pallas kernels, slices(): pl.pallas_call(functools.partial(slice_kernel, first, len(widths)), grid_...  8.66 us
    unnamed x62, local copies, waits for them, and re-layouts  7.98 us
    ppermute x10, waiting for transfers between devices, flip(): return lax.ppermute(value, 'x', [(i, i ^ mask) for i in range(4)])  6.47 us
  transfers between devices with their start and end apart: 24, of which 11 were waited for; matrix products, arithmetic and copies ran while one was open for 0% of the time, Pallas kernels for 22%

profile of v2, /device:TPU:12, one launch (start us, length us, event | category | flops | bytes accessed | tf_op | source)
XLA Modules:
  0.0 154.5 jit_solution(9978690634814148279)
XLA Ops:
  2.0 0.9 route.1
  2.9 1.2 copy-done.4
  5.5 2.6 %collective-permute-start.1 = (bf16[4,8,64,128]{3,2,1,0:T(8,128)(2,1)S(1)}, bf16[4,8,64,128]{3,2,1,0:T(8,128)(2,1)S(1)}, u32[]{:S(2)}, u32[]{:S(2)}) collective-permute-start(bf16[4,8,64,128]{3,2,1,0:T(8,128)(2,1)S(1)} %leave.1.refs_1_.refs_0_), channel_id=1, source_target_pairs={{0,128},{64,192},{128,0},{192,64},{1,129},{65,193},{129,1},{193,65... | collective-permute-start | bytes 1572872 | tf_op jit(solution)/shard_map/ppermute | solution.py:31
  8.1 1.9 %collective-permute-start = (bf16[4,8,64,128]{3,2,1,0:T(8,128)(2,1)S(1)}, bf16[4,8,64,128]{3,2,1,0:T(8,128)(2,1)S(1)}, u32[]{:S(2)}, u32[]{:S(2)}) collective-permute-start(bf16[4,8,64,128]{3,2,1,0:T(8,128)(2,1)S(1)} %leave.1.refs_1_.refs_0_), channel_id=1, source_target_pairs={{0,64},{64,128},{128,192},{192,0},{1,65},{65,129},{129,193},{193,1... | collective-permute-start | bytes 1572872 | tf_op jit(solution)/shard_map/ppermute | solution.py:31
  10.0 3.6 %slices.2 = (bf16[512,1024]{1,0:T(8,128)(2,1)}, bf16[512,1024]{1,0:T(8,128)(2,1)}) custom-call(s32[128]{0:T(128)} %bitcast.15, bf16[512,8192]{1,0:T(8,128)(2,1)} %refs_0_.6, bf16[4,8,64,128]{3,2,1,0:T(8,128)(2,1)} %copy-done.2), custom_call_target="tpu_custom_call" | custom-call | tf_op jit(solution)/shard_map/slices/pallas_call | solution.py:438
  14.2 1.1 collective-permute-start.4
  15.4 1.2 copy-done.17
  17.3 6.2 %ssm.2 = (f32[4,64,512]{2,1,0:T(8,128)S(1)}, f32[4,1,64]{2,1,0:T(1,128)S(1)}, bf16[8,8,64,128]{3,2,1,0:T(8,128)(2,1)}) custom-call(s32[128]{0:T(128)S(1)} %bitcast.17, bf16[8,64,512]{2,1,0:T(8,128)(2,1)S(1)} %copy-done.9, bf16[8,64,512]{2,1,0:T(8,128)(2,1)S(1)} %copy-done.11, bf16[8,256,128]{2,1,0:T(8,128)(2,1)S(1)} %bitcast.10, ...), custom_call_target="tpu_custom_call" | custom-call | tf_op jit(solution)/shard_map/ssm/pallas_call | solution.py:261
  23.6 0.8 copy-done.18
  24.4 15.5 %psum.7.refs_1_.refs_0_ = f32[4,1,64]{2,1,0:T(1,128)} all-reduce(f32[4,1,64]{2,1,0:T(1,128)S(1)} %get-tuple-element.26), channel_id=1, replica_groups=mesh['y'=4,'zl'=2,'c'=2,'x'=4,'zh'=4] {'zh'}, use_global_device_ids=true, to_apply=%region_0.0 | all-reduce | flops 256 | bytes 2048 | tf_op jit(solution)/shard_map/psum | solution.py:657
  39.8 5.0 %slices.3 = (bf16[512,1024]{1,0:T(8,128)(2,1)}, bf16[512,1024]{1,0:T(8,128)(2,1)}, bf16[512,2048]{1,0:T(8,128)(2,1)}) custom-call(s32[128]{0:T(128)} %bitcast.16, bf16[512,8192]{1,0:T(8,128)(2,1)} %refs_0_.6, f32[4,1,64]{2,1,0:T(1,128)} %psum.7.refs_1_.refs_0_), custom_call_target="tpu_custom_call" | custom-call | tf_op jit(solution)/shard_map/slices/pallas_call | solution.py:438
  44.9 1.6 %copy-done = bf16[512,2048]{1,0:T(8,128)(2,1)S(1)} copy-done((bf16[512,2048]{1,0:T(8,128)(2,1)S(1)}, bf16[512,2048]{1,0:T(8,128)(2,1)}, u32[]{:S(2)}) %copy-start) | copy-done | bytes 2097176
  46.5 2.2 %pick.2.after = bf16[8,8,64,128]{3,2,1,0:T(8,128)(2,1)S(1)} custom-call(s32[128]{0:T(128)S(1)} %bitcast.18, bf16[4,8,64,128]{3,2,1,0:T(8,128)(2,1)S(1)} %copy-done.3, bf16[4,8,64,128]{3,2,1,0:T(8,128)(2,1)S(1)} %collective-permute-done.refs_1_.refs_2_, bf16[4,8,64,128]{3,2,1,0:T(8,128)(2,1)S(1)} %collective-permute-done.1.refs_2_.refs_3_, ...), custom_call_target="tpu_custom_call" | custom-call | tf_op jit(solution)/shard_map/pick/pallas_call | solution.py:595
  48.9 1.6 %join.1.refs_2_.value = bf16[2,512,1024]{2,1,0:T(8,128)(2,1)S(1)} custom-call(bf16[512,1024]{1,0:T(8,128)(2,1)} %collective-permute-done.4.first, bf16[512,1024]{1,0:T(8,128)(2,1)} %collective-permute-done.5.second, bf16[8,8,64,128]{3,2,1,0:T(8,128)(2,1)S(1)} %pick.2.after), custom_call_target="tpu_custom_call" | custom-call | tf_op jit(solution)/shard_map/join/pallas_call | solution.py:482
  50.7 0.9 collective-permute-done.3.refs_4_.refs_5_
  51.5 1.4 pick.3.after
  53.2 2.2 %collective-permute-start.8 = (bf16[256,512]{1,0:T(8,128)(2,1)S(1)}, bf16[256,512]{1,0:T(8,128)(2,1)S(1)}, u32[]{:S(2)}, u32[]{:S(2)}) collective-permute-start(bf16[256,512]{1,0:T(8,128)(2,1)S(1)} %normalise.2.refs_5_.a), channel_id=1, source_target_pairs={{0,12},{4,8},{8,4},{12,0},{1,13},{5,9},{9,5},{13,1},{2,14},{6,10},... | collective-permute-start | bytes 786440 | tf_op jit(solution)/shard_map/ppermute | solution.py:35
  55.4 0.8 collective-permute-start.7
  56.2 1.0 collective-permute-start.6
  57.2 5.0 %collective-permute-done.8.near1 = bf16[256,512]{1,0:T(8,128)(2,1)S(1)} collective-permute-done((bf16[256,512]{1,0:T(8,128)(2,1)S(1)}, bf16[256,512]{1,0:T(8,128)(2,1)S(1)}, u32[]{:S(2)}, u32[]{:S(2)}) %collective-permute-start.8) | collective-permute-done | bytes 262176 | tf_op jit(solution)/shard_map/ppermute | solution.py:35
  62.2 1.5 collective-permute-done.7.near0
  63.8 2.0 %project.2 = (bf16[256,1024]{1,0:T(8,128)(2,1)S(1)}, bf16[256,1024]{1,0:T(8,128)(2,1)S(1)}) custom-call(s32[128]{0:T(128)S(1)} %bitcast.20, bf16[256,512]{1,0:T(8,128)(2,1)S(1)} %normalise.2.refs_5_.a, bf16[256,512]{1,0:T(8,128)(2,1)S(1)} %collective-permute-done.7.near0, bf16[256,512]{1,0:T(8,128)(2,1)S(1)} %collective-permute-done.8.near1, ...), custom_call_target="tpu_custom_call" | custom-call | tf_op jit(solution)/shard_map/project/pallas_call | solution.py:328
  65.8 0.9 collective-permute-start.13
  66.7 0.9 collective-permute-start.12
  67.6 2.3 %collective-permute-done.6.refs_6_ = bf16[4,8,64,128]{3,2,1,0:T(8,128)(2,1)S(1)} collective-permute-done((bf16[4,8,64,128]{3,2,1,0:T(8,128)(2,1)S(1)}, bf16[4,8,64,128]{3,2,1,0:T(8,128)(2,1)S(1)}, u32[]{:S(2)}, u32[]{:S(2)}) %collective-permute-start.6) | collective-permute-done | bytes 524320 | tf_op jit(solution)/shard_map/ppermute | solution.py:31
  69.9 6.5 %ssm.3 = (f32[4,64,512]{2,1,0:T(8,128)S(1)}, f32[4,1,64]{2,1,0:T(1,128)S(1)}, bf16[8,8,64,128]{3,2,1,0:T(8,128)(2,1)}) custom-call(s32[128]{0:T(128)S(1)} %bitcast.21, bf16[8,64,512]{2,1,0:T(8,128)(2,1)S(1)} %copy-done.10, bf16[8,64,512]{2,1,0:T(8,128)(2,1)S(1)} %copy-done.12, bf16[8,256,128]{2,1,0:T(8,128)(2,1)S(1)} %bitcast.11, ...), custom_call_target="tpu_custom_call", output_to_operand_aliasing={{2}: (17, {})} | custom-call | tf_op jit(solution)/shard_map/ssm/pallas_call | solution.py:261
  76.9 4.2 %collective-permute-done.10 = f32[4,1,64]{2,1,0:T(1,128)S(1)} collective-permute-done((f32[4,1,64]{2,1,0:T(1,128)S(1)}, f32[4,1,64]{2,1,0:T(1,128)S(1)}, u32[]{:S(2)}, u32[]{:S(2)}) %collective-permute-start.10) | collective-permute-done | bytes 1056 | tf_op jit(solution)/shard_map/ppermute | solution.py:128
  81.1 1.5 collective-permute-start.11
  82.6 2.0 %base.2 = f32[256,2048]{1,0:T(8,128)S(1)} custom-call(s32[128]{0:T(128)S(1)} %bitcast.22, bf16[256,512]{1,0:T(8,128)(2,1)S(1)} %normalise.2.refs_5_.a, bf16[256,512]{1,0:T(8,128)(2,1)S(1)} %collective-permute-done.7.near0, bf16[256,512]{1,0:T(8,128)(2,1)S(1)} %collective-permute-done.8.near1, bf16[512,2048]{1,0:T(8,128)(2,1)S(1)} %copy-done.1, ...), custom_call_target="tpu_custom_call" | custom-call | tf_op jit(solution)/shard_map/base/pallas_call | solution.py:359
  84.6 1.7 %combine.2 = (f32[256,512]{1,0:T(8,128)S(1)}, bf16[256,512]{1,0:T(8,128)(2,1)S(1)}, bf16[256,512]{1,0:T(8,128)(2,1)S(1)}, bf16[256,512]{1,0:T(8,128)(2,1)S(1)}) custom-call(s32[128]{0:T(128)S(1)} %bitcast.23, f32[256,2048]{1,0:T(8,128)S(1)} %base.2, bf16[256,1024]{1,0:T(8,128)(2,1)S(1)} %collective-permute-done.12.e0, ...), custom_call_target="tpu_custom_call" | custom-call | tf_op jit(solution)/shard_map/combine/pallas_call | solution.py:394
  86.2 1.6 %collective-permute-start.16 = (bf16[256,512]{1,0:T(8,128)(2,1)S(1)}, bf16[256,512]{1,0:T(8,128)(2,1)S(1)}, u32[]{:S(2)}, u32[]{:S(2)}) collective-permute-start(bf16[256,512]{1,0:T(8,128)(2,1)S(1)} %get-tuple-element.38), channel_id=1, source_target_pairs={{0,1},{1,2},{2,3},{3,0},{4,5},{5,6},{6,7},{7,4},{8,9},{9,10},{10,1... | collective-permute-start | bytes 786440 | tf_op jit(solution)/shard_map/ppermute | solution.py:31
  87.8 2.6 %collective-permute-start.17 = (bf16[256,512]{1,0:T(8,128)(2,1)S(1)}, bf16[256,512]{1,0:T(8,128)(2,1)S(1)}, u32[]{:S(2)}, u32[]{:S(2)}) collective-permute-start(bf16[256,512]{1,0:T(8,128)(2,1)S(1)} %get-tuple-element.39), channel_id=1, source_target_pairs={{0,3},{1,0},{2,1},{3,2},{4,7},{5,4},{6,5},{7,6},{8,11},{9,8},{10,9... | collective-permute-start | bytes 786440 | tf_op jit(solution)/shard_map/ppermute | solution.py:31
  91.2 1.5 collective-permute-start.14
  92.8 4.6 %collective-permute-done.16.r1 = bf16[256,512]{1,0:T(8,128)(2,1)S(1)} collective-permute-done((bf16[256,512]{1,0:T(8,128)(2,1)S(1)}, bf16[256,512]{1,0:T(8,128)(2,1)S(1)}, u32[]{:S(2)}, u32[]{:S(2)}) %collective-permute-start.16) | collective-permute-done | bytes 262176 | tf_op jit(solution)/shard_map/ppermute | solution.py:31
  97.4 2.5 %collective-permute-done.17.r3 = bf16[256,512]{1,0:T(8,128)(2,1)S(1)} collective-permute-done((bf16[256,512]{1,0:T(8,128)(2,1)S(1)}, bf16[256,512]{1,0:T(8,128)(2,1)S(1)}, u32[]{:S(2)}, u32[]{:S(2)}) %collective-permute-start.17) | collective-permute-done | bytes 262176 | tf_op jit(solution)/shard_map/ppermute | solution.py:31
  100.0 2.0 %project.3 = (bf16[256,1024]{1,0:T(8,128)(2,1)S(1)}, bf16[256,1024]{1,0:T(8,128)(2,1)S(1)}) custom-call(s32[128]{0:T(128)S(1)} %bitcast.24, bf16[256,512]{1,0:T(8,128)(2,1)S(1)} %normalise.3.a, bf16[256,512]{1,0:T(8,128)(2,1)S(1)} %collective-permute-done.14.near0, bf16[256,512]{1,0:T(8,128)(2,1)S(1)} %collective-permute-done.15.near1, ...), custom_call_target="tpu_custom_call" | custom-call | tf_op jit(solution)/shard_map/project/pallas_call | solution.py:328
  102.0 1.5 collective-permute-start.19
  104.0 3.6 %collective-permute-start.20 = (bf16[256,512]{1,0:T(8,128)(2,1)S(1)}, bf16[256,512]{1,0:T(8,128)(2,1)S(1)}, u32[]{:S(2)}, u32[]{:S(2)}) collective-permute-start(bf16[256,512]{1,0:T(8,128)(2,1)S(1)} %get-tuple-element.42), channel_id=1, source_target_pairs={{0,2},{1,3},{2,0},{3,1},{4,6},{5,7},{6,4},{7,5},{8,10},{9,11},{10,... | collective-permute-start | bytes 786440 | tf_op jit(solution)/shard_map/ppermute | solution.py:31
  107.6 2.0 %base.3 = f32[256,2048]{1,0:T(8,128)S(1)} custom-call(s32[128]{0:T(128)S(1)} %bitcast.25, bf16[256,512]{1,0:T(8,128)(2,1)S(1)} %normalise.3.a, bf16[256,512]{1,0:T(8,128)(2,1)S(1)} %collective-permute-done.14.near0, bf16[256,512]{1,0:T(8,128)(2,1)S(1)} %collective-permute-done.15.near1, bf16[512,2048]{1,0:T(8,128)(2,1)S(1)} %copy-done.1, ...), custom_call_target="tpu_custom_call" | custom-call | tf_op jit(solution)/shard_map/base/pallas_call | solution.py:359
  109.6 5.1 %collective-permute-done.20.refs_1_ = bf16[256,512]{1,0:T(8,128)(2,1)S(1)} collective-permute-done((bf16[256,512]{1,0:T(8,128)(2,1)S(1)}, bf16[256,512]{1,0:T(8,128)(2,1)S(1)}, u32[]{:S(2)}, u32[]{:S(2)}) %collective-permute-start.20) | collective-permute-done | bytes 262176 | tf_op jit(solution)/shard_map/ppermute | solution.py:31
  114.6 1.3 finish.2.after.refs_4_
  116.0 1.0 copy-done.6
  117.0 1.7 %combine.3 = (f32[256,512]{1,0:T(8,128)S(1)}, bf16[256,512]{1,0:T(8,128)(2,1)S(1)}, bf16[256,512]{1,0:T(8,128)(2,1)S(1)}, bf16[256,512]{1,0:T(8,128)(2,1)S(1)}) custom-call(s32[128]{0:T(128)S(1)} %bitcast.27, f32[256,2048]{1,0:T(8,128)S(1)} %base.3, bf16[256,1024]{1,0:T(8,128)(2,1)S(1)} %collective-permute-done.18.e0, ...), custom_call_target="tpu_custom_call" | custom-call | tf_op jit(solution)/shard_map/combine/pallas_call | solution.py:394
  118.7 7.9 %collective-permute-start.21 = (bf16[256,512]{1,0:T(8,128)(2,1)S(1)}, bf16[256,512]{1,0:T(8,128)(2,1)S(1)}, u32[]{:S(2)}, u32[]{:S(2)}) collective-permute-start(bf16[256,512]{1,0:T(8,128)(2,1)S(1)} %get-tuple-element.44), channel_id=1, source_target_pairs={{0,1},{1,2},{2,3},{3,0},{4,5},{5,6},{6,7},{7,4},{8,9},{9,10},{10,1... | collective-permute-start | bytes 786440 | tf_op jit(solution)/shard_map/ppermute | solution.py:31
  126.6 3.5 %collective-permute-start.22 = (bf16[256,512]{1,0:T(8,128)(2,1)S(1)}, bf16[256,512]{1,0:T(8,128)(2,1)S(1)}, u32[]{:S(2)}, u32[]{:S(2)}) collective-permute-start(bf16[256,512]{1,0:T(8,128)(2,1)S(1)} %get-tuple-element.45), channel_id=1, source_target_pairs={{0,2},{1,3},{2,0},{3,1},{4,6},{5,7},{6,4},{7,5},{8,10},{9,11},{10,... | collective-permute-start | bytes 786440 | tf_op jit(solution)/shard_map/ppermute | solution.py:31
  130.3 8.0 %collective-permute-done.21.refs_1_ = bf16[256,512]{1,0:T(8,128)(2,1)S(1)} collective-permute-done((bf16[256,512]{1,0:T(8,128)(2,1)S(1)}, bf16[256,512]{1,0:T(8,128)(2,1)S(1)}, u32[]{:S(2)}, u32[]{:S(2)}) %collective-permute-start.21) | collective-permute-done | bytes 262176 | tf_op jit(solution)/shard_map/ppermute | solution.py:31
  138.3 14.4 %collective-permute-done.22.refs_2_ = bf16[256,512]{1,0:T(8,128)(2,1)S(1)} collective-permute-done((bf16[256,512]{1,0:T(8,128)(2,1)S(1)}, bf16[256,512]{1,0:T(8,128)(2,1)S(1)}, u32[]{:S(2)}, u32[]{:S(2)}) %collective-permute-start.22) | collective-permute-done | bytes 262176 | tf_op jit(solution)/shard_map/ppermute | solution.py:31
  153.0 1.4 finish.3
  (86 shorter events, 6.9 us)
Async XLA Ops:
  2.9 7.0 %copy-start.21 = (s32[1,128]{1,0:T(1,128)}, s32[1,128]{1,0:T(1,128)S(1)}, u32[]{:S(2)}) copy-start(s32[1,128]{1,0:T(1,128)S(1)} %route.1) | copy-start | bytes 1540
  4.8 5.1 %copy-start.2 = (bf16[4,8,64,128]{3,2,1,0:T(8,128)(2,1)}, bf16[4,8,64,128]{3,2,1,0:T(8,128)(2,1)S(1)}, u32[]{:S(2)}) copy-start(bf16[4,8,64,128]{3,2,1,0:T(8,128)(2,1)S(1)} %leave.1.refs_1_.refs_0_) | copy-start | bytes 1572868
  4.9 10.5 %copy-start.5 = (bf16[8,8,64,128]{3,2,1,0:T(8,128)(2,1)S(1)}, bf16[8,8,64,128]{3,2,1,0:T(8,128)(2,1)}, u32[]{:S(2)}) copy-start(bf16[8,8,64,128]{3,2,1,0:T(8,128)(2,1)} %refs_0_.7) | copy-start | bytes 3145732
  4.9 10.5 %copy-start.9 = (bf16[8,64,512]{2,1,0:T(8,128)(2,1)S(1)}, bf16[8,64,512]{2,1,0:T(8,128)(2,1)}, u32[]{:S(2)}) copy-start(bf16[8,64,512]{2,1,0:T(8,128)(2,1)} %x_ref.3) | copy-start | bytes 1572868
  4.9 10.5 %copy-start.11 = (bf16[8,64,512]{2,1,0:T(8,128)(2,1)S(1)}, bf16[8,64,512]{2,1,0:T(8,128)(2,1)}, u32[]{:S(2)}) copy-start(bf16[8,64,512]{2,1,0:T(8,128)(2,1)} %g_ref.3) | copy-start | bytes 1572868
  4.9 10.5 %copy-start.13 = (bf16[8,64,4,128]{3,2,1,0:T(4,128)(2,1)S(1)}, bf16[8,64,4,128]{3,2,1,0:T(4,128)(2,1)}, u32[]{:S(2)}) copy-start(bf16[8,64,4,128]{3,2,1,0:T(4,128)(2,1)} %param.15) | copy-start | bytes 1572868
  4.9 10.5 %copy-start.15 = (bf16[8,64,4,128]{3,2,1,0:T(4,128)(2,1)S(1)}, bf16[8,64,4,128]{3,2,1,0:T(4,128)(2,1)}, u32[]{:S(2)}) copy-start(bf16[8,64,4,128]{3,2,1,0:T(4,128)(2,1)} %param.16) | copy-start | bytes 1572868
  4.9 10.5 %copy-start.20 = (f32[8,8,64]{2,1,0:T(8,128)S(1)}, f32[8,8,64]{2,1,0:T(8,128)}, u32[]{:S(2)}) copy-start(f32[8,8,64]{2,1,0:T(8,128)} %dt_ref.3) | copy-start | bytes 49156
  4.9 10.5 %copy-start.26 = (f32[8]{0:T(128)S(1)}, f32[8]{0:T(128)}, u32[]{:S(2)}) copy-start(f32[8]{0:T(128)} %bias.3) | copy-start | bytes 100
  4.9 10.5 %copy-start.27 = (f32[8]{0:T(128)S(1)}, f32[8]{0:T(128)}, u32[]{:S(2)}) copy-start(f32[8]{0:T(128)} %rate.3) | copy-start | bytes 100
  5.0 10.5 %copy-start.28 = (f32[8]{0:T(128)S(1)}, f32[8]{0:T(128)}, u32[]{:S(2)}) copy-start(f32[8]{0:T(128)} %skip.3) | copy-start | bytes 100
  5.0 39.9 %collective-permute-start.2 = (bf16[4,8,64,128]{3,2,1,0:T(8,128)(2,1)S(1)}, bf16[4,8,64,128]{3,2,1,0:T(8,128)(2,1)S(1)}, u32[]{:S(2)}, u32[]{:S(2)}) collective-permute-start(bf16[4,8,64,128]{3,2,1,0:T(8,128)(2,1)S(1)} %leave.1.refs_1_.refs_0_), channel_id=1, source_target_pairs={{0,192},{64,0},{128,64},{192,128},{1,193},{65,1},{129,65},{193,129... | collective-permute-start | bytes 1572872 | tf_op jit(solution)/shard_map/ppermute | solution.py:31
  5.5 39.4 %collective-permute-start.1 = (bf16[4,8,64,128]{3,2,1,0:T(8,128)(2,1)S(1)}, bf16[4,8,64,128]{3,2,1,0:T(8,128)(2,1)S(1)}, u32[]{:S(2)}, u32[]{:S(2)}) collective-permute-start(bf16[4,8,64,128]{3,2,1,0:T(8,128)(2,1)S(1)} %leave.1.refs_1_.refs_0_), channel_id=1, source_target_pairs={{0,128},{64,192},{128,0},{192,64},{1,129},{65,193},{129,1},{193,65... | collective-permute-start | bytes 1572872 | tf_op jit(solution)/shard_map/ppermute | solution.py:31
  8.1 36.8 %collective-permute-start = (bf16[4,8,64,128]{3,2,1,0:T(8,128)(2,1)S(1)}, bf16[4,8,64,128]{3,2,1,0:T(8,128)(2,1)S(1)}, u32[]{:S(2)}, u32[]{:S(2)}) collective-permute-start(bf16[4,8,64,128]{3,2,1,0:T(8,128)(2,1)S(1)} %leave.1.refs_1_.refs_0_), channel_id=1, source_target_pairs={{0,64},{64,128},{128,192},{192,0},{1,65},{65,129},{129,193},{193,1... | collective-permute-start | bytes 1572872 | tf_op jit(solution)/shard_map/ppermute | solution.py:31
  13.6 35.3 %collective-permute-start.5 = (bf16[512,1024]{1,0:T(8,128)(2,1)}, bf16[512,1024]{1,0:T(8,128)(2,1)}, u32[]{:S(2)}, u32[]{:S(2)}) collective-permute-start(bf16[512,1024]{1,0:T(8,128)(2,1)} %get-tuple-element.29), channel_id=1, source_target_pairs={{0,12},{4,8},{8,4},{12,0},{1,13},{5,9},{9,5},{13,1},{2,14},{6,10},... | collective-permute-start | bytes 3145736 | tf_op jit(solution)/shard_map/ppermute | solution.py:35
  14.2 34.7 %collective-permute-start.4 = (bf16[512,1024]{1,0:T(8,128)(2,1)}, bf16[512,1024]{1,0:T(8,128)(2,1)}, u32[]{:S(2)}, u32[]{:S(2)}) collective-permute-start(bf16[512,1024]{1,0:T(8,128)(2,1)} %get-tuple-element.25.refs_1_), channel_id=1, source_target_pairs={{0,4},{4,0},{8,12},{12,8},{1,5},{5,1},{9,13},{13,9},{2,6},{6,2},{1... | collective-permute-start | bytes 3145736 | tf_op jit(solution)/shard_map/ppermute | solution.py:35
  39.8 5.1 %copy-start.3 = (bf16[4,8,64,128]{3,2,1,0:T(8,128)(2,1)S(1)}, bf16[4,8,64,128]{3,2,1,0:T(8,128)(2,1)}, u32[]{:S(2)}) copy-start(bf16[4,8,64,128]{3,2,1,0:T(8,128)(2,1)} %copy-done.2) | copy-start | bytes 1572868
  39.8 5.1 %copy-start.23 = (s32[1,128]{1,0:T(1,128)S(1)}, s32[1,128]{1,0:T(1,128)}, u32[]{:S(2)}) copy-start(s32[1,128]{1,0:T(1,128)} %copy-done.21) | copy-start | bytes 1540
  44.9 1.6 %copy-start = (bf16[512,2048]{1,0:T(8,128)(2,1)S(1)}, bf16[512,2048]{1,0:T(8,128)(2,1)}, u32[]{:S(2)}) copy-start(bf16[512,2048]{1,0:T(8,128)(2,1)} %get-tuple-element.27.refs_4_.w) | copy-start | bytes 6291460
  48.8 1.8 %copy-start.19 = (f32[4,64,512]{2,1,0:T(8,128)S(1)}, f32[4,64,512]{2,1,0:T(8,128)}, u32[]{:S(2)}) copy-start(f32[4,64,512]{2,1,0:T(8,128)} %copy-done.18) | copy-start | bytes 1572868
  48.8 1.8 %copy-start.24 = (f32[4,1,64]{2,1,0:T(1,128)S(1)}, f32[4,1,64]{2,1,0:T(1,128)}, u32[]{:S(2)}) copy-start(f32[4,1,64]{2,1,0:T(1,128)} %psum.7.refs_1_.refs_0_) | copy-start | bytes 3076
  48.8 1.8 %copy-start.25 = (f32[512]{0:T(512)S(1)}, f32[512]{0:T(512)}, u32[]{:S(2)}) copy-start(f32[512]{0:T(512)} %param.21) | copy-start | bytes 6148
  48.8 2.7 %collective-permute-start.3 = (bf16[8,8,64,128]{3,2,1,0:T(8,128)(2,1)S(1)}, bf16[8,8,64,128]{3,2,1,0:T(8,128)(2,1)S(1)}, u32[]{:S(2)}, u32[]{:S(2)}) collective-permute-start(bf16[8,8,64,128]{3,2,1,0:T(8,128)(2,1)S(1)} %pick.2.after), channel_id=1, source_target_pairs={{0,16},{16,0},{1,17},{17,1},{2,18},{18,2},{3,19},{19,3},{4,20},{20... | collective-permute-start | bytes 3145736 | tf_op jit(solution)/shard_map/ppermute | solution.py:31
  53.0 10.7 %copy-start.7 = (bf16[512,1024]{1,0:T(8,128)(2,1)S(1)}, bf16[512,1024]{1,0:T(8,128)(2,1)}, u32[]{:S(2)}) copy-start(bf16[512,1024]{1,0:T(8,128)(2,1)} %get-tuple-element.30.w0) | copy-start | bytes 3145732
  53.0 10.7 %copy-start.8 = (bf16[512,1024]{1,0:T(8,128)(2,1)S(1)}, bf16[512,1024]{1,0:T(8,128)(2,1)}, u32[]{:S(2)}) copy-start(bf16[512,1024]{1,0:T(8,128)(2,1)} %get-tuple-element.31.w1) | copy-start | bytes 3145732
  53.0 10.7 %collective-permute-start.9 = (bf16[2,512,1024]{2,1,0:T(8,128)(2,1)S(1)}, bf16[2,512,1024]{2,1,0:T(8,128)(2,1)S(1)}, u32[]{:S(2)}, u32[]{:S(2)}) collective-permute-start(bf16[2,512,1024]{2,1,0:T(8,128)(2,1)S(1)} %hold.1.got), channel_id=1, source_target_pairs={{0,16},{16,0},{1,17},{17,1},{2,18},{18,2},{3,19},{19,3},{4,20},{20... | collective-permute-start | bytes 6291464 | tf_op jit(solution)/shard_map/ppermute | solution.py:31
  53.2 9.0 %collective-permute-start.8 = (bf16[256,512]{1,0:T(8,128)(2,1)S(1)}, bf16[256,512]{1,0:T(8,128)(2,1)S(1)}, u32[]{:S(2)}, u32[]{:S(2)}) collective-permute-start(bf16[256,512]{1,0:T(8,128)(2,1)S(1)} %normalise.2.refs_5_.a), channel_id=1, source_target_pairs={{0,12},{4,8},{8,4},{12,0},{1,13},{5,9},{9,5},{13,1},{2,14},{6,10},... | collective-permute-start | bytes 786440 | tf_op jit(solution)/shard_map/ppermute | solution.py:35
  55.4 8.3 %collective-permute-start.7 = (bf16[256,512]{1,0:T(8,128)(2,1)S(1)}, bf16[256,512]{1,0:T(8,128)(2,1)S(1)}, u32[]{:S(2)}, u32[]{:S(2)}) collective-permute-start(bf16[256,512]{1,0:T(8,128)(2,1)S(1)} %normalise.2.refs_5_.a), channel_id=1, source_target_pairs={{0,4},{4,0},{8,12},{12,8},{1,5},{5,1},{9,13},{13,9},{2,6},{6,2},{1... | collective-permute-start | bytes 786440 | tf_op jit(solution)/shard_map/ppermute | solution.py:35
  56.2 13.6 %collective-permute-start.6 = (bf16[4,8,64,128]{3,2,1,0:T(8,128)(2,1)S(1)}, bf16[4,8,64,128]{3,2,1,0:T(8,128)(2,1)S(1)}, u32[]{:S(2)}, u32[]{:S(2)}) collective-permute-start(bf16[4,8,64,128]{3,2,1,0:T(8,128)(2,1)S(1)} %pick.3.after), channel_id=1, source_target_pairs={{0,32},{32,0},{1,33},{33,1},{2,34},{34,2},{3,35},{35,3},{4,36},{36... | collective-permute-start | bytes 1572872 | tf_op jit(solution)/shard_map/ppermute | solution.py:31
  63.7 6.1 %copy-start.10 = (bf16[8,64,512]{2,1,0:T(8,128)(2,1)S(1)}, bf16[8,64,512]{2,1,0:T(8,128)(2,1)}, u32[]{:S(2)}) copy-start(bf16[8,64,512]{2,1,0:T(8,128)(2,1)} %x_ref.3) | copy-start | bytes 1572868
  63.7 6.1 %copy-start.12 = (bf16[8,64,512]{2,1,0:T(8,128)(2,1)S(1)}, bf16[8,64,512]{2,1,0:T(8,128)(2,1)}, u32[]{:S(2)}) copy-start(bf16[8,64,512]{2,1,0:T(8,128)(2,1)} %g_ref.3) | copy-start | bytes 1572868
  63.7 6.1 %copy-start.14 = (bf16[8,64,4,128]{3,2,1,0:T(4,128)(2,1)S(1)}, bf16[8,64,4,128]{3,2,1,0:T(4,128)(2,1)}, u32[]{:S(2)}) copy-start(bf16[8,64,4,128]{3,2,1,0:T(4,128)(2,1)} %param.15) | copy-start | bytes 1572868
  63.7 6.1 %copy-start.16 = (bf16[8,64,4,128]{3,2,1,0:T(4,128)(2,1)S(1)}, bf16[8,64,4,128]{3,2,1,0:T(4,128)(2,1)}, u32[]{:S(2)}) copy-start(bf16[8,64,4,128]{3,2,1,0:T(4,128)(2,1)} %param.16) | copy-start | bytes 1572868
  65.8 18.8 %collective-permute-start.13 = (bf16[256,1024]{1,0:T(8,128)(2,1)S(1)}, bf16[256,1024]{1,0:T(8,128)(2,1)S(1)}, u32[]{:S(2)}, u32[]{:S(2)}) collective-permute-start(bf16[256,1024]{1,0:T(8,128)(2,1)S(1)} %get-tuple-element.36), channel_id=1, source_target_pairs={{0,4},{4,0},{8,12},{12,8},{1,5},{5,1},{9,13},{13,9},{2,6},{6,2},{1... | collective-permute-start | bytes 1572872 | tf_op jit(solution)/shard_map/ppermute | solution.py:35
  66.7 17.9 %collective-permute-start.12 = (bf16[256,1024]{1,0:T(8,128)(2,1)S(1)}, bf16[256,1024]{1,0:T(8,128)(2,1)S(1)}, u32[]{:S(2)}, u32[]{:S(2)}) collective-permute-start(bf16[256,1024]{1,0:T(8,128)(2,1)S(1)} %get-tuple-element.32.refs_7_.after), channel_id=1, source_target_pairs={{0,12},{4,8},{8,4},{12,0},{1,13},{5,9},{9,5},{13,1},{2,14},{6,10},... | collective-permute-start | bytes 1572872 | tf_op jit(solution)/shard_map/ppermute | solution.py:35
  69.9 12.7 %copy-start.1 = (bf16[512,2048]{1,0:T(8,128)(2,1)S(1)}, bf16[512,2048]{1,0:T(8,128)(2,1)}, u32[]{:S(2)}) copy-start(bf16[512,2048]{1,0:T(8,128)(2,1)} %get-tuple-element.27.refs_4_.w) | copy-start | bytes 6291460
  76.4 4.8 %collective-permute-start.10 = (f32[4,1,64]{2,1,0:T(1,128)S(1)}, f32[4,1,64]{2,1,0:T(1,128)S(1)}, u32[]{:S(2)}, u32[]{:S(2)}) collective-permute-start(f32[4,1,64]{2,1,0:T(1,128)S(1)} %get-tuple-element.35.after), channel_id=1, source_target_pairs={{0,1},{1,0},{2,3},{3,2},{4,5},{5,4},{6,7},{7,6},{8,9},{9,8},{10,11... | collective-permute-start | bytes 3080 | tf_op jit(solution)/shard_map/ppermute | solution.py:128
  81.1 9.3 %collective-permute-start.11 = (f32[4,1,64]{2,1,0:T(1,128)S(1)}, f32[4,1,64]{2,1,0:T(1,128)S(1)}, u32[]{:S(2)}, u32[]{:S(2)}) collective-permute-start(f32[4,1,64]{2,1,0:T(1,128)S(1)} %add.5.refs_0_), channel_id=1, source_target_pairs={{0,3},{1,2},{2,1},{3,0},{4,7},{5,6},{6,5},{7,4},{8,11},{9,10},{10,... | collective-permute-start | bytes 3080 | tf_op jit(solution)/shard_map/ppermute | solution.py:130
  86.2 11.2 %collective-permute-start.16 = (bf16[256,512]{1,0:T(8,128)(2,1)S(1)}, bf16[256,512]{1,0:T(8,128)(2,1)S(1)}, u32[]{:S(2)}, u32[]{:S(2)}) collective-permute-start(bf16[256,512]{1,0:T(8,128)(2,1)S(1)} %get-tuple-element.38), channel_id=1, source_target_pairs={{0,1},{1,2},{2,3},{3,0},{4,5},{5,6},{6,7},{7,4},{8,9},{9,10},{10,1... | collective-permute-start | bytes 786440 | tf_op jit(solution)/shard_map/ppermute | solution.py:31
  87.8 12.0 %collective-permute-start.17 = (bf16[256,512]{1,0:T(8,128)(2,1)S(1)}, bf16[256,512]{1,0:T(8,128)(2,1)S(1)}, u32[]{:S(2)}, u32[]{:S(2)}) collective-permute-start(bf16[256,512]{1,0:T(8,128)(2,1)S(1)} %get-tuple-element.39), channel_id=1, source_target_pairs={{0,3},{1,0},{2,1},{3,2},{4,7},{5,4},{6,5},{7,6},{8,11},{9,8},{10,9... | collective-permute-start | bytes 786440 | tf_op jit(solution)/shard_map/ppermute | solution.py:31
  90.6 9.4 %collective-permute-start.15 = (bf16[256,512]{1,0:T(8,128)(2,1)S(1)}, bf16[256,512]{1,0:T(8,128)(2,1)S(1)}, u32[]{:S(2)}, u32[]{:S(2)}) collective-permute-start(bf16[256,512]{1,0:T(8,128)(2,1)S(1)} %normalise.3.a), channel_id=1, source_target_pairs={{0,12},{4,8},{8,4},{12,0},{1,13},{5,9},{9,5},{13,1},{2,14},{6,10},... | collective-permute-start | bytes 786440 | tf_op jit(solution)/shard_map/ppermute | solution.py:35
  91.2 8.7 %collective-permute-start.14 = (bf16[256,512]{1,0:T(8,128)(2,1)S(1)}, bf16[256,512]{1,0:T(8,128)(2,1)S(1)}, u32[]{:S(2)}, u32[]{:S(2)}) collective-permute-start(bf16[256,512]{1,0:T(8,128)(2,1)S(1)} %normalise.3.a), channel_id=1, source_target_pairs={{0,4},{4,0},{8,12},{12,8},{1,5},{5,1},{9,13},{13,9},{2,6},{6,2},{1... | collective-permute-start | bytes 786440 | tf_op jit(solution)/shard_map/ppermute | solution.py:35
  102.0 14.0 %collective-permute-start.19 = (bf16[256,1024]{1,0:T(8,128)(2,1)S(1)}, bf16[256,1024]{1,0:T(8,128)(2,1)S(1)}, u32[]{:S(2)}, u32[]{:S(2)}) collective-permute-start(bf16[256,1024]{1,0:T(8,128)(2,1)S(1)} %get-tuple-element.41), channel_id=1, source_target_pairs={{0,4},{4,0},{8,12},{12,8},{1,5},{5,1},{9,13},{13,9},{2,6},{6,2},{1... | collective-permute-start | bytes 1572872 | tf_op jit(solution)/shard_map/ppermute | solution.py:35
  103.5 12.5 %collective-permute-start.18 = (bf16[256,1024]{1,0:T(8,128)(2,1)S(1)}, bf16[256,1024]{1,0:T(8,128)(2,1)S(1)}, u32[]{:S(2)}, u32[]{:S(2)}) collective-permute-start(bf16[256,1024]{1,0:T(8,128)(2,1)S(1)} %get-tuple-element.40.after), channel_id=1, source_target_pairs={{0,12},{4,8},{8,4},{12,0},{1,13},{5,9},{9,5},{13,1},{2,14},{6,10},... | collective-permute-start | bytes 1572872 | tf_op jit(solution)/shard_map/ppermute | solution.py:35
  104.0 10.6 %collective-permute-start.20 = (bf16[256,512]{1,0:T(8,128)(2,1)S(1)}, bf16[256,512]{1,0:T(8,128)(2,1)S(1)}, u32[]{:S(2)}, u32[]{:S(2)}) collective-permute-start(bf16[256,512]{1,0:T(8,128)(2,1)S(1)} %get-tuple-element.42), channel_id=1, source_target_pairs={{0,2},{1,3},{2,0},{3,1},{4,6},{5,7},{6,4},{7,5},{8,10},{9,11},{10,... | collective-permute-start | bytes 786440 | tf_op jit(solution)/shard_map/ppermute | solution.py:31
  118.7 19.6 %collective-permute-start.21 = (bf16[256,512]{1,0:T(8,128)(2,1)S(1)}, bf16[256,512]{1,0:T(8,128)(2,1)S(1)}, u32[]{:S(2)}, u32[]{:S(2)}) collective-permute-start(bf16[256,512]{1,0:T(8,128)(2,1)S(1)} %get-tuple-element.44), channel_id=1, source_target_pairs={{0,1},{1,2},{2,3},{3,0},{4,5},{5,6},{6,7},{7,4},{8,9},{9,10},{10,1... | collective-permute-start | bytes 786440 | tf_op jit(solution)/shard_map/ppermute | solution.py:31
  126.6 26.0 %collective-permute-start.22 = (bf16[256,512]{1,0:T(8,128)(2,1)S(1)}, bf16[256,512]{1,0:T(8,128)(2,1)S(1)}, u32[]{:S(2)}, u32[]{:S(2)}) collective-permute-start(bf16[256,512]{1,0:T(8,128)(2,1)S(1)} %get-tuple-element.45), channel_id=1, source_target_pairs={{0,2},{1,3},{2,0},{3,1},{4,6},{5,7},{6,4},{7,5},{8,10},{9,11},{10,... | collective-permute-start | bytes 786440 | tf_op jit(solution)/shard_map/ppermute | solution.py:31
  130.1 22.8 %collective-permute-start.23 = (bf16[256,512]{1,0:T(8,128)(2,1)S(1)}, bf16[256,512]{1,0:T(8,128)(2,1)S(1)}, u32[]{:S(2)}, u32[]{:S(2)}) collective-permute-start(bf16[256,512]{1,0:T(8,128)(2,1)S(1)} %get-tuple-element.46), channel_id=1, source_target_pairs={{0,3},{1,0},{2,1},{3,2},{4,7},{5,4},{6,5},{7,6},{8,11},{9,8},{10,9... | collective-permute-start | bytes 786440 | tf_op jit(solution)/shard_map/ppermute | solution.py:31
  (7 other events, 6.3 us)

commit v3 on v2

--- a/solution.py
+++ b/solution.py
@@ -310,19 +310,26 @@
     )(gated, *sums, gain, after)
 
 
-def project_kernel(sc, a, near0, near1, w0, w1, got, other, after, out0, out1):
-    for side, near, w, out in ((0, near0, w0, out0), (1, near1, w1, out1)):
+def project_kernel(sc, a, near0, near1, w0, w1, got, other, after, *outs):
+    count = len(outs) // 2
+    rows = a.shape[0] // count
+
+    def store(side, value):
+        for k in range(count):
+            outs[side * count + k][...] = value[k * rows : (k + 1) * rows].astype(BF16)
+
+    for side, near, w in ((0, near0, w0), (1, near1, w1)):
 
         @pl.when(sc[C_AT] == 1)
         def _():
-            out[...] = (product(a[...], w[...]) + product(near[...], got[side])).astype(BF16)
+            store(side, product(a[...], w[...]) + product(near[...], got[side]))
 
         @pl.when(sc[C_AT] != 1)
         def _():
-            out[...] = (product(a[...], w[...]) + product(near[...], other[side])).astype(BF16)
-
-
-def project(table, a, nears, parts, weights, after):
+            store(side, product(a[...], w[...]) + product(near[...], other[side]))
+
+
+def project(table, a, nears, parts, weights, after, count=1):
     rows = HALF * NEW
     whole = pl.BlockSpec(memory_space=pltpu.VMEM)
     return pl.pallas_call(
@@ -331,9 +338,9 @@
             num_scalar_prefetch=1,
             grid=(1,),
             in_specs=[whole] * 7 + [ANYWHERE],
-            out_specs=[whole] * 2,
+            out_specs=[whole] * (2 * count),
         ),
-        out_shape=[jax.ShapeDtypeStruct((rows, 1024), BF16)] * 2,
+        out_shape=[jax.ShapeDtypeStruct((rows // count, 1024), BF16)] * (2 * count),
         compiler_params=LIMIT,
         cost_estimate=FREE,
         name="project",
@@ -371,7 +378,8 @@
     )(table, a, *nears, own, *weights, after)
 
 
-def combine_kernel(sc, base, e0, e1, after, z0, z1, z2, z3):
+def combine_kernel(sc, base, e0, e1, *refs):
+    z0, z1, z2, z3 = refs[-4:]
     j = pl.program_id(0)
     arrived = jnp.where((sc[ZH_AT] + j) % 4 < 2, e0[...].astype(F32), e1[...].astype(F32))
     value = base[...] + arrived
@@ -387,8 +395,8 @@
             ref[...] = value.astype(BF16)
 
 
-def combine(table, base, e0, e1, after):
-    rows = HALF * NEW
+def combine(table, base, e0, e1, after, part=0):
+    rows = e0.shape[0]
     whole = pl.BlockSpec((rows, 512), lambda j, sc: (0, 0))
     at = lambda j, sc: (sc[ZH_AT] + j) % 4
     return pl.pallas_call(
@@ -397,10 +405,10 @@
             num_scalar_prefetch=1,
             grid=(4,),
             in_specs=[
-                pl.BlockSpec((rows, 512), lambda j, sc: (0, at(j, sc))),
+                pl.BlockSpec((rows, 512), lambda j, sc: (part, at(j, sc))),
                 pl.BlockSpec((rows, 512), lambda j, sc: (0, jnp.minimum(at(j, sc), 1))),
                 pl.BlockSpec((rows, 512), lambda j, sc: (0, jnp.maximum(at(j, sc) - 2, 0))),
-                ANYWHERE,
+                *[ANYWHERE] * len(after),
             ],
             out_specs=[whole] * 4,
         ),
@@ -411,7 +419,7 @@
         compiler_params=LIMIT,
         cost_estimate=FREE,
         name="combine",
-    )(table, base, e0, e1, after)
+    )(table, base, e0, e1, *after)
 
 
 def slice_kernel(first, count, sc, *refs):
@@ -451,6 +459,22 @@
     )(table, w, after)
 
 
+def wait_kernel(after, out):
+    out[...] = jnp.zeros_like(out)
+
+
+def wait(after):
+    return pl.pallas_call(
+        wait_kernel,
+        in_specs=[ANYWHERE],
+        out_specs=pl.BlockSpec(memory_space=pltpu.VMEM),
+        out_shape=jax.ShapeDtypeStruct((8, 128), F32),
+        compiler_params=LIMIT,
+        cost_estimate=pl.CostEstimate(flops=0, bytes_accessed=16 << 20, transcendentals=0),
+        name="wait",
+    )(after)
+
+
 def hold_kernel(value, after, out):
     pass
 
@@ -491,69 +515,71 @@
     )(first, second, after)
 
 
-def gather_kernel(z0, r1, r3, out):
-    out[...] = z0[...] + r1[...].astype(F32) + r3[...].astype(F32)
-
-
-def gather_sum(z0, r1, r3):
+def gather_kernel(*refs):
+    out = refs[-1]
+    value = refs[0][...]
+    for part in refs[1:-1]:
+        value = value + part[...].astype(F32)
+    out[...] = value.astype(out.dtype)
+
+
+def gather_sum(parts, dtype):
     whole = pl.BlockSpec(memory_space=pltpu.VMEM)
     return pl.pallas_call(
         gather_kernel,
-        in_specs=[whole] * 3,
+        in_specs=[whole] * len(parts),
         out_specs=whole,
-        out_shape=jax.ShapeDtypeStruct(z0.shape, F32),
+        out_shape=jax.ShapeDtypeStruct(parts[0].shape, dtype),
         compiler_params=LIMIT,
         cost_estimate=FREE,
         name="gather_sum",
-    )(z0, r1, r3)
-
-
-def finish_kernel(count, first, sc, *refs):
-    parts = refs[:count]
-    out, held, sem = refs[-3:]
-    value = parts[0][...]
-    for part in parts[1:]:
-        value = value + part[...].astype(F32)
-    held[...] = value.astype(BF16)
-    copies = [
-        pltpu.make_async_copy(
-            held.at[pl.ds(r * NEW, NEW)], out.at[sc[ORDER + first + r]], sem.at[r]
-        )
-        for r in range(HALF)
-    ]
-    for copy in copies:
-        copy.start()
+    )(*parts)
+
+
+def finish_kernel(sc, half, *refs):
+    parts, (out, held, sem) = refs[:-3], refs[-3:]
+
+    def rows_out(source, p):
+        rows = pl.ds(p % HALF * NEW, NEW)
+        return pltpu.make_async_copy(source.at[rows], out.at[sc[ORDER + p]], sem.at[p])
+
+    copies = [rows_out(half, p) for p in range(HALF)]
+    copies += [rows_out(held, p) for p in range(HALF, ROWS)]
+    for p in range(HALF):
+        copies[p].start()
+    at = 0
+    for count in 2, 4:
+        group, parts = parts[:count], parts[count:]
+        value = group[0][...]
+        for part in group[1:]:
+            value = value + part[...].astype(F32)
+        held[at : at + value.shape[0]] = value.astype(BF16)
+        at += value.shape[0]
+    for p in range(HALF, ROWS):
+        copies[p].start()
     for copy in copies:
         copy.wait()
 
 
-def finish(table, parts, first, alias):
+def finish(table, half, parts):
     whole = pl.BlockSpec(memory_space=pltpu.VMEM)
-    in_specs = [whole] * len(parts)
-    operands = [table, *parts]
-    aliases = {}
-    if alias is not None:
-        in_specs.append(ANYWHERE)
-        aliases = {len(operands): 0}
-        operands.append(alias)
-    return pl.pallas_call(
-        functools.partial(finish_kernel, len(parts), first),
+    return pl.pallas_call(
+        finish_kernel,
         grid_spec=pltpu.PrefetchScalarGridSpec(
             num_scalar_prefetch=1,
             grid=(1,),
-            in_specs=in_specs,
+            in_specs=[whole] * (1 + len(parts)),
             out_specs=ANYWHERE,
             scratch_shapes=[
                 pltpu.VMEM((HALF * NEW, 512), BF16),
-                pltpu.SemaphoreType.DMA((HALF,)),
+                pltpu.SemaphoreType.DMA((ROWS,)),
             ],
         ),
         out_shape=jax.ShapeDtypeStruct((ROWS, NEW, 512), BF16),
-        input_output_aliases=aliases,
         compiler_params=LIMIT,
         cost_estimate=FREE,
         name="finish",
-    )(*operands)
+    )(table, half, *parts)
 
 
 def copy_kernel(sc, source, out):
@@ -630,6 +656,7 @@
 
     shares = slices(table, out_weight, buf, 0, 2)
     got = [flip(shares[0], 1), flip(shares[1], 3)]
+    part0, part1, own = slices(table, out_weight, shares[0], 2, 5)
 
     b = write_basis.reshape(ROWS, 4 * NEW, 128)
     c = read_basis.reshape(ROWS, 4 * NEW, 128)
@@ -649,17 +676,16 @@
         a = normalise(gated, sums, gain, after)
         return a, [flip(a, 1), flip(a, 3)]
 
-    def reduce_rest(base, moved, after):
-        zs = combine(table, base, *moved, after)
+    def reduce_rest(base, moved, after, part=0):
+        zs = combine(table, base, *moved, after, part)
         return [zs[0]] + [shift(zs[k], "zh", k) for k in (1, 2, 3)]
 
-    gated1, sq1, states1 = ssm(start=0, sources=[ssm_states], alias=None, after=[shares[0]])
+    gated1, sq1, states1 = ssm(start=0, sources=[ssm_states], alias=None, after=[own])
     sums1 = lax.psum(sq1, "zh")
 
-    part0, part1, own = slices(table, out_weight, sums1, 2, 5)
-    chosen = pick(table, along, BESIDE, BESIDE_ROW, 8, own)
+    chosen = pick(table, along, BESIDE, BESIDE_ROW, 8, sums1)
     beside = shift(chosen, "c", 1)
-    near_weights = join(*got, chosen)
+    near_weights = join(*got, wait(chosen))
     a1, nears1 = spread_rows(gated1, [sums1], near_weights)
     picked = pick(table, [*along, beside], ACROSS, ACROSS_ROW, HALF, a1)
     across = shift(picked, "zl", 1)
@@ -670,18 +696,20 @@
     base1 = base_project(table, a1, nears1, own, weights, sent1[0])
 
     gated2, sq2, new_states = ssm(
-        start=HALF, sources=[ssm_states, *along, beside, across], alias=states1, after=[sent1[0]]
+        start=HALF, sources=[ssm_states, *along, beside, across], alias=states1, after=[base1]
     )
     sums2 = fly(sq2)
-    z0, r1, r2, r3 = reduce_rest(base1, moved1, sq2)
+    z0, r1, r2, r3 = reduce_rest(base1, moved1, [sq2])
     a2, nears2 = spread_rows(gated2, sums2, z0)
-    gathered = gather_sum(z0, r1, r3)
-    sent2 = project(table, a2, nears2, [part0, part1], weights, gathered)
-    moved2 = [flip(sent2[0], 3), flip(sent2[1], 1)]
+    gathered = gather_sum([z0, r1, r3], F32)
+    sent2 = project(table, a2, nears2, [part0, part1], weights, gathered, 2)
+    moved2 = [[flip(sent2[k], 3), flip(sent2[2 + k], 1)] for k in range(2)]
     base2 = base_project(table, a2, nears2, own, weights, sent2[0])
-    half_out = finish(table, [gathered, r2], 0, None)
-    done2 = reduce_rest(base2, moved2, half_out)
-    return finish(table, done2, HALF, half_out), new_states
+    z0, r1, late, r3 = reduce_rest(base2, moved2[0], [base2], 0)
+    gathered2 = gather_sum([z0, r1, r3], F32)
+    half_out = gather_sum([gathered, r2], BF16)
+    done2 = reduce_rest(base2, moved2[1], [half_out, gathered2], 1)
+    return finish(table, half_out, [gathered2, late, *done2]), new_states
 
 
 def solution(mesh):

time: 156 us -> 145 us (0.929)
  waiting for transfers between devices: 48.7 us -> 31.3 us
  starting transfers between devices: 38.4 us -> 47.1 us
  local copies, waits for them, and re-layouts: 8.07 us -> 5.12 us
    ppermute x12 -> x15, waiting for transfers between devices: 38 us -> 20.7 us  [shift(): lax.ppermute(value, axis, [(i, (i + step) % size) for i in range(size)])]
    ppermute x10 -> x12, starting transfers between devices: 10.8 us -> 15.7 us  [flip(): return lax.ppermute(value, 'x', [(i, i ^ mask) for i in range(4)])]
    ppermute x12 -> x15, starting transfers between devices: 25.7 us -> 29.7 us  [shift(): lax.ppermute(value, axis, [(i, (i + step) % size) for i in range(size)])]
    unnamed x62 -> x48, local copies, waits for them, and re-layouts: 7.98 us -> 5.03 us
    pallas_call x2 -> x3, Pallas kernels: 3.32 us -> 4.11 us  [combine(): pl.pallas_call(combine_kernel, grid_spec=pltpu.PrefetchScalarGridSpec(num...]
    ppermute x10 -> x12, waiting for transfers between devices: 6.47 us -> 6.32 us  [flip(): return lax.ppermute(value, 'x', [(i, i ^ mask) for i in range(4)])]
  transfers between devices with their start and end apart: 24 -> 29, of which waited for: 11 -> 11; matrix products, arithmetic and copies ran while one was open for 0% -> 0% of each run, Pallas kernels for 22% -> 25%
where the time goes in v3:
time: 145 us; the launch traced here: 144 us
  starting transfers between devices  47.1 us (32%)
  Pallas kernels  43.9 us (30%)
  waiting for transfers between devices  31.3 us (22%)
  blocking collectives  14.9 us (10%)
  local copies, waits for them, and re-layouts  5.12 us (4%)
    ppermute x15, starting transfers between devices, shift(): lax.ppermute(value, axis, [(i, (i + step) % size) for i in range(size)])  29.7 us
    ppermute x15, waiting for transfers between devices, shift(): lax.ppermute(value, axis, [(i, (i + step) % size) for i in range(size)])  20.7 us
    ppermute x12, starting transfers between devices, flip(): return lax.ppermute(value, 'x', [(i, i ^ mask) for i in range(4)])  15.7 us
    psum x1, blocking collectives, local(): sums1 = lax.psum(sq1, 'zh')  14.9 us
    pallas_call x2, Pallas kernels, run_ssm(): pl.pallas_call(functools.partial(ssm_kernel, start, len(sources), unused)...  12.6 us
    pallas_call x2, Pallas kernels, slices(): pl.pallas_call(functools.partial(slice_kernel, first, len(widths)), grid_...  8.51 us
    ppermute x12, waiting for transfers between devices, flip(): return lax.ppermute(value, 'x', [(i, i ^ mask) for i in range(4)])  6.32 us
    unnamed x48, local copies, waits for them, and re-layouts  5.03 us
  transfers between devices with their start and end apart: 29, of which 11 were waited for; matrix products, arithmetic and copies ran while one was open for 0% of the time, Pallas kernels for 25%

profile of v3, /device:TPU:12, one launch (start us, length us, event | category | flops | bytes accessed | tf_op | source)
XLA Modules:
  0.0 143.6 jit_solution(9131386196398025929)
XLA Ops:
  2.9 1.2 copy-done.2
  4.2 1.9 %leave.1.refs_1_.refs_0_ = bf16[4,8,64,128]{3,2,1,0:T(8,128)(2,1)} custom-call(s32[128]{0:T(128)S(1)} %bitcast.14, bf16[8,8,64,128]{3,2,1,0:T(8,128)(2,1)S(1)} %copy-done.2), custom_call_target="tpu_custom_call" | custom-call | tf_op jit(solution)/shard_map/leave/pallas_call | solution.py:590
  6.6 2.6 %collective-permute-start.3 = (bf16[4,8,64,128]{3,2,1,0:T(8,128)(2,1)}, bf16[4,8,64,128]{3,2,1,0:T(8,128)(2,1)S(1)}, u32[]{:S(2)}, u32[]{:S(2)}) collective-permute-start(bf16[4,8,64,128]{3,2,1,0:T(8,128)(2,1)} %leave.1.refs_1_.refs_0_), channel_id=1, source_target_pairs={{0,128},{64,192},{128,0},{192,64},{1,129},{65,193},{129,1},{193,65... | collective-permute-start | bytes 1572872 | tf_op jit(solution)/shard_map/ppermute | solution.py:31
  9.2 1.9 %collective-permute-start.2 = (bf16[4,8,64,128]{3,2,1,0:T(8,128)(2,1)}, bf16[4,8,64,128]{3,2,1,0:T(8,128)(2,1)S(1)}, u32[]{:S(2)}, u32[]{:S(2)}) collective-permute-start(bf16[4,8,64,128]{3,2,1,0:T(8,128)(2,1)} %leave.1.refs_1_.refs_0_), channel_id=1, source_target_pairs={{0,64},{64,128},{128,192},{192,0},{1,65},{65,129},{129,193},{193,1... | collective-permute-start | bytes 1572872 | tf_op jit(solution)/shard_map/ppermute | solution.py:31
  11.1 3.6 %slices.2 = (bf16[512,1024]{1,0:T(8,128)(2,1)}, bf16[512,1024]{1,0:T(8,128)(2,1)}) custom-call(s32[128]{0:T(128)} %bitcast.15, bf16[512,8192]{1,0:T(8,128)(2,1)} %refs_0_.5, bf16[4,8,64,128]{3,2,1,0:T(8,128)(2,1)} %leave.1.refs_1_.refs_0_), custom_call_target="tpu_custom_call" | custom-call | tf_op jit(solution)/shard_map/slices/pallas_call | solution.py:446
  15.4 1.2 collective-permute-start
  16.6 4.9 %slices.3 = (bf16[512,1024]{1,0:T(8,128)(2,1)}, bf16[512,1024]{1,0:T(8,128)(2,1)}, bf16[512,2048]{1,0:T(8,128)(2,1)}) custom-call(s32[128]{0:T(128)} %bitcast.16, bf16[512,8192]{1,0:T(8,128)(2,1)} %refs_0_.5, bf16[512,1024]{1,0:T(8,128)(2,1)} %get-tuple-element.31.refs_1_), custom_call_target="tpu_custom_call" | custom-call | tf_op jit(solution)/shard_map/slices/pallas_call | solution.py:446
  21.6 1.6 %copy-done = bf16[512,2048]{1,0:T(8,128)(2,1)S(1)} copy-done((bf16[512,2048]{1,0:T(8,128)(2,1)S(1)}, bf16[512,2048]{1,0:T(8,128)(2,1)}, u32[]{:S(2)}) %copy-start) | copy-done | bytes 2097176
  23.2 6.2 %ssm.2 = (f32[4,64,512]{2,1,0:T(8,128)S(1)}, f32[4,1,64]{2,1,0:T(1,128)S(1)}, bf16[8,8,64,128]{3,2,1,0:T(8,128)(2,1)}) custom-call(s32[128]{0:T(128)S(1)} %bitcast.17, bf16[8,64,512]{2,1,0:T(8,128)(2,1)S(1)} %copy-done.6, bf16[8,64,512]{2,1,0:T(8,128)(2,1)S(1)} %copy-done.7, bf16[8,256,128]{2,1,0:T(8,128)(2,1)S(1)} %bitcast.10, ...), custom_call_target="tpu_custom_call" | custom-call | tf_op jit(solution)/shard_map/ssm/pallas_call | solution.py:261
  30.2 14.9 %psum.7.refs_4_.refs_0_ = f32[4,1,64]{2,1,0:T(1,128)S(1)} all-reduce(f32[4,1,64]{2,1,0:T(1,128)S(1)} %get-tuple-element.34), channel_id=1, replica_groups=mesh['y'=4,'zl'=2,'c'=2,'x'=4,'zh'=4] {'zh'}, use_global_device_ids=true, to_apply=%region_0.0 | all-reduce | flops 256 | bytes 2048 | tf_op jit(solution)/shard_map/psum | solution.py:684
  45.1 2.1 %pick.2.after = bf16[8,8,64,128]{3,2,1,0:T(8,128)(2,1)S(1)} custom-call(s32[128]{0:T(128)S(1)} %bitcast.18, bf16[4,8,64,128]{3,2,1,0:T(8,128)(2,1)} %leave.1.refs_1_.refs_0_, bf16[4,8,64,128]{3,2,1,0:T(8,128)(2,1)S(1)} %collective-permute-done.2.refs_1_.refs_2_, bf16[4,8,64,128]{3,2,1,0:T(8,128)(2,1)S(1)} %collective-permute-done.3.refs_2_.refs_3_, ...), custom_call_target="tpu_custom_call" | custom-call | tf_op jit(solution)/shard_map/pick/pallas_call | solution.py:621
  47.4 1.6 %join.1.refs_2_.value = bf16[2,512,1024]{2,1,0:T(8,128)(2,1)S(1)} custom-call(bf16[512,1024]{1,0:T(8,128)(2,1)} %collective-permute-done.first, bf16[512,1024]{1,0:T(8,128)(2,1)} %collective-permute-done.1.second, f32[8,128]{1,0:T(8,128)S(1)} %wait.1.after), custom_call_target="tpu_custom_call" | custom-call | tf_op jit(solution)/shard_map/join/pallas_call | solution.py:506
  50.0 2.0 %pick.3.after = bf16[4,8,64,128]{3,2,1,0:T(8,128)(2,1)S(1)} custom-call(s32[128]{0:T(128)S(1)} %bitcast.19, bf16[4,8,64,128]{3,2,1,0:T(8,128)(2,1)} %leave.1.refs_1_.refs_0_, bf16[4,8,64,128]{3,2,1,0:T(8,128)(2,1)S(1)} %collective-permute-done.2.refs_1_.refs_2_, bf16[4,8,64,128]{3,2,1,0:T(8,128)(2,1)S(1)} %collective-permute-done.3.refs_2_.refs_3_, ...), custom_call_target="tpu_custom_call" | custom-call | tf_op jit(solution)/shard_map/pick/pallas_call | solution.py:621
  52.3 2.2 %collective-permute-start.6 = (bf16[256,512]{1,0:T(8,128)(2,1)S(1)}, bf16[256,512]{1,0:T(8,128)(2,1)S(1)}, u32[]{:S(2)}, u32[]{:S(2)}) collective-permute-start(bf16[256,512]{1,0:T(8,128)(2,1)S(1)} %normalise.2.refs_5_.a), channel_id=1, source_target_pairs={{0,12},{4,8},{8,4},{12,0},{1,13},{5,9},{9,5},{13,1},{2,14},{6,10},... | collective-permute-start | bytes 786440 | tf_op jit(solution)/shard_map/ppermute | solution.py:35
  55.4 1.0 collective-permute-start.11
  56.4 4.8 %collective-permute-done.6.near1 = bf16[256,512]{1,0:T(8,128)(2,1)S(1)} collective-permute-done((bf16[256,512]{1,0:T(8,128)(2,1)S(1)}, bf16[256,512]{1,0:T(8,128)(2,1)S(1)}, u32[]{:S(2)}, u32[]{:S(2)}) %collective-permute-start.6) | collective-permute-done | bytes 262176 | tf_op jit(solution)/shard_map/ppermute | solution.py:35
  61.3 1.5 %collective-permute-done.5.near0 = bf16[256,512]{1,0:T(8,128)(2,1)S(1)} collective-permute-done((bf16[256,512]{1,0:T(8,128)(2,1)S(1)}, bf16[256,512]{1,0:T(8,128)(2,1)S(1)}, u32[]{:S(2)}, u32[]{:S(2)}) %collective-permute-start.5) | collective-permute-done | bytes 262176 | tf_op jit(solution)/shard_map/ppermute | solution.py:35
  62.7 2.0 %project.2 = (bf16[256,1024]{1,0:T(8,128)(2,1)S(1)}, bf16[256,1024]{1,0:T(8,128)(2,1)S(1)}) custom-call(s32[128]{0:T(128)S(1)} %bitcast.20, bf16[256,512]{1,0:T(8,128)(2,1)S(1)} %normalise.2.refs_5_.a, bf16[256,512]{1,0:T(8,128)(2,1)S(1)} %collective-permute-done.5.near0, bf16[256,512]{1,0:T(8,128)(2,1)S(1)} %collective-permute-done.6.near1, ...), custom_call_target="tpu_custom_call" | custom-call | tf_op jit(solution)/shard_map/project/pallas_call | solution.py:335
  64.7 1.1 collective-permute-start.10
  66.7 2.1 %base.2.refs_7_ = f32[256,2048]{1,0:T(8,128)S(1)} custom-call(s32[128]{0:T(128)S(1)} %bitcast.21, bf16[256,512]{1,0:T(8,128)(2,1)S(1)} %normalise.2.refs_5_.a, bf16[256,512]{1,0:T(8,128)(2,1)S(1)} %collective-permute-done.5.near0, bf16[256,512]{1,0:T(8,128)(2,1)S(1)} %collective-permute-done.6.near1, bf16[512,2048]{1,0:T(8,128)(2,1)S(1)} %copy-done.1, ...), custom_call_target="tpu_custom_call" | custom-call | tf_op jit(solution)/shard_map/base/pallas_call | solution.py:366
  69.1 6.4 %ssm.3 = (f32[4,64,512]{2,1,0:T(8,128)S(1)}, f32[4,1,64]{2,1,0:T(1,128)S(1)}, bf16[8,8,64,128]{3,2,1,0:T(8,128)(2,1)}) custom-call(s32[128]{0:T(128)S(1)} %bitcast.22, bf16[8,64,512]{2,1,0:T(8,128)(2,1)S(1)} %copy-done.6, bf16[8,64,512]{2,1,0:T(8,128)(2,1)S(1)} %copy-done.8, bf16[8,256,128]{2,1,0:T(8,128)(2,1)S(1)} %bitcast.11, ...), custom_call_target="tpu_custom_call", output_to_operand_aliasing={{2}: (17, {})} | custom-call | tf_op jit(solution)/shard_map/ssm/pallas_call | solution.py:261
  75.8 4.3 %collective-permute-done.15 = f32[4,1,64]{2,1,0:T(1,128)S(1)} collective-permute-done((f32[4,1,64]{2,1,0:T(1,128)S(1)}, f32[4,1,64]{2,1,0:T(1,128)S(1)}, u32[]{:S(2)}, u32[]{:S(2)}) %collective-permute-start.15) | collective-permute-done | bytes 1056 | tf_op jit(solution)/shard_map/ppermute | solution.py:128
  80.1 1.4 collective-permute-start.16
  81.5 1.7 %combine.3 = (f32[256,512]{1,0:T(8,128)S(1)}, bf16[256,512]{1,0:T(8,128)(2,1)S(1)}, bf16[256,512]{1,0:T(8,128)(2,1)S(1)}, bf16[256,512]{1,0:T(8,128)(2,1)S(1)}) custom-call(s32[128]{0:T(128)S(1)} %bitcast.23, f32[256,2048]{1,0:T(8,128)S(1)} %base.2.refs_7_, bf16[256,1024]{1,0:T(8,128)(2,1)S(1)} %collective-permute-done.9.e0, ...), custom_call_target="tpu_custom_call" | custom-call | tf_op jit(solution)/shard_map/combine/pallas_call | solution.py:402
  83.2 1.6 %collective-permute-start.12 = (bf16[256,512]{1,0:T(8,128)(2,1)S(1)}, bf16[256,512]{1,0:T(8,128)(2,1)S(1)}, u32[]{:S(2)}, u32[]{:S(2)}) collective-permute-start(bf16[256,512]{1,0:T(8,128)(2,1)S(1)} %get-tuple-element.43), channel_id=1, source_target_pairs={{0,1},{1,2},{2,3},{3,0},{4,5},{5,6},{6,7},{7,4},{8,9},{9,10},{10,1... | collective-permute-start | bytes 786440 | tf_op jit(solution)/shard_map/ppermute | solution.py:31
  84.8 2.6 %collective-permute-start.13 = (bf16[256,512]{1,0:T(8,128)(2,1)S(1)}, bf16[256,512]{1,0:T(8,128)(2,1)S(1)}, u32[]{:S(2)}, u32[]{:S(2)}) collective-permute-start(bf16[256,512]{1,0:T(8,128)(2,1)S(1)} %get-tuple-element.44), channel_id=1, source_target_pairs={{0,3},{1,0},{2,1},{3,2},{4,7},{5,4},{6,5},{7,6},{8,11},{9,8},{10,9... | collective-permute-start | bytes 786440 | tf_op jit(solution)/shard_map/ppermute | solution.py:31
  87.5 1.1 collective-permute-start.18
  88.6 2.3 %collective-permute-start.17 = (bf16[256,512]{1,0:T(8,128)(2,1)S(1)}, bf16[256,512]{1,0:T(8,128)(2,1)S(1)}, u32[]{:S(2)}, u32[]{:S(2)}) collective-permute-start(bf16[256,512]{1,0:T(8,128)(2,1)S(1)} %normalise.3.a), channel_id=1, source_target_pairs={{0,4},{4,0},{8,12},{12,8},{1,5},{5,1},{9,13},{13,9},{2,6},{6,2},{1... | collective-permute-start | bytes 786440 | tf_op jit(solution)/shard_map/ppermute | solution.py:35
  90.9 3.5 %collective-permute-done.12.refs_1_ = bf16[256,512]{1,0:T(8,128)(2,1)S(1)} collective-permute-done((bf16[256,512]{1,0:T(8,128)(2,1)S(1)}, bf16[256,512]{1,0:T(8,128)(2,1)S(1)}, u32[]{:S(2)}, u32[]{:S(2)}) %collective-permute-start.12) | collective-permute-done | bytes 262176 | tf_op jit(solution)/shard_map/ppermute | solution.py:31
  94.4 2.3 %collective-permute-done.13.refs_2_ = bf16[256,512]{1,0:T(8,128)(2,1)S(1)} collective-permute-done((bf16[256,512]{1,0:T(8,128)(2,1)S(1)}, bf16[256,512]{1,0:T(8,128)(2,1)S(1)}, u32[]{:S(2)}, u32[]{:S(2)}) %collective-permute-start.13) | collective-permute-done | bytes 262176 | tf_op jit(solution)/shard_map/ppermute | solution.py:31
  96.8 2.0 %project.3 = (bf16[128,1024]{1,0:T(8,128)(2,1)S(1)}, bf16[128,1024]{1,0:T(8,128)(2,1)S(1)}, bf16[128,1024]{1,0:T(8,128)(2,1)S(1)}, bf16[128,1024]{1,0:T(8,128)(2,1)S(1)}) custom-call(s32[128]{0:T(128)S(1)} %bitcast.24, bf16[256,512]{1,0:T(8,128)(2,1)S(1)} %normalise.3.a, bf16[256,512]{1,0:T(8,128)(2,1)S(1)} %collective-permute-done.17.near0, ...), custom_call_target="tpu_custom_call" | custom-call | tf_op jit(solution)/shard_map/project/pallas_call | solution.py:335
  98.8 1.4 collective-permute-start.20
  100.2 1.3 collective-permute-start.19
  101.5 3.6 %collective-permute-start.14 = (bf16[256,512]{1,0:T(8,128)(2,1)S(1)}, bf16[256,512]{1,0:T(8,128)(2,1)S(1)}, u32[]{:S(2)}, u32[]{:S(2)}) collective-permute-start(bf16[256,512]{1,0:T(8,128)(2,1)S(1)} %get-tuple-element.45), channel_id=1, source_target_pairs={{0,2},{1,3},{2,0},{3,1},{4,6},{5,7},{6,4},{7,5},{8,10},{9,11},{10,... | collective-permute-start | bytes 786440 | tf_op jit(solution)/shard_map/ppermute | solution.py:31
  105.8 1.9 %collective-permute-start.25 = (bf16[128,1024]{1,0:T(8,128)(2,1)S(1)}, bf16[128,1024]{1,0:T(8,128)(2,1)S(1)}, u32[]{:S(2)}, u32[]{:S(2)}) collective-permute-start(bf16[128,1024]{1,0:T(8,128)(2,1)S(1)} %get-tuple-element.54), channel_id=1, source_target_pairs={{0,4},{4,0},{8,12},{12,8},{1,5},{5,1},{9,13},{13,9},{2,6},{6,2},{1... | collective-permute-start | bytes 786440 | tf_op jit(solution)/shard_map/ppermute | solution.py:35
  107.7 2.2 %base.3.refs_0_ = f32[256,2048]{1,0:T(8,128)S(1)} custom-call(s32[128]{0:T(128)S(1)} %bitcast.25, bf16[256,512]{1,0:T(8,128)(2,1)S(1)} %normalise.3.a, bf16[256,512]{1,0:T(8,128)(2,1)S(1)} %collective-permute-done.17.near0, bf16[256,512]{1,0:T(8,128)(2,1)S(1)} %collective-permute-done.18.near1, bf16[512,2048]{1,0:T(8,128)(2,1)S(1)} %copy-done.1, ...), custom_call_target="tpu_custom_call" | custom-call | tf_op jit(solution)/shard_map/base/pallas_call | solution.py:366
  109.9 1.2 combine.4
  111.2 2.5 %collective-permute-start.21 = (bf16[128,512]{1,0:T(8,128)(2,1)S(1)}, bf16[128,512]{1,0:T(8,128)(2,1)S(1)}, u32[]{:S(2)}, u32[]{:S(2)}) collective-permute-start(bf16[128,512]{1,0:T(8,128)(2,1)S(1)} %get-tuple-element.50), channel_id=1, source_target_pairs={{0,1},{1,2},{2,3},{3,0},{4,5},{5,6},{6,7},{7,4},{8,9},{9,10},{10,1... | collective-permute-start | bytes 393224 | tf_op jit(solution)/shard_map/ppermute | solution.py:31
  113.7 1.7 %collective-permute-start.22 = (bf16[128,512]{1,0:T(8,128)(2,1)S(1)}, bf16[128,512]{1,0:T(8,128)(2,1)S(1)}, u32[]{:S(2)}, u32[]{:S(2)}) collective-permute-start(bf16[128,512]{1,0:T(8,128)(2,1)S(1)} %get-tuple-element.51), channel_id=1, source_target_pairs={{0,3},{1,0},{2,1},{3,2},{4,7},{5,4},{6,5},{7,6},{8,11},{9,8},{10,9... | collective-permute-start | bytes 393224 | tf_op jit(solution)/shard_map/ppermute | solution.py:31
  115.4 3.2 %collective-permute-start.23 = (bf16[128,512]{1,0:T(8,128)(2,1)S(1)}, bf16[128,512]{1,0:T(8,128)(2,1)S(1)}, u32[]{:S(2)}, u32[]{:S(2)}) collective-permute-start(bf16[128,512]{1,0:T(8,128)(2,1)S(1)} %get-tuple-element.52), channel_id=1, source_target_pairs={{0,2},{1,3},{2,0},{3,1},{4,6},{5,7},{6,4},{7,5},{8,10},{9,11},{10,... | collective-permute-start | bytes 393224 | tf_op jit(solution)/shard_map/ppermute | solution.py:31
  118.6 4.3 %collective-permute-done.21.refs_1_ = bf16[128,512]{1,0:T(8,128)(2,1)S(1)} collective-permute-done((bf16[128,512]{1,0:T(8,128)(2,1)S(1)}, bf16[128,512]{1,0:T(8,128)(2,1)S(1)}, u32[]{:S(2)}, u32[]{:S(2)}) %collective-permute-start.21) | collective-permute-done | bytes 131104 | tf_op jit(solution)/shard_map/ppermute | solution.py:31
  123.8 1.2 combine.5
  125.0 2.2 %collective-permute-start.26 = (bf16[128,512]{1,0:T(8,128)(2,1)S(1)}, bf16[128,512]{1,0:T(8,128)(2,1)S(1)}, u32[]{:S(2)}, u32[]{:S(2)}) collective-permute-start(bf16[128,512]{1,0:T(8,128)(2,1)S(1)} %get-tuple-element.56), channel_id=1, source_target_pairs={{0,1},{1,2},{2,3},{3,0},{4,5},{5,6},{6,7},{7,4},{8,9},{9,10},{10,1... | collective-permute-start | bytes 393224 | tf_op jit(solution)/shard_map/ppermute | solution.py:31
  127.3 3.6 %collective-permute-start.27 = (bf16[128,512]{1,0:T(8,128)(2,1)S(1)}, bf16[128,512]{1,0:T(8,128)(2,1)S(1)}, u32[]{:S(2)}, u32[]{:S(2)}) collective-permute-start(bf16[128,512]{1,0:T(8,128)(2,1)S(1)} %get-tuple-element.57), channel_id=1, source_target_pairs={{0,2},{1,3},{2,0},{3,1},{4,6},{5,7},{6,4},{7,5},{8,10},{9,11},{10,... | collective-permute-start | bytes 393224 | tf_op jit(solution)/shard_map/ppermute | solution.py:31
  130.9 2.4 %collective-permute-start.28 = (bf16[128,512]{1,0:T(8,128)(2,1)S(1)}, bf16[128,512]{1,0:T(8,128)(2,1)S(1)}, u32[]{:S(2)}, u32[]{:S(2)}) collective-permute-start(bf16[128,512]{1,0:T(8,128)(2,1)S(1)} %get-tuple-element.58), channel_id=1, source_target_pairs={{0,3},{1,0},{2,1},{3,2},{4,7},{5,4},{6,5},{7,6},{8,11},{9,8},{10,9... | collective-permute-start | bytes 393224 | tf_op jit(solution)/shard_map/ppermute | solution.py:31
  133.3 1.0 collective-permute-done.26.refs_3_
  134.3 7.7 %collective-permute-done.27.refs_4_ = bf16[128,512]{1,0:T(8,128)(2,1)S(1)} collective-permute-done((bf16[128,512]{1,0:T(8,128)(2,1)S(1)}, bf16[128,512]{1,0:T(8,128)(2,1)S(1)}, u32[]{:S(2)}, u32[]{:S(2)}) %collective-permute-start.27) | collective-permute-done | bytes 131104 | tf_op jit(solution)/shard_map/ppermute | solution.py:31
  142.0 1.4 finish.1
  (85 shorter events, 9.7 us)
Async XLA Ops:
  2.9 8.1 %copy-start.16 = (s32[1,128]{1,0:T(1,128)}, s32[1,128]{1,0:T(1,128)S(1)}, u32[]{:S(2)}) copy-start(s32[1,128]{1,0:T(1,128)S(1)} %route.1) | copy-start | bytes 1540
  6.1 39.0 %collective-permute-start.4 = (bf16[4,8,64,128]{3,2,1,0:T(8,128)(2,1)}, bf16[4,8,64,128]{3,2,1,0:T(8,128)(2,1)S(1)}, u32[]{:S(2)}, u32[]{:S(2)}) collective-permute-start(bf16[4,8,64,128]{3,2,1,0:T(8,128)(2,1)} %leave.1.refs_1_.refs_0_), channel_id=1, source_target_pairs={{0,192},{64,0},{128,64},{192,128},{1,193},{65,1},{129,65},{193,129... | collective-permute-start | bytes 1572872 | tf_op jit(solution)/shard_map/ppermute | solution.py:31
  6.6 38.6 %collective-permute-start.3 = (bf16[4,8,64,128]{3,2,1,0:T(8,128)(2,1)}, bf16[4,8,64,128]{3,2,1,0:T(8,128)(2,1)S(1)}, u32[]{:S(2)}, u32[]{:S(2)}) collective-permute-start(bf16[4,8,64,128]{3,2,1,0:T(8,128)(2,1)} %leave.1.refs_1_.refs_0_), channel_id=1, source_target_pairs={{0,128},{64,192},{128,0},{192,64},{1,129},{65,193},{129,1},{193,65... | collective-permute-start | bytes 1572872 | tf_op jit(solution)/shard_map/ppermute | solution.py:31
  9.2 36.0 %collective-permute-start.2 = (bf16[4,8,64,128]{3,2,1,0:T(8,128)(2,1)}, bf16[4,8,64,128]{3,2,1,0:T(8,128)(2,1)S(1)}, u32[]{:S(2)}, u32[]{:S(2)}) collective-permute-start(bf16[4,8,64,128]{3,2,1,0:T(8,128)(2,1)} %leave.1.refs_1_.refs_0_), channel_id=1, source_target_pairs={{0,64},{64,128},{128,192},{192,0},{1,65},{65,129},{129,193},{193,1... | collective-permute-start | bytes 1572872 | tf_op jit(solution)/shard_map/ppermute | solution.py:31
  14.7 32.8 %collective-permute-start.1 = (bf16[512,1024]{1,0:T(8,128)(2,1)}, bf16[512,1024]{1,0:T(8,128)(2,1)}, u32[]{:S(2)}, u32[]{:S(2)}) collective-permute-start(bf16[512,1024]{1,0:T(8,128)(2,1)} %get-tuple-element.35), channel_id=1, source_target_pairs={{0,12},{4,8},{8,4},{12,0},{1,13},{5,9},{9,5},{13,1},{2,14},{6,10},... | collective-permute-start | bytes 3145736 | tf_op jit(solution)/shard_map/ppermute | solution.py:35
  15.3 6.2 %copy-start.3 = (bf16[8,8,64,128]{3,2,1,0:T(8,128)(2,1)S(1)}, bf16[8,8,64,128]{3,2,1,0:T(8,128)(2,1)}, u32[]{:S(2)}) copy-start(bf16[8,8,64,128]{3,2,1,0:T(8,128)(2,1)} %refs_0_.7) | copy-start | bytes 3145732
  15.3 6.2 %copy-start.6 = (bf16[8,64,512]{2,1,0:T(8,128)(2,1)S(1)}, bf16[8,64,512]{2,1,0:T(8,128)(2,1)}, u32[]{:S(2)}) copy-start(bf16[8,64,512]{2,1,0:T(8,128)(2,1)} %x_ref.3) | copy-start | bytes 1572868
  15.3 6.3 %copy-start.7 = (bf16[8,64,512]{2,1,0:T(8,128)(2,1)S(1)}, bf16[8,64,512]{2,1,0:T(8,128)(2,1)}, u32[]{:S(2)}) copy-start(bf16[8,64,512]{2,1,0:T(8,128)(2,1)} %g_ref.3) | copy-start | bytes 1572868
  15.3 6.3 %copy-start.9 = (bf16[8,64,4,128]{3,2,1,0:T(4,128)(2,1)S(1)}, bf16[8,64,4,128]{3,2,1,0:T(4,128)(2,1)}, u32[]{:S(2)}) copy-start(bf16[8,64,4,128]{3,2,1,0:T(4,128)(2,1)} %param.15) | copy-start | bytes 1572868
  15.3 6.3 %copy-start.11 = (bf16[8,64,4,128]{3,2,1,0:T(4,128)(2,1)S(1)}, bf16[8,64,4,128]{3,2,1,0:T(4,128)(2,1)}, u32[]{:S(2)}) copy-start(bf16[8,64,4,128]{3,2,1,0:T(4,128)(2,1)} %param.16) | copy-start | bytes 1572868
  15.3 6.3 %copy-start.15 = (f32[8,8,64]{2,1,0:T(8,128)S(1)}, f32[8,8,64]{2,1,0:T(8,128)}, u32[]{:S(2)}) copy-start(f32[8,8,64]{2,1,0:T(8,128)} %dt_ref.3) | copy-start | bytes 49156
  15.3 6.3 %copy-start.17 = (s32[1,128]{1,0:T(1,128)S(1)}, s32[1,128]{1,0:T(1,128)}, u32[]{:S(2)}) copy-start(s32[1,128]{1,0:T(1,128)} %copy-done.16) | copy-start | bytes 1540
  15.3 6.3 %copy-start.19 = (f32[8]{0:T(128)S(1)}, f32[8]{0:T(128)}, u32[]{:S(2)}) copy-start(f32[8]{0:T(128)} %bias.3) | copy-start | bytes 100
  15.3 6.3 %copy-start.20 = (f32[8]{0:T(128)S(1)}, f32[8]{0:T(128)}, u32[]{:S(2)}) copy-start(f32[8]{0:T(128)} %rate.3) | copy-start | bytes 100
  15.3 6.3 %copy-start.21 = (f32[8]{0:T(128)S(1)}, f32[8]{0:T(128)}, u32[]{:S(2)}) copy-start(f32[8]{0:T(128)} %skip.3) | copy-start | bytes 100
  15.4 32.1 %collective-permute-start = (bf16[512,1024]{1,0:T(8,128)(2,1)}, bf16[512,1024]{1,0:T(8,128)(2,1)}, u32[]{:S(2)}, u32[]{:S(2)}) collective-permute-start(bf16[512,1024]{1,0:T(8,128)(2,1)} %get-tuple-element.31.refs_1_), channel_id=1, source_target_pairs={{0,4},{4,0},{8,12},{12,8},{1,5},{5,1},{9,13},{13,9},{2,6},{6,2},{1... | collective-permute-start | bytes 3145736 | tf_op jit(solution)/shard_map/ppermute | solution.py:35
  47.3 2.7 %collective-permute-start.7 = (bf16[8,8,64,128]{3,2,1,0:T(8,128)(2,1)S(1)}, bf16[8,8,64,128]{3,2,1,0:T(8,128)(2,1)S(1)}, u32[]{:S(2)}, u32[]{:S(2)}) collective-permute-start(bf16[8,8,64,128]{3,2,1,0:T(8,128)(2,1)S(1)} %pick.2.after), channel_id=1, source_target_pairs={{0,16},{16,0},{1,17},{17,1},{2,18},{18,2},{3,19},{19,3},{4,20},{20... | collective-permute-start | bytes 3145736 | tf_op jit(solution)/shard_map/ppermute | solution.py:31
  47.4 1.7 %copy-start.14 = (f32[4,64,512]{2,1,0:T(8,128)S(1)}, f32[4,64,512]{2,1,0:T(8,128)}, u32[]{:S(2)}) copy-start(f32[4,64,512]{2,1,0:T(8,128)} %copy-done.13) | copy-start | bytes 1572868
  47.4 1.7 %copy-start.18 = (f32[512]{0:T(512)S(1)}, f32[512]{0:T(512)}, u32[]{:S(2)}) copy-start(f32[512]{0:T(512)} %param.21) | copy-start | bytes 6148
  52.0 10.7 %copy-start.4 = (bf16[512,1024]{1,0:T(8,128)(2,1)S(1)}, bf16[512,1024]{1,0:T(8,128)(2,1)}, u32[]{:S(2)}) copy-start(bf16[512,1024]{1,0:T(8,128)(2,1)} %get-tuple-element.36.w0) | copy-start | bytes 3145732
  52.0 10.7 %copy-start.5 = (bf16[512,1024]{1,0:T(8,128)(2,1)S(1)}, bf16[512,1024]{1,0:T(8,128)(2,1)}, u32[]{:S(2)}) copy-start(bf16[512,1024]{1,0:T(8,128)(2,1)} %get-tuple-element.37.w1) | copy-start | bytes 3145732
  52.0 10.7 %collective-permute-start.8 = (bf16[2,512,1024]{2,1,0:T(8,128)(2,1)S(1)}, bf16[2,512,1024]{2,1,0:T(8,128)(2,1)S(1)}, u32[]{:S(2)}, u32[]{:S(2)}) collective-permute-start(bf16[2,512,1024]{2,1,0:T(8,128)(2,1)S(1)} %hold.1.got), channel_id=1, source_target_pairs={{0,16},{16,0},{1,17},{17,1},{2,18},{18,2},{3,19},{19,3},{4,20},{20... | collective-permute-start | bytes 6291464 | tf_op jit(solution)/shard_map/ppermute | solution.py:31
  52.3 9.0 %collective-permute-start.6 = (bf16[256,512]{1,0:T(8,128)(2,1)S(1)}, bf16[256,512]{1,0:T(8,128)(2,1)S(1)}, u32[]{:S(2)}, u32[]{:S(2)}) collective-permute-start(bf16[256,512]{1,0:T(8,128)(2,1)S(1)} %normalise.2.refs_5_.a), channel_id=1, source_target_pairs={{0,12},{4,8},{8,4},{12,0},{1,13},{5,9},{9,5},{13,1},{2,14},{6,10},... | collective-permute-start | bytes 786440 | tf_op jit(solution)/shard_map/ppermute | solution.py:35
  54.4 8.3 %collective-permute-start.5 = (bf16[256,512]{1,0:T(8,128)(2,1)S(1)}, bf16[256,512]{1,0:T(8,128)(2,1)S(1)}, u32[]{:S(2)}, u32[]{:S(2)}) collective-permute-start(bf16[256,512]{1,0:T(8,128)(2,1)S(1)} %normalise.2.refs_5_.a), channel_id=1, source_target_pairs={{0,4},{4,0},{8,12},{12,8},{1,5},{5,1},{9,13},{13,9},{2,6},{6,2},{1... | collective-permute-start | bytes 786440 | tf_op jit(solution)/shard_map/ppermute | solution.py:35
  55.4 13.6 %collective-permute-start.11 = (bf16[4,8,64,128]{3,2,1,0:T(8,128)(2,1)S(1)}, bf16[4,8,64,128]{3,2,1,0:T(8,128)(2,1)S(1)}, u32[]{:S(2)}, u32[]{:S(2)}) collective-permute-start(bf16[4,8,64,128]{3,2,1,0:T(8,128)(2,1)S(1)} %pick.3.after), channel_id=1, source_target_pairs={{0,32},{32,0},{1,33},{33,1},{2,34},{34,2},{3,35},{35,3},{4,36},{36... | collective-permute-start | bytes 1572872 | tf_op jit(solution)/shard_map/ppermute | solution.py:31
  62.7 4.0 %copy-start.1 = (bf16[512,2048]{1,0:T(8,128)(2,1)S(1)}, bf16[512,2048]{1,0:T(8,128)(2,1)}, u32[]{:S(2)}) copy-start(bf16[512,2048]{1,0:T(8,128)(2,1)} %get-tuple-element.32.refs_1_.w) | copy-start | bytes 6291460
  64.7 16.8 %collective-permute-start.10 = (bf16[256,1024]{1,0:T(8,128)(2,1)S(1)}, bf16[256,1024]{1,0:T(8,128)(2,1)S(1)}, u32[]{:S(2)}, u32[]{:S(2)}) collective-permute-start(bf16[256,1024]{1,0:T(8,128)(2,1)S(1)} %get-tuple-element.39), channel_id=1, source_target_pairs={{0,4},{4,0},{8,12},{12,8},{1,5},{5,1},{9,13},{13,9},{2,6},{6,2},{1... | collective-permute-start | bytes 1572872 | tf_op jit(solution)/shard_map/ppermute | solution.py:35
  65.8 3.3 %copy-start.8 = (bf16[8,64,512]{2,1,0:T(8,128)(2,1)S(1)}, bf16[8,64,512]{2,1,0:T(8,128)(2,1)}, u32[]{:S(2)}) copy-start(bf16[8,64,512]{2,1,0:T(8,128)(2,1)} %g_ref.3) | copy-start | bytes 1572868
  65.8 3.3 %copy-start.10 = (bf16[8,64,4,128]{3,2,1,0:T(4,128)(2,1)S(1)}, bf16[8,64,4,128]{3,2,1,0:T(4,128)(2,1)}, u32[]{:S(2)}) copy-start(bf16[8,64,4,128]{3,2,1,0:T(4,128)(2,1)} %param.15) | copy-start | bytes 1572868
  65.8 3.3 %copy-start.12 = (bf16[8,64,4,128]{3,2,1,0:T(4,128)(2,1)S(1)}, bf16[8,64,4,128]{3,2,1,0:T(4,128)(2,1)}, u32[]{:S(2)}) copy-start(bf16[8,64,4,128]{3,2,1,0:T(4,128)(2,1)} %param.16) | copy-start | bytes 1572868
  65.8 15.7 %collective-permute-start.9 = (bf16[256,1024]{1,0:T(8,128)(2,1)S(1)}, bf16[256,1024]{1,0:T(8,128)(2,1)S(1)}, u32[]{:S(2)}, u32[]{:S(2)}) collective-permute-start(bf16[256,1024]{1,0:T(8,128)(2,1)S(1)} %get-tuple-element.38.after), channel_id=1, source_target_pairs={{0,12},{4,8},{8,4},{12,0},{1,13},{5,9},{9,5},{13,1},{2,14},{6,10},... | collective-permute-start | bytes 1572872 | tf_op jit(solution)/shard_map/ppermute | solution.py:35
  75.5 4.6 %collective-permute-start.15 = (f32[4,1,64]{2,1,0:T(1,128)S(1)}, f32[4,1,64]{2,1,0:T(1,128)S(1)}, u32[]{:S(2)}, u32[]{:S(2)}) collective-permute-start(f32[4,1,64]{2,1,0:T(1,128)S(1)} %get-tuple-element.41.refs_0_), channel_id=1, source_target_pairs={{0,1},{1,0},{2,3},{3,2},{4,5},{5,4},{6,7},{7,6},{8,9},{9,8},{10,11... | collective-permute-start | bytes 3080 | tf_op jit(solution)/shard_map/ppermute | solution.py:128
  80.1 7.3 %collective-permute-start.16 = (f32[4,1,64]{2,1,0:T(1,128)S(1)}, f32[4,1,64]{2,1,0:T(1,128)S(1)}, u32[]{:S(2)}, u32[]{:S(2)}) collective-permute-start(f32[4,1,64]{2,1,0:T(1,128)S(1)} %add.5.refs_0_), channel_id=1, source_target_pairs={{0,3},{1,2},{2,1},{3,0},{4,7},{5,6},{6,5},{7,4},{8,11},{9,10},{10,... | collective-permute-start | bytes 3080 | tf_op jit(solution)/shard_map/ppermute | solution.py:130
  83.2 11.2 %collective-permute-start.12 = (bf16[256,512]{1,0:T(8,128)(2,1)S(1)}, bf16[256,512]{1,0:T(8,128)(2,1)S(1)}, u32[]{:S(2)}, u32[]{:S(2)}) collective-permute-start(bf16[256,512]{1,0:T(8,128)(2,1)S(1)} %get-tuple-element.43), channel_id=1, source_target_pairs={{0,1},{1,2},{2,3},{3,0},{4,5},{5,6},{6,7},{7,4},{8,9},{9,10},{10,1... | collective-permute-start | bytes 786440 | tf_op jit(solution)/shard_map/ppermute | solution.py:31
  84.8 11.9 %collective-permute-start.13 = (bf16[256,512]{1,0:T(8,128)(2,1)S(1)}, bf16[256,512]{1,0:T(8,128)(2,1)S(1)}, u32[]{:S(2)}, u32[]{:S(2)}) collective-permute-start(bf16[256,512]{1,0:T(8,128)(2,1)S(1)} %get-tuple-element.44), channel_id=1, source_target_pairs={{0,3},{1,0},{2,1},{3,2},{4,7},{5,4},{6,5},{7,6},{8,11},{9,8},{10,9... | collective-permute-start | bytes 786440 | tf_op jit(solution)/shard_map/ppermute | solution.py:31
  87.5 9.3 %collective-permute-start.18 = (bf16[256,512]{1,0:T(8,128)(2,1)S(1)}, bf16[256,512]{1,0:T(8,128)(2,1)S(1)}, u32[]{:S(2)}, u32[]{:S(2)}) collective-permute-start(bf16[256,512]{1,0:T(8,128)(2,1)S(1)} %normalise.3.a), channel_id=1, source_target_pairs={{0,12},{4,8},{8,4},{12,0},{1,13},{5,9},{9,5},{13,1},{2,14},{6,10},... | collective-permute-start | bytes 786440 | tf_op jit(solution)/shard_map/ppermute | solution.py:35
  88.6 8.2 %collective-permute-start.17 = (bf16[256,512]{1,0:T(8,128)(2,1)S(1)}, bf16[256,512]{1,0:T(8,128)(2,1)S(1)}, u32[]{:S(2)}, u32[]{:S(2)}) collective-permute-start(bf16[256,512]{1,0:T(8,128)(2,1)S(1)} %normalise.3.a), channel_id=1, source_target_pairs={{0,4},{4,0},{8,12},{12,8},{1,5},{5,1},{9,13},{13,9},{2,6},{6,2},{1... | collective-permute-start | bytes 786440 | tf_op jit(solution)/shard_map/ppermute | solution.py:35
  98.8 11.1 %collective-permute-start.20 = (bf16[128,1024]{1,0:T(8,128)(2,1)S(1)}, bf16[128,1024]{1,0:T(8,128)(2,1)S(1)}, u32[]{:S(2)}, u32[]{:S(2)}) collective-permute-start(bf16[128,1024]{1,0:T(8,128)(2,1)S(1)} %get-tuple-element.48), channel_id=1, source_target_pairs={{0,4},{4,0},{8,12},{12,8},{1,5},{5,1},{9,13},{13,9},{2,6},{6,2},{1... | collective-permute-start | bytes 786440 | tf_op jit(solution)/shard_map/ppermute | solution.py:35
  100.2 9.7 %collective-permute-start.19 = (bf16[128,1024]{1,0:T(8,128)(2,1)S(1)}, bf16[128,1024]{1,0:T(8,128)(2,1)S(1)}, u32[]{:S(2)}, u32[]{:S(2)}) collective-permute-start(bf16[128,1024]{1,0:T(8,128)(2,1)S(1)} %get-tuple-element.47.after), channel_id=1, source_target_pairs={{0,12},{4,8},{8,4},{12,0},{1,13},{5,9},{9,5},{13,1},{2,14},{6,10},... | collective-permute-start | bytes 786440 | tf_op jit(solution)/shard_map/ppermute | solution.py:35
  101.5 13.8 %collective-permute-start.14 = (bf16[256,512]{1,0:T(8,128)(2,1)S(1)}, bf16[256,512]{1,0:T(8,128)(2,1)S(1)}, u32[]{:S(2)}, u32[]{:S(2)}) collective-permute-start(bf16[256,512]{1,0:T(8,128)(2,1)S(1)} %get-tuple-element.45), channel_id=1, source_target_pairs={{0,2},{1,3},{2,0},{3,1},{4,6},{5,7},{6,4},{7,5},{8,10},{9,11},{10,... | collective-permute-start | bytes 786440 | tf_op jit(solution)/shard_map/ppermute | solution.py:31
  105.1 18.7 %collective-permute-start.24 = (bf16[128,1024]{1,0:T(8,128)(2,1)S(1)}, bf16[128,1024]{1,0:T(8,128)(2,1)S(1)}, u32[]{:S(2)}, u32[]{:S(2)}) collective-permute-start(bf16[128,1024]{1,0:T(8,128)(2,1)S(1)} %get-tuple-element.53), channel_id=1, source_target_pairs={{0,12},{4,8},{8,4},{12,0},{1,13},{5,9},{9,5},{13,1},{2,14},{6,10},... | collective-permute-start | bytes 786440 | tf_op jit(solution)/shard_map/ppermute | solution.py:35
  105.8 18.0 %collective-permute-start.25 = (bf16[128,1024]{1,0:T(8,128)(2,1)S(1)}, bf16[128,1024]{1,0:T(8,128)(2,1)S(1)}, u32[]{:S(2)}, u32[]{:S(2)}) collective-permute-start(bf16[128,1024]{1,0:T(8,128)(2,1)S(1)} %get-tuple-element.54), channel_id=1, source_target_pairs={{0,4},{4,0},{8,12},{12,8},{1,5},{5,1},{9,13},{13,9},{2,6},{6,2},{1... | collective-permute-start | bytes 786440 | tf_op jit(solution)/shard_map/ppermute | solution.py:35
  111.2 11.8 %collective-permute-start.21 = (bf16[128,512]{1,0:T(8,128)(2,1)S(1)}, bf16[128,512]{1,0:T(8,128)(2,1)S(1)}, u32[]{:S(2)}, u32[]{:S(2)}) collective-permute-start(bf16[128,512]{1,0:T(8,128)(2,1)S(1)} %get-tuple-element.50), channel_id=1, source_target_pairs={{0,1},{1,2},{2,3},{3,0},{4,5},{5,6},{6,7},{7,4},{8,9},{9,10},{10,1... | collective-permute-start | bytes 393224 | tf_op jit(solution)/shard_map/ppermute | solution.py:31
  113.7 10.1 %collective-permute-start.22 = (bf16[128,512]{1,0:T(8,128)(2,1)S(1)}, bf16[128,512]{1,0:T(8,128)(2,1)S(1)}, u32[]{:S(2)}, u32[]{:S(2)}) collective-permute-start(bf16[128,512]{1,0:T(8,128)(2,1)S(1)} %get-tuple-element.51), channel_id=1, source_target_pairs={{0,3},{1,0},{2,1},{3,2},{4,7},{5,4},{6,5},{7,6},{8,11},{9,8},{10,9... | collective-permute-start | bytes 393224 | tf_op jit(solution)/shard_map/ppermute | solution.py:31
  115.4 17.8 %collective-permute-start.23 = (bf16[128,512]{1,0:T(8,128)(2,1)S(1)}, bf16[128,512]{1,0:T(8,128)(2,1)S(1)}, u32[]{:S(2)}, u32[]{:S(2)}) collective-permute-start(bf16[128,512]{1,0:T(8,128)(2,1)S(1)} %get-tuple-element.52), channel_id=1, source_target_pairs={{0,2},{1,3},{2,0},{3,1},{4,6},{5,7},{6,4},{7,5},{8,10},{9,11},{10,... | collective-permute-start | bytes 393224 | tf_op jit(solution)/shard_map/ppermute | solution.py:31
  125.0 9.2 %collective-permute-start.26 = (bf16[128,512]{1,0:T(8,128)(2,1)S(1)}, bf16[128,512]{1,0:T(8,128)(2,1)S(1)}, u32[]{:S(2)}, u32[]{:S(2)}) collective-permute-start(bf16[128,512]{1,0:T(8,128)(2,1)S(1)} %get-tuple-element.56), channel_id=1, source_target_pairs={{0,1},{1,2},{2,3},{3,0},{4,5},{5,6},{6,7},{7,4},{8,9},{9,10},{10,1... | collective-permute-start | bytes 393224 | tf_op jit(solution)/shard_map/ppermute | solution.py:31
  127.3 14.7 %collective-permute-start.27 = (bf16[128,512]{1,0:T(8,128)(2,1)S(1)}, bf16[128,512]{1,0:T(8,128)(2,1)S(1)}, u32[]{:S(2)}, u32[]{:S(2)}) collective-permute-start(bf16[128,512]{1,0:T(8,128)(2,1)S(1)} %get-tuple-element.57), channel_id=1, source_target_pairs={{0,2},{1,3},{2,0},{3,1},{4,6},{5,7},{6,4},{7,5},{8,10},{9,11},{10,... | collective-permute-start | bytes 393224 | tf_op jit(solution)/shard_map/ppermute | solution.py:31
  130.9 11.1 %collective-permute-start.28 = (bf16[128,512]{1,0:T(8,128)(2,1)S(1)}, bf16[128,512]{1,0:T(8,128)(2,1)S(1)}, u32[]{:S(2)}, u32[]{:S(2)}) collective-permute-start(bf16[128,512]{1,0:T(8,128)(2,1)S(1)} %get-tuple-element.58), channel_id=1, source_target_pairs={{0,3},{1,0},{2,1},{3,2},{4,7},{5,4},{6,5},{7,6},{8,11},{9,8},{10,9... | collective-permute-start | bytes 393224 | tf_op jit(solution)/shard_map/ppermute | solution.py:31
  (5 other events, 4.9 us)

commit v4 on v3

--- a/solution.py
+++ b/solution.py
@@ -124,10 +124,25 @@
     return jnp.concatenate([jnp.where(first, ref[2 * p], ref[2 * p + 1]) for p in range(4)], axis=0)
 
 
-def fly(value):
-    near = lax.ppermute(value, "zh", [(i, i ^ 1) for i in range(4)])
-    half = value + near
-    return [half, lax.ppermute(half, "zh", [(i, i ^ 3) for i in range(4)])]
+def add_kernel(first, second, after, out):
+    out[...] = first[...] + second[...]
+
+
+def add(first, second, after):
+    whole = pl.BlockSpec(memory_space=pltpu.VMEM)
+    return pl.pallas_call(
+        add_kernel,
+        in_specs=[whole, whole, ANYWHERE],
+        out_specs=whole,
+        out_shape=jax.ShapeDtypeStruct(first.shape, F32),
+        compiler_params=LIMIT,
+        cost_estimate=FREE,
+        name="add",
+    )(first, second, after)
+
+
+def trade(value, mask):
+    return lax.ppermute(value, "zh", [(i, i ^ mask) for i in range(4)])
 
 
 def product(left, right):
@@ -453,7 +468,7 @@
             scratch_shapes=[pltpu.SemaphoreType.DMA((len(widths), 4))],
         ),
         out_shape=[jax.ShapeDtypeStruct((512, width), BF16) for width in widths],
-        compiler_params=WIDE,
+        compiler_params=WIDE if first == 0 else LIMIT,
         cost_estimate=FREE,
         name="slices",
     )(table, w, after)
@@ -656,7 +671,6 @@
 
     shares = slices(table, out_weight, buf, 0, 2)
     got = [flip(shares[0], 1), flip(shares[1], 3)]
-    part0, part1, own = slices(table, out_weight, shares[0], 2, 5)
 
     b = write_basis.reshape(ROWS, 4 * NEW, 128)
     c = read_basis.reshape(ROWS, 4 * NEW, 128)
@@ -680,7 +694,7 @@
         zs = combine(table, base, *moved, after, part)
         return [zs[0]] + [shift(zs[k], "zh", k) for k in (1, 2, 3)]
 
-    gated1, sq1, states1 = ssm(start=0, sources=[ssm_states], alias=None, after=[own])
+    gated1, sq1, states1 = ssm(start=0, sources=[ssm_states], alias=None, after=[shares[0]])
     sums1 = lax.psum(sq1, "zh")
 
     chosen = pick(table, along, BESIDE, BESIDE_ROW, 8, sums1)
@@ -691,6 +705,7 @@
     across = shift(picked, "zl", 1)
     near_weights = hold(near_weights, picked)
     weights = [near_weights, shift(near_weights, "c", 1)]
+    part0, part1, own = slices(table, out_weight, picked, 2, 5)
     sent1 = project(table, a1, nears1, [part0, part1], weights, picked)
     moved1 = [flip(sent1[0], 3), flip(sent1[1], 1)]
     base1 = base_project(table, a1, nears1, own, weights, sent1[0])
@@ -698,9 +713,10 @@
     gated2, sq2, new_states = ssm(
         start=HALF, sources=[ssm_states, *along, beside, across], alias=states1, after=[base1]
     )
-    sums2 = fly(sq2)
+    near_sums = trade(sq2, 1)
     z0, r1, r2, r3 = reduce_rest(base1, moved1, [sq2])
-    a2, nears2 = spread_rows(gated2, sums2, z0)
+    half_sums = add(sq2, near_sums, z0)
+    a2, nears2 = spread_rows(gated2, [half_sums, trade(half_sums, 3)], z0)
     gathered = gather_sum([z0, r1, r3], F32)
     sent2 = project(table, a2, nears2, [part0, part1], weights, gathered, 2)
     moved2 = [[flip(sent2[k], 3), flip(sent2[2 + k], 1)] for k in range(2)]

time: 145 us -> 140 us (0.966)
  Pallas kernels: 43.9 us -> 40 us
    ppermute x2, waiting for transfers between devices: 4.26 us -> 0.01 us  [trade(): return lax.ppermute(value, 'zh', [(i, i ^ mask) for i in range(4)])]
    pallas_call x2, Pallas kernels: 8.51 us -> 4.57 us  [slices(): pl.pallas_call(functools.partial(slice_kernel, first, len(widths)), grid_...]
    ppermute x15, starting transfers between devices: 29.7 us -> 25.9 us  [shift(): lax.ppermute(value, axis, [(i, (i + step) % size) for i in range(size)])]
    ppermute x2, starting transfers between devices: 1.73 us -> 4.93 us  [trade(): return lax.ppermute(value, 'zh', [(i, i ^ mask) for i in range(4)])]
    ppermute x15, waiting for transfers between devices: 20.7 us -> 23.4 us  [shift(): lax.ppermute(value, axis, [(i, (i + step) % size) for i in range(size)])]
    ppermute x12, waiting for transfers between devices: 6.32 us -> 7.95 us  [flip(): return lax.ppermute(value, 'x', [(i, i ^ mask) for i in range(4)])]
  transfers between devices with their start and end apart: 29 -> 29, of which waited for: 11 -> 13; matrix products, arithmetic and copies ran while one was open for 0% -> 0% of each run, Pallas kernels for 25% -> 23%
where the time goes in v4:
time: 140 us; the launch traced here: 139 us
  starting transfers between devices  46.2 us (33%)
  Pallas kernels  40 us (29%)
  waiting for transfers between devices  31.4 us (22%)
  blocking collectives  14.9 us (11%)
  local copies, waits for them, and re-layouts  5.36 us (4%)
    ppermute x15, starting transfers between devices, shift(): lax.ppermute(value, axis, [(i, (i + step) % size) for i in range(size)])  25.9 us
    ppermute x15, waiting for transfers between devices, shift(): lax.ppermute(value, axis, [(i, (i + step) % size) for i in range(size)])  23.4 us
    ppermute x12, starting transfers between devices, flip(): return lax.ppermute(value, 'x', [(i, i ^ mask) for i in range(4)])  15.4 us
    psum x1, blocking collectives, local(): sums1 = lax.psum(sq1, 'zh')  14.9 us
    pallas_call x2, Pallas kernels, run_ssm(): pl.pallas_call(functools.partial(ssm_kernel, start, len(sources), unused)...  12.7 us
    ppermute x12, waiting for transfers between devices, flip(): return lax.ppermute(value, 'x', [(i, i ^ mask) for i in range(4)])  7.95 us
    unnamed x48, local copies, waits for them, and re-layouts  5.28 us
    ppermute x2, starting transfers between devices, trade(): return lax.ppermute(value, 'zh', [(i, i ^ mask) for i in range(4)])  4.93 us
  transfers between devices with their start and end apart: 29, of which 13 were waited for; matrix products, arithmetic and copies ran while one was open for 0% of the time, Pallas kernels for 23%

profile of v4, /device:TPU:12, one launch (start us, length us, event | category | flops | bytes accessed | tf_op | source)
XLA Modules:
  0.0 139.1 jit_solution(5387650176377366666)
XLA Ops:
  2.9 1.2 copy-done
  4.2 1.9 %leave.1.refs_1_.refs_0_ = bf16[4,8,64,128]{3,2,1,0:T(8,128)(2,1)} custom-call(s32[128]{0:T(128)S(1)} %bitcast.16, bf16[8,8,64,128]{3,2,1,0:T(8,128)(2,1)S(1)} %copy-done), custom_call_target="tpu_custom_call" | custom-call | tf_op jit(solution)/shard_map/leave/pallas_call | solution.py:605
  6.7 2.6 %collective-permute-start.3 = (bf16[4,8,64,128]{3,2,1,0:T(8,128)(2,1)}, bf16[4,8,64,128]{3,2,1,0:T(8,128)(2,1)S(1)}, u32[]{:S(2)}, u32[]{:S(2)}) collective-permute-start(bf16[4,8,64,128]{3,2,1,0:T(8,128)(2,1)} %leave.1.refs_1_.refs_0_), channel_id=1, source_target_pairs={{0,128},{64,192},{128,0},{192,64},{1,129},{65,193},{129,1},{193,65... | collective-permute-start | bytes 1572872 | tf_op jit(solution)/shard_map/ppermute | solution.py:31
  9.3 1.9 %collective-permute-start.2 = (bf16[4,8,64,128]{3,2,1,0:T(8,128)(2,1)}, bf16[4,8,64,128]{3,2,1,0:T(8,128)(2,1)S(1)}, u32[]{:S(2)}, u32[]{:S(2)}) collective-permute-start(bf16[4,8,64,128]{3,2,1,0:T(8,128)(2,1)} %leave.1.refs_1_.refs_0_), channel_id=1, source_target_pairs={{0,64},{64,128},{128,192},{192,0},{1,65},{65,129},{129,193},{193,1... | collective-permute-start | bytes 1572872 | tf_op jit(solution)/shard_map/ppermute | solution.py:31
  11.2 3.6 %slices.2 = (bf16[512,1024]{1,0:T(8,128)(2,1)}, bf16[512,1024]{1,0:T(8,128)(2,1)}) custom-call(s32[128]{0:T(128)} %bitcast.17, bf16[512,8192]{1,0:T(8,128)(2,1)} %refs_0_.6, bf16[4,8,64,128]{3,2,1,0:T(8,128)(2,1)} %leave.1.refs_1_.refs_0_), custom_call_target="tpu_custom_call" | custom-call | tf_op jit(solution)/shard_map/slices/pallas_call | solution.py:461
  15.4 1.1 collective-permute-start
  16.7 1.2 copy-done.9
  18.5 6.2 %ssm.2 = (f32[4,64,512]{2,1,0:T(8,128)S(1)}, f32[4,1,64]{2,1,0:T(1,128)S(1)}, bf16[8,8,64,128]{3,2,1,0:T(8,128)(2,1)}) custom-call(s32[128]{0:T(128)S(1)} %bitcast.18, bf16[8,64,512]{2,1,0:T(8,128)(2,1)S(1)} %copy-done.2, bf16[8,64,512]{2,1,0:T(8,128)(2,1)S(1)} %copy-done.3, bf16[8,256,128]{2,1,0:T(8,128)(2,1)S(1)} %bitcast.12, ...), custom_call_target="tpu_custom_call" | custom-call | tf_op jit(solution)/shard_map/ssm/pallas_call | solution.py:276
  25.5 14.9 %psum.7.refs_4_.refs_0_ = f32[4,1,64]{2,1,0:T(1,128)S(1)} all-reduce(f32[4,1,64]{2,1,0:T(1,128)S(1)} %get-tuple-element.33), channel_id=1, replica_groups=mesh['y'=4,'zl'=2,'c'=2,'x'=4,'zh'=4] {'zh'}, use_global_device_ids=true, to_apply=%region_0.0 | all-reduce | flops 256 | bytes 2048 | tf_op jit(solution)/shard_map/psum | solution.py:698
  40.4 2.0 %pick.2.after = bf16[8,8,64,128]{3,2,1,0:T(8,128)(2,1)S(1)} custom-call(s32[128]{0:T(128)S(1)} %bitcast.19, bf16[4,8,64,128]{3,2,1,0:T(8,128)(2,1)} %leave.1.refs_1_.refs_0_, bf16[4,8,64,128]{3,2,1,0:T(8,128)(2,1)S(1)} %collective-permute-done.2.refs_1_.refs_2_, bf16[4,8,64,128]{3,2,1,0:T(8,128)(2,1)S(1)} %collective-permute-done.3.refs_2_.refs_3_, ...), custom_call_target="tpu_custom_call" | custom-call | tf_op jit(solution)/shard_map/pick/pallas_call | solution.py:636
  42.6 1.7 %join.1.refs_2_.value = bf16[2,512,1024]{2,1,0:T(8,128)(2,1)S(1)} custom-call(bf16[512,1024]{1,0:T(8,128)(2,1)} %collective-permute-done.first, bf16[512,1024]{1,0:T(8,128)(2,1)} %collective-permute-done.1.second, f32[8,128]{1,0:T(8,128)S(1)} %wait.1.after), custom_call_target="tpu_custom_call" | custom-call | tf_op jit(solution)/shard_map/join/pallas_call | solution.py:521
  45.2 2.0 %pick.3.refs_1_.after = bf16[4,8,64,128]{3,2,1,0:T(8,128)(2,1)S(1)} custom-call(s32[128]{0:T(128)S(1)} %bitcast.20, bf16[4,8,64,128]{3,2,1,0:T(8,128)(2,1)} %leave.1.refs_1_.refs_0_, bf16[4,8,64,128]{3,2,1,0:T(8,128)(2,1)S(1)} %collective-permute-done.2.refs_1_.refs_2_, bf16[4,8,64,128]{3,2,1,0:T(8,128)(2,1)S(1)} %collective-permute-done.3.refs_2_.refs_3_, ...), custom_call_target="tpu_custom_call" | custom-call | tf_op jit(solution)/shard_map/pick/pallas_call | solution.py:636
  47.4 2.2 %collective-permute-start.6 = (bf16[256,512]{1,0:T(8,128)(2,1)S(1)}, bf16[256,512]{1,0:T(8,128)(2,1)S(1)}, u32[]{:S(2)}, u32[]{:S(2)}) collective-permute-start(bf16[256,512]{1,0:T(8,128)(2,1)S(1)} %normalise.2.refs_5_.a), channel_id=1, source_target_pairs={{0,12},{4,8},{8,4},{12,0},{1,13},{5,9},{9,5},{13,1},{2,14},{6,10},... | collective-permute-start | bytes 786440 | tf_op jit(solution)/shard_map/ppermute | solution.py:35
  50.4 1.2 collective-permute-start.11
  51.6 1.0 slices.3
  52.6 3.8 %collective-permute-done.6.near1 = bf16[256,512]{1,0:T(8,128)(2,1)S(1)} collective-permute-done((bf16[256,512]{1,0:T(8,128)(2,1)S(1)}, bf16[256,512]{1,0:T(8,128)(2,1)S(1)}, u32[]{:S(2)}, u32[]{:S(2)}) %collective-permute-start.6) | collective-permute-done | bytes 262176 | tf_op jit(solution)/shard_map/ppermute | solution.py:35
  56.4 1.5 %collective-permute-done.5.near0 = bf16[256,512]{1,0:T(8,128)(2,1)S(1)} collective-permute-done((bf16[256,512]{1,0:T(8,128)(2,1)S(1)}, bf16[256,512]{1,0:T(8,128)(2,1)S(1)}, u32[]{:S(2)}, u32[]{:S(2)}) %collective-permute-start.5) | collective-permute-done | bytes 262176 | tf_op jit(solution)/shard_map/ppermute | solution.py:35
  57.9 2.0 %project.2 = (bf16[256,1024]{1,0:T(8,128)(2,1)S(1)}, bf16[256,1024]{1,0:T(8,128)(2,1)S(1)}) custom-call(s32[128]{0:T(128)S(1)} %bitcast.22, bf16[256,512]{1,0:T(8,128)(2,1)S(1)} %normalise.2.refs_5_.a, bf16[256,512]{1,0:T(8,128)(2,1)S(1)} %collective-permute-done.5.near0, bf16[256,512]{1,0:T(8,128)(2,1)S(1)} %collective-permute-done.6.near1, ...), custom_call_target="tpu_custom_call" | custom-call | tf_op jit(solution)/shard_map/project/pallas_call | solution.py:350
  61.6 2.1 %base.2.refs_7_ = f32[256,2048]{1,0:T(8,128)S(1)} custom-call(s32[128]{0:T(128)S(1)} %bitcast.23, bf16[256,512]{1,0:T(8,128)(2,1)S(1)} %normalise.2.refs_5_.a, bf16[256,512]{1,0:T(8,128)(2,1)S(1)} %collective-permute-done.5.near0, bf16[256,512]{1,0:T(8,128)(2,1)S(1)} %collective-permute-done.6.near1, bf16[512,2048]{1,0:T(8,128)(2,1)S(1)} %get-tuple-element.35.w, ...), custom_call_target="tpu_custom_call" | custom-call | tf_op jit(solution)/shard_map/base/pallas_call | solution.py:381
  64.0 6.4 %ssm.3 = (f32[4,64,512]{2,1,0:T(8,128)S(1)}, f32[4,1,64]{2,1,0:T(1,128)S(1)}, bf16[8,8,64,128]{3,2,1,0:T(8,128)(2,1)}) custom-call(s32[128]{0:T(128)S(1)} %bitcast.24, bf16[8,64,512]{2,1,0:T(8,128)(2,1)S(1)} %copy-done.2, bf16[8,64,512]{2,1,0:T(8,128)(2,1)S(1)} %copy-done.4, bf16[8,256,128]{2,1,0:T(8,128)(2,1)S(1)} %bitcast.13, ...), custom_call_target="tpu_custom_call", output_to_operand_aliasing={{2}: (17, {})} | custom-call | tf_op jit(solution)/shard_map/ssm/pallas_call | solution.py:276
  70.5 0.9 collective-permute-start.15
  71.4 1.6 %collective-permute-done.10.e1 = bf16[256,1024]{1,0:T(8,128)(2,1)S(1)} collective-permute-done((bf16[256,1024]{1,0:T(8,128)(2,1)S(1)}, bf16[256,1024]{1,0:T(8,128)(2,1)S(1)}, u32[]{:S(2)}, u32[]{:S(2)}) %collective-permute-start.10) | collective-permute-done | bytes 524320 | tf_op jit(solution)/shard_map/ppermute | solution.py:35
  73.5 1.7 %combine.3 = (f32[256,512]{1,0:T(8,128)S(1)}, bf16[256,512]{1,0:T(8,128)(2,1)S(1)}, bf16[256,512]{1,0:T(8,128)(2,1)S(1)}, bf16[256,512]{1,0:T(8,128)(2,1)S(1)}) custom-call(s32[128]{0:T(128)S(1)} %bitcast.25, f32[256,2048]{1,0:T(8,128)S(1)} %base.2.refs_7_, bf16[256,1024]{1,0:T(8,128)(2,1)S(1)} %collective-permute-done.9.e0, ...), custom_call_target="tpu_custom_call" | custom-call | tf_op jit(solution)/shard_map/combine/pallas_call | solution.py:417
  75.2 4.0 %collective-permute-start.16 = (f32[4,1,64]{2,1,0:T(1,128)S(1)}, f32[4,1,64]{2,1,0:T(1,128)S(1)}, u32[]{:S(2)}, u32[]{:S(2)}) collective-permute-start(f32[4,1,64]{2,1,0:T(1,128)S(1)} %add.3.refs_0_), channel_id=1, source_target_pairs={{0,3},{1,2},{2,1},{3,0},{4,7},{5,6},{6,5},{7,4},{8,11},{9,10},{10,... | collective-permute-start | bytes 3080 | tf_op jit(solution)/shard_map/ppermute | solution.py:145
  79.2 1.5 %collective-permute-start.12 = (bf16[256,512]{1,0:T(8,128)(2,1)S(1)}, bf16[256,512]{1,0:T(8,128)(2,1)S(1)}, u32[]{:S(2)}, u32[]{:S(2)}) collective-permute-start(bf16[256,512]{1,0:T(8,128)(2,1)S(1)} %get-tuple-element.43), channel_id=1, source_target_pairs={{0,1},{1,2},{2,3},{3,0},{4,5},{5,6},{6,7},{7,4},{8,9},{9,10},{10,1... | collective-permute-start | bytes 786440 | tf_op jit(solution)/shard_map/ppermute | solution.py:31
  80.7 2.7 %collective-permute-start.13 = (bf16[256,512]{1,0:T(8,128)(2,1)S(1)}, bf16[256,512]{1,0:T(8,128)(2,1)S(1)}, u32[]{:S(2)}, u32[]{:S(2)}) collective-permute-start(bf16[256,512]{1,0:T(8,128)(2,1)S(1)} %get-tuple-element.44), channel_id=1, source_target_pairs={{0,3},{1,0},{2,1},{3,2},{4,7},{5,4},{6,5},{7,6},{8,11},{9,8},{10,9... | collective-permute-start | bytes 786440 | tf_op jit(solution)/shard_map/ppermute | solution.py:31
  83.5 1.2 collective-permute-start.18
  84.7 2.2 %collective-permute-start.17 = (bf16[256,512]{1,0:T(8,128)(2,1)S(1)}, bf16[256,512]{1,0:T(8,128)(2,1)S(1)}, u32[]{:S(2)}, u32[]{:S(2)}) collective-permute-start(bf16[256,512]{1,0:T(8,128)(2,1)S(1)} %normalise.3.a), channel_id=1, source_target_pairs={{0,4},{4,0},{8,12},{12,8},{1,5},{5,1},{9,13},{13,9},{2,6},{6,2},{1... | collective-permute-start | bytes 786440 | tf_op jit(solution)/shard_map/ppermute | solution.py:35
  86.9 5.7 %collective-permute-done.12.refs_1_ = bf16[256,512]{1,0:T(8,128)(2,1)S(1)} collective-permute-done((bf16[256,512]{1,0:T(8,128)(2,1)S(1)}, bf16[256,512]{1,0:T(8,128)(2,1)S(1)}, u32[]{:S(2)}, u32[]{:S(2)}) %collective-permute-start.12) | collective-permute-done | bytes 262176 | tf_op jit(solution)/shard_map/ppermute | solution.py:31
  93.3 2.0 %project.3 = (bf16[128,1024]{1,0:T(8,128)(2,1)S(1)}, bf16[128,1024]{1,0:T(8,128)(2,1)S(1)}, bf16[128,1024]{1,0:T(8,128)(2,1)S(1)}, bf16[128,1024]{1,0:T(8,128)(2,1)S(1)}) custom-call(s32[128]{0:T(128)S(1)} %bitcast.26, bf16[256,512]{1,0:T(8,128)(2,1)S(1)} %normalise.3.a, bf16[256,512]{1,0:T(8,128)(2,1)S(1)} %collective-permute-done.17.near0, ...), custom_call_target="tpu_custom_call" | custom-call | tf_op jit(solution)/shard_map/project/pallas_call | solution.py:350
  95.3 2.1 %collective-permute-start.20 = (bf16[128,1024]{1,0:T(8,128)(2,1)S(1)}, bf16[128,1024]{1,0:T(8,128)(2,1)S(1)}, u32[]{:S(2)}, u32[]{:S(2)}) collective-permute-start(bf16[128,1024]{1,0:T(8,128)(2,1)S(1)} %get-tuple-element.48), channel_id=1, source_target_pairs={{0,4},{4,0},{8,12},{12,8},{1,5},{5,1},{9,13},{13,9},{2,6},{6,2},{1... | collective-permute-start | bytes 786440 | tf_op jit(solution)/shard_map/ppermute | solution.py:35
  97.3 1.1 collective-permute-start.19
  98.4 2.3 %collective-permute-start.14 = (bf16[256,512]{1,0:T(8,128)(2,1)S(1)}, bf16[256,512]{1,0:T(8,128)(2,1)S(1)}, u32[]{:S(2)}, u32[]{:S(2)}) collective-permute-start(bf16[256,512]{1,0:T(8,128)(2,1)S(1)} %get-tuple-element.45), channel_id=1, source_target_pairs={{0,2},{1,3},{2,0},{3,1},{4,6},{5,7},{6,4},{7,5},{8,10},{9,11},{10,... | collective-permute-start | bytes 786440 | tf_op jit(solution)/shard_map/ppermute | solution.py:31
  101.6 1.3 collective-permute-start.25
  102.9 2.2 %base.3.refs_0_ = f32[256,2048]{1,0:T(8,128)S(1)} custom-call(s32[128]{0:T(128)S(1)} %bitcast.27, bf16[256,512]{1,0:T(8,128)(2,1)S(1)} %normalise.3.a, bf16[256,512]{1,0:T(8,128)(2,1)S(1)} %collective-permute-done.17.near0, bf16[256,512]{1,0:T(8,128)(2,1)S(1)} %collective-permute-done.18.near1, bf16[512,2048]{1,0:T(8,128)(2,1)S(1)} %get-tuple-element.35.w, ...), custom_call_target="tpu_custom_call" | custom-call | tf_op jit(solution)/shard_map/base/pallas_call | solution.py:381
  105.7 1.2 combine.4
  106.9 3.4 %collective-permute-start.21 = (bf16[128,512]{1,0:T(8,128)(2,1)S(1)}, bf16[128,512]{1,0:T(8,128)(2,1)S(1)}, u32[]{:S(2)}, u32[]{:S(2)}) collective-permute-start(bf16[128,512]{1,0:T(8,128)(2,1)S(1)} %get-tuple-element.50), channel_id=1, source_target_pairs={{0,1},{1,2},{2,3},{3,0},{4,5},{5,6},{6,7},{7,4},{8,9},{9,10},{10,1... | collective-permute-start | bytes 393224 | tf_op jit(solution)/shard_map/ppermute | solution.py:31
  110.3 1.4 %collective-permute-start.22 = (bf16[128,512]{1,0:T(8,128)(2,1)S(1)}, bf16[128,512]{1,0:T(8,128)(2,1)S(1)}, u32[]{:S(2)}, u32[]{:S(2)}) collective-permute-start(bf16[128,512]{1,0:T(8,128)(2,1)S(1)} %get-tuple-element.51), channel_id=1, source_target_pairs={{0,3},{1,0},{2,1},{3,2},{4,7},{5,4},{6,5},{7,6},{8,11},{9,8},{10,9... | collective-permute-start | bytes 393224 | tf_op jit(solution)/shard_map/ppermute | solution.py:31
  111.7 2.7 %collective-permute-start.23 = (bf16[128,512]{1,0:T(8,128)(2,1)S(1)}, bf16[128,512]{1,0:T(8,128)(2,1)S(1)}, u32[]{:S(2)}, u32[]{:S(2)}) collective-permute-start(bf16[128,512]{1,0:T(8,128)(2,1)S(1)} %get-tuple-element.52), channel_id=1, source_target_pairs={{0,2},{1,3},{2,0},{3,1},{4,6},{5,7},{6,4},{7,5},{8,10},{9,11},{10,... | collective-permute-start | bytes 393224 | tf_op jit(solution)/shard_map/ppermute | solution.py:31
  114.5 4.8 %collective-permute-done.21.refs_1_ = bf16[128,512]{1,0:T(8,128)(2,1)S(1)} collective-permute-done((bf16[128,512]{1,0:T(8,128)(2,1)S(1)}, bf16[128,512]{1,0:T(8,128)(2,1)S(1)}, u32[]{:S(2)}, u32[]{:S(2)}) %collective-permute-start.21) | collective-permute-done | bytes 131104 | tf_op jit(solution)/shard_map/ppermute | solution.py:31
  119.3 2.0 %collective-permute-done.22.refs_2_ = bf16[128,512]{1,0:T(8,128)(2,1)S(1)} collective-permute-done((bf16[128,512]{1,0:T(8,128)(2,1)S(1)}, bf16[128,512]{1,0:T(8,128)(2,1)S(1)}, u32[]{:S(2)}, u32[]{:S(2)}) %collective-permute-start.22) | collective-permute-done | bytes 131104 | tf_op jit(solution)/shard_map/ppermute | solution.py:31
  121.4 1.2 combine.5
  122.6 1.5 %collective-permute-start.26 = (bf16[128,512]{1,0:T(8,128)(2,1)S(1)}, bf16[128,512]{1,0:T(8,128)(2,1)S(1)}, u32[]{:S(2)}, u32[]{:S(2)}) collective-permute-start(bf16[128,512]{1,0:T(8,128)(2,1)S(1)} %get-tuple-element.56), channel_id=1, source_target_pairs={{0,1},{1,2},{2,3},{3,0},{4,5},{5,6},{6,7},{7,4},{8,9},{9,10},{10,1... | collective-permute-start | bytes 393224 | tf_op jit(solution)/shard_map/ppermute | solution.py:31
  124.1 2.1 %collective-permute-start.27 = (bf16[128,512]{1,0:T(8,128)(2,1)S(1)}, bf16[128,512]{1,0:T(8,128)(2,1)S(1)}, u32[]{:S(2)}, u32[]{:S(2)}) collective-permute-start(bf16[128,512]{1,0:T(8,128)(2,1)S(1)} %get-tuple-element.57), channel_id=1, source_target_pairs={{0,2},{1,3},{2,0},{3,1},{4,6},{5,7},{6,4},{7,5},{8,10},{9,11},{10,... | collective-permute-start | bytes 393224 | tf_op jit(solution)/shard_map/ppermute | solution.py:31
  126.2 1.8 %collective-permute-start.28 = (bf16[128,512]{1,0:T(8,128)(2,1)S(1)}, bf16[128,512]{1,0:T(8,128)(2,1)S(1)}, u32[]{:S(2)}, u32[]{:S(2)}) collective-permute-start(bf16[128,512]{1,0:T(8,128)(2,1)S(1)} %get-tuple-element.58), channel_id=1, source_target_pairs={{0,3},{1,0},{2,1},{3,2},{4,7},{5,4},{6,5},{7,6},{8,11},{9,8},{10,9... | collective-permute-start | bytes 393224 | tf_op jit(solution)/shard_map/ppermute | solution.py:31
  128.0 3.8 %collective-permute-done.26.refs_3_ = bf16[128,512]{1,0:T(8,128)(2,1)S(1)} collective-permute-done((bf16[128,512]{1,0:T(8,128)(2,1)S(1)}, bf16[128,512]{1,0:T(8,128)(2,1)S(1)}, u32[]{:S(2)}, u32[]{:S(2)}) %collective-permute-start.26) | collective-permute-done | bytes 131104 | tf_op jit(solution)/shard_map/ppermute | solution.py:31
  131.9 5.6 %collective-permute-done.27.refs_4_ = bf16[128,512]{1,0:T(8,128)(2,1)S(1)} collective-permute-done((bf16[128,512]{1,0:T(8,128)(2,1)S(1)}, bf16[128,512]{1,0:T(8,128)(2,1)S(1)}, u32[]{:S(2)}, u32[]{:S(2)}) %collective-permute-start.27) | collective-permute-done | bytes 131104 | tf_op jit(solution)/shard_map/ppermute | solution.py:31
  137.5 1.4 %finish.1 = bf16[8,64,512]{2,1,0:T(8,128)(2,1)} custom-call(s32[128]{0:T(128)S(1)} %bitcast.30, bf16[256,512]{1,0:T(8,128)(2,1)S(1)} %gather_sum.4.refs_0_.half, f32[128,512]{1,0:T(8,128)S(1)} %gather_sum.5.refs_1_.refs_0_, bf16[128,512]{1,0:T(8,128)(2,1)S(1)} %collective-permute-done.23.refs_1_, f32[128,512]{1,0:T(8,128)S(1)} %get-tuple-element.55.refs_2_, ...), custom_call_target="tpu_custom_call" | custom-call | tf_op jit(solution)/shard_map/finish/pallas_call | solution.py:581
  (86 shorter events, 11.9 us)
Async XLA Ops:
  2.9 8.3 %copy-start.13 = (s32[1,128]{1,0:T(1,128)}, s32[1,128]{1,0:T(1,128)S(1)}, u32[]{:S(2)}) copy-start(s32[1,128]{1,0:T(1,128)S(1)} %route.1) | copy-start | bytes 1540
  2.9 1.2 copy-start
  6.1 10.5 %copy-start.1 = (bf16[8,8,64,128]{3,2,1,0:T(8,128)(2,1)S(1)}, bf16[8,8,64,128]{3,2,1,0:T(8,128)(2,1)}, u32[]{:S(2)}) copy-start(bf16[8,8,64,128]{3,2,1,0:T(8,128)(2,1)} %refs_0_.7) | copy-start | bytes 3145732
  6.1 10.5 %copy-start.2 = (bf16[8,64,512]{2,1,0:T(8,128)(2,1)S(1)}, bf16[8,64,512]{2,1,0:T(8,128)(2,1)}, u32[]{:S(2)}) copy-start(bf16[8,64,512]{2,1,0:T(8,128)(2,1)} %x_ref.3) | copy-start | bytes 1572868
  6.1 10.5 %copy-start.3 = (bf16[8,64,512]{2,1,0:T(8,128)(2,1)S(1)}, bf16[8,64,512]{2,1,0:T(8,128)(2,1)}, u32[]{:S(2)}) copy-start(bf16[8,64,512]{2,1,0:T(8,128)(2,1)} %g_ref.3) | copy-start | bytes 1572868
  6.1 10.5 %copy-start.5 = (bf16[8,64,4,128]{3,2,1,0:T(4,128)(2,1)S(1)}, bf16[8,64,4,128]{3,2,1,0:T(4,128)(2,1)}, u32[]{:S(2)}) copy-start(bf16[8,64,4,128]{3,2,1,0:T(4,128)(2,1)} %param.15) | copy-start | bytes 1572868
  6.1 10.5 %copy-start.7 = (bf16[8,64,4,128]{3,2,1,0:T(4,128)(2,1)S(1)}, bf16[8,64,4,128]{3,2,1,0:T(4,128)(2,1)}, u32[]{:S(2)}) copy-start(bf16[8,64,4,128]{3,2,1,0:T(4,128)(2,1)} %param.16) | copy-start | bytes 1572868
  6.1 10.5 %copy-start.12 = (f32[8,8,64]{2,1,0:T(8,128)S(1)}, f32[8,8,64]{2,1,0:T(8,128)}, u32[]{:S(2)}) copy-start(f32[8,8,64]{2,1,0:T(8,128)} %dt_ref.3) | copy-start | bytes 49156
  6.2 10.5 %copy-start.17 = (f32[8]{0:T(128)S(1)}, f32[8]{0:T(128)}, u32[]{:S(2)}) copy-start(f32[8]{0:T(128)} %bias.3) | copy-start | bytes 100
  6.2 10.5 %copy-start.18 = (f32[8]{0:T(128)S(1)}, f32[8]{0:T(128)}, u32[]{:S(2)}) copy-start(f32[8]{0:T(128)} %rate.3) | copy-start | bytes 100
  6.2 10.5 %copy-start.19 = (f32[8]{0:T(128)S(1)}, f32[8]{0:T(128)}, u32[]{:S(2)}) copy-start(f32[8]{0:T(128)} %skip.3) | copy-start | bytes 100
  6.2 34.2 %collective-permute-start.4 = (bf16[4,8,64,128]{3,2,1,0:T(8,128)(2,1)}, bf16[4,8,64,128]{3,2,1,0:T(8,128)(2,1)S(1)}, u32[]{:S(2)}, u32[]{:S(2)}) collective-permute-start(bf16[4,8,64,128]{3,2,1,0:T(8,128)(2,1)} %leave.1.refs_1_.refs_0_), channel_id=1, source_target_pairs={{0,192},{64,0},{128,64},{192,128},{1,193},{65,1},{129,65},{193,129... | collective-permute-start | bytes 1572872 | tf_op jit(solution)/shard_map/ppermute | solution.py:31
  6.7 33.7 %collective-permute-start.3 = (bf16[4,8,64,128]{3,2,1,0:T(8,128)(2,1)}, bf16[4,8,64,128]{3,2,1,0:T(8,128)(2,1)S(1)}, u32[]{:S(2)}, u32[]{:S(2)}) collective-permute-start(bf16[4,8,64,128]{3,2,1,0:T(8,128)(2,1)} %leave.1.refs_1_.refs_0_), channel_id=1, source_target_pairs={{0,128},{64,192},{128,0},{192,64},{1,129},{65,193},{129,1},{193,65... | collective-permute-start | bytes 1572872 | tf_op jit(solution)/shard_map/ppermute | solution.py:31
  9.3 31.1 %collective-permute-start.2 = (bf16[4,8,64,128]{3,2,1,0:T(8,128)(2,1)}, bf16[4,8,64,128]{3,2,1,0:T(8,128)(2,1)S(1)}, u32[]{:S(2)}, u32[]{:S(2)}) collective-permute-start(bf16[4,8,64,128]{3,2,1,0:T(8,128)(2,1)} %leave.1.refs_1_.refs_0_), channel_id=1, source_target_pairs={{0,64},{64,128},{128,192},{192,0},{1,65},{65,129},{129,193},{193,1... | collective-permute-start | bytes 1572872 | tf_op jit(solution)/shard_map/ppermute | solution.py:31
  14.8 27.8 %collective-permute-start.1 = (bf16[512,1024]{1,0:T(8,128)(2,1)}, bf16[512,1024]{1,0:T(8,128)(2,1)}, u32[]{:S(2)}, u32[]{:S(2)}) collective-permute-start(bf16[512,1024]{1,0:T(8,128)(2,1)} %get-tuple-element.34), channel_id=1, source_target_pairs={{0,12},{4,8},{8,4},{12,0},{1,13},{5,9},{9,5},{13,1},{2,14},{6,10},... | collective-permute-start | bytes 3145736 | tf_op jit(solution)/shard_map/ppermute | solution.py:35
  15.4 27.1 %collective-permute-start = (bf16[512,1024]{1,0:T(8,128)(2,1)}, bf16[512,1024]{1,0:T(8,128)(2,1)}, u32[]{:S(2)}, u32[]{:S(2)}) collective-permute-start(bf16[512,1024]{1,0:T(8,128)(2,1)} %get-tuple-element.31.refs_1_), channel_id=1, source_target_pairs={{0,4},{4,0},{8,12},{12,8},{1,5},{5,1},{9,13},{13,9},{2,6},{6,2},{1... | collective-permute-start | bytes 3145736 | tf_op jit(solution)/shard_map/ppermute | solution.py:35
  18.5 22.0 %copy-start.15 = (s32[1,128]{1,0:T(1,128)S(1)}, s32[1,128]{1,0:T(1,128)}, u32[]{:S(2)}) copy-start(s32[1,128]{1,0:T(1,128)} %copy-done.13) | copy-start | bytes 1540
  42.4 2.7 %collective-permute-start.7 = (bf16[8,8,64,128]{3,2,1,0:T(8,128)(2,1)S(1)}, bf16[8,8,64,128]{3,2,1,0:T(8,128)(2,1)S(1)}, u32[]{:S(2)}, u32[]{:S(2)}) collective-permute-start(bf16[8,8,64,128]{3,2,1,0:T(8,128)(2,1)S(1)} %pick.2.after), channel_id=1, source_target_pairs={{0,16},{16,0},{1,17},{17,1},{2,18},{18,2},{3,19},{19,3},{4,20},{20... | collective-permute-start | bytes 3145736 | tf_op jit(solution)/shard_map/ppermute | solution.py:31
  42.5 1.8 %copy-start.11 = (f32[4,64,512]{2,1,0:T(8,128)S(1)}, f32[4,64,512]{2,1,0:T(8,128)}, u32[]{:S(2)}) copy-start(f32[4,64,512]{2,1,0:T(8,128)} %copy-done.10) | copy-start | bytes 1572868
  42.6 1.8 %copy-start.16 = (f32[512]{0:T(512)S(1)}, f32[512]{0:T(512)}, u32[]{:S(2)}) copy-start(f32[512]{0:T(512)} %param.21) | copy-start | bytes 6148
  42.6 9.0 %slice-start = ((s8[8388608]{0:T(1024)(128)(4,1)}), s8[4194304]{0:T(1024)(128)(4,1)S(1)}, s32[]{:S(2)}) async-start(s8[8388608]{0:T(1024)(128)(4,1)} %bitcast.10), calls=%async_computation | async-start | bytes 8388608
  44.5 7.1 %slice-start.1 = ((s8[8388608]{0:T(1024)(128)(4,1)}), s8[4194304]{0:T(1024)(128)(4,1)S(1)}, s32[]{:S(2)}) async-start(s8[8388608]{0:T(1024)(128)(4,1)} %bitcast.10), calls=%async_computation.1 | async-start | bytes 8388608
  47.2 10.7 %collective-permute-start.8 = (bf16[2,512,1024]{2,1,0:T(8,128)(2,1)S(1)}, bf16[2,512,1024]{2,1,0:T(8,128)(2,1)S(1)}, u32[]{:S(2)}, u32[]{:S(2)}) collective-permute-start(bf16[2,512,1024]{2,1,0:T(8,128)(2,1)S(1)} %hold.1.got), channel_id=1, source_target_pairs={{0,16},{16,0},{1,17},{17,1},{2,18},{18,2},{3,19},{19,3},{4,20},{20... | collective-permute-start | bytes 6291464 | tf_op jit(solution)/shard_map/ppermute | solution.py:31
  47.4 9.0 %collective-permute-start.6 = (bf16[256,512]{1,0:T(8,128)(2,1)S(1)}, bf16[256,512]{1,0:T(8,128)(2,1)S(1)}, u32[]{:S(2)}, u32[]{:S(2)}) collective-permute-start(bf16[256,512]{1,0:T(8,128)(2,1)S(1)} %normalise.2.refs_5_.a), channel_id=1, source_target_pairs={{0,12},{4,8},{8,4},{12,0},{1,13},{5,9},{9,5},{13,1},{2,14},{6,10},... | collective-permute-start | bytes 786440 | tf_op jit(solution)/shard_map/ppermute | solution.py:35
  49.6 8.3 %collective-permute-start.5 = (bf16[256,512]{1,0:T(8,128)(2,1)S(1)}, bf16[256,512]{1,0:T(8,128)(2,1)S(1)}, u32[]{:S(2)}, u32[]{:S(2)}) collective-permute-start(bf16[256,512]{1,0:T(8,128)(2,1)S(1)} %normalise.2.refs_5_.a), channel_id=1, source_target_pairs={{0,4},{4,0},{8,12},{12,8},{1,5},{5,1},{9,13},{13,9},{2,6},{6,2},{1... | collective-permute-start | bytes 786440 | tf_op jit(solution)/shard_map/ppermute | solution.py:35
  50.4 13.6 %collective-permute-start.11 = (bf16[4,8,64,128]{3,2,1,0:T(8,128)(2,1)S(1)}, bf16[4,8,64,128]{3,2,1,0:T(8,128)(2,1)S(1)}, u32[]{:S(2)}, u32[]{:S(2)}) collective-permute-start(bf16[4,8,64,128]{3,2,1,0:T(8,128)(2,1)S(1)} %pick.3.refs_1_.after), channel_id=1, source_target_pairs={{0,32},{32,0},{1,33},{33,1},{2,34},{34,2},{3,35},{35,3},{4,36},{36... | collective-permute-start | bytes 1572872 | tf_op jit(solution)/shard_map/ppermute | solution.py:31
  59.8 13.1 %collective-permute-start.10 = (bf16[256,1024]{1,0:T(8,128)(2,1)S(1)}, bf16[256,1024]{1,0:T(8,128)(2,1)S(1)}, u32[]{:S(2)}, u32[]{:S(2)}) collective-permute-start(bf16[256,1024]{1,0:T(8,128)(2,1)S(1)} %get-tuple-element.39), channel_id=1, source_target_pairs={{0,4},{4,0},{8,12},{12,8},{1,5},{5,1},{9,13},{13,9},{2,6},{6,2},{1... | collective-permute-start | bytes 1572872 | tf_op jit(solution)/shard_map/ppermute | solution.py:35
  60.7 12.8 %collective-permute-start.9 = (bf16[256,1024]{1,0:T(8,128)(2,1)S(1)}, bf16[256,1024]{1,0:T(8,128)(2,1)S(1)}, u32[]{:S(2)}, u32[]{:S(2)}) collective-permute-start(bf16[256,1024]{1,0:T(8,128)(2,1)S(1)} %get-tuple-element.38.after), channel_id=1, source_target_pairs={{0,12},{4,8},{8,4},{12,0},{1,13},{5,9},{9,5},{13,1},{2,14},{6,10},... | collective-permute-start | bytes 1572872 | tf_op jit(solution)/shard_map/ppermute | solution.py:35
  61.6 2.4 %copy-start.4 = (bf16[8,64,512]{2,1,0:T(8,128)(2,1)S(1)}, bf16[8,64,512]{2,1,0:T(8,128)(2,1)}, u32[]{:S(2)}) copy-start(bf16[8,64,512]{2,1,0:T(8,128)(2,1)} %g_ref.3) | copy-start | bytes 1572868
  61.6 2.4 %copy-start.6 = (bf16[8,64,4,128]{3,2,1,0:T(4,128)(2,1)S(1)}, bf16[8,64,4,128]{3,2,1,0:T(4,128)(2,1)}, u32[]{:S(2)}) copy-start(bf16[8,64,4,128]{3,2,1,0:T(4,128)(2,1)} %param.15) | copy-start | bytes 1572868
  61.6 2.4 %copy-start.8 = (bf16[8,64,4,128]{3,2,1,0:T(4,128)(2,1)S(1)}, bf16[8,64,4,128]{3,2,1,0:T(4,128)(2,1)}, u32[]{:S(2)}) copy-start(bf16[8,64,4,128]{3,2,1,0:T(4,128)(2,1)} %param.16) | copy-start | bytes 1572868
  70.5 4.7 %collective-permute-start.15 = (f32[4,1,64]{2,1,0:T(1,128)S(1)}, f32[4,1,64]{2,1,0:T(1,128)S(1)}, u32[]{:S(2)}, u32[]{:S(2)}) collective-permute-start(f32[4,1,64]{2,1,0:T(1,128)S(1)} %get-tuple-element.41.refs_0_.first), channel_id=1, source_target_pairs={{0,1},{1,0},{2,3},{3,2},{4,5},{5,4},{6,7},{7,6},{8,9},{9,8},{10,11... | collective-permute-start | bytes 3080 | tf_op jit(solution)/shard_map/ppermute | solution.py:145
  75.2 8.1 %collective-permute-start.16 = (f32[4,1,64]{2,1,0:T(1,128)S(1)}, f32[4,1,64]{2,1,0:T(1,128)S(1)}, u32[]{:S(2)}, u32[]{:S(2)}) collective-permute-start(f32[4,1,64]{2,1,0:T(1,128)S(1)} %add.3.refs_0_), channel_id=1, source_target_pairs={{0,3},{1,2},{2,1},{3,0},{4,7},{5,6},{6,5},{7,4},{8,11},{9,10},{10,... | collective-permute-start | bytes 3080 | tf_op jit(solution)/shard_map/ppermute | solution.py:145
  79.2 13.4 %collective-permute-start.12 = (bf16[256,512]{1,0:T(8,128)(2,1)S(1)}, bf16[256,512]{1,0:T(8,128)(2,1)S(1)}, u32[]{:S(2)}, u32[]{:S(2)}) collective-permute-start(bf16[256,512]{1,0:T(8,128)(2,1)S(1)} %get-tuple-element.43), channel_id=1, source_target_pairs={{0,1},{1,2},{2,3},{3,0},{4,5},{5,6},{6,7},{7,4},{8,9},{9,10},{10,1... | collective-permute-start | bytes 786440 | tf_op jit(solution)/shard_map/ppermute | solution.py:31
  80.7 12.5 %collective-permute-start.13 = (bf16[256,512]{1,0:T(8,128)(2,1)S(1)}, bf16[256,512]{1,0:T(8,128)(2,1)S(1)}, u32[]{:S(2)}, u32[]{:S(2)}) collective-permute-start(bf16[256,512]{1,0:T(8,128)(2,1)S(1)} %get-tuple-element.44), channel_id=1, source_target_pairs={{0,3},{1,0},{2,1},{3,2},{4,7},{5,4},{6,5},{7,6},{8,11},{9,8},{10,9... | collective-permute-start | bytes 786440 | tf_op jit(solution)/shard_map/ppermute | solution.py:31
  83.5 9.8 %collective-permute-start.18 = (bf16[256,512]{1,0:T(8,128)(2,1)S(1)}, bf16[256,512]{1,0:T(8,128)(2,1)S(1)}, u32[]{:S(2)}, u32[]{:S(2)}) collective-permute-start(bf16[256,512]{1,0:T(8,128)(2,1)S(1)} %normalise.3.a), channel_id=1, source_target_pairs={{0,12},{4,8},{8,4},{12,0},{1,13},{5,9},{9,5},{13,1},{2,14},{6,10},... | collective-permute-start | bytes 786440 | tf_op jit(solution)/shard_map/ppermute | solution.py:35
  84.7 8.5 %collective-permute-start.17 = (bf16[256,512]{1,0:T(8,128)(2,1)S(1)}, bf16[256,512]{1,0:T(8,128)(2,1)S(1)}, u32[]{:S(2)}, u32[]{:S(2)}) collective-permute-start(bf16[256,512]{1,0:T(8,128)(2,1)S(1)} %normalise.3.a), channel_id=1, source_target_pairs={{0,4},{4,0},{8,12},{12,8},{1,5},{5,1},{9,13},{13,9},{2,6},{6,2},{1... | collective-permute-start | bytes 786440 | tf_op jit(solution)/shard_map/ppermute | solution.py:35
  95.3 9.9 %collective-permute-start.20 = (bf16[128,1024]{1,0:T(8,128)(2,1)S(1)}, bf16[128,1024]{1,0:T(8,128)(2,1)S(1)}, u32[]{:S(2)}, u32[]{:S(2)}) collective-permute-start(bf16[128,1024]{1,0:T(8,128)(2,1)S(1)} %get-tuple-element.48), channel_id=1, source_target_pairs={{0,4},{4,0},{8,12},{12,8},{1,5},{5,1},{9,13},{13,9},{2,6},{6,2},{1... | collective-permute-start | bytes 786440 | tf_op jit(solution)/shard_map/ppermute | solution.py:35
  97.3 8.3 %collective-permute-start.19 = (bf16[128,1024]{1,0:T(8,128)(2,1)S(1)}, bf16[128,1024]{1,0:T(8,128)(2,1)S(1)}, u32[]{:S(2)}, u32[]{:S(2)}) collective-permute-start(bf16[128,1024]{1,0:T(8,128)(2,1)S(1)} %get-tuple-element.47.after), channel_id=1, source_target_pairs={{0,12},{4,8},{8,4},{12,0},{1,13},{5,9},{9,5},{13,1},{2,14},{6,10},... | collective-permute-start | bytes 786440 | tf_op jit(solution)/shard_map/ppermute | solution.py:35
  98.4 13.3 %collective-permute-start.14 = (bf16[256,512]{1,0:T(8,128)(2,1)S(1)}, bf16[256,512]{1,0:T(8,128)(2,1)S(1)}, u32[]{:S(2)}, u32[]{:S(2)}) collective-permute-start(bf16[256,512]{1,0:T(8,128)(2,1)S(1)} %get-tuple-element.45), channel_id=1, source_target_pairs={{0,2},{1,3},{2,0},{3,1},{4,6},{5,7},{6,4},{7,5},{8,10},{9,11},{10,... | collective-permute-start | bytes 786440 | tf_op jit(solution)/shard_map/ppermute | solution.py:31
  100.7 20.7 %collective-permute-start.24 = (bf16[128,1024]{1,0:T(8,128)(2,1)S(1)}, bf16[128,1024]{1,0:T(8,128)(2,1)S(1)}, u32[]{:S(2)}, u32[]{:S(2)}) collective-permute-start(bf16[128,1024]{1,0:T(8,128)(2,1)S(1)} %get-tuple-element.53), channel_id=1, source_target_pairs={{0,12},{4,8},{8,4},{12,0},{1,13},{5,9},{9,5},{13,1},{2,14},{6,10},... | collective-permute-start | bytes 786440 | tf_op jit(solution)/shard_map/ppermute | solution.py:35
  101.6 19.7 %collective-permute-start.25 = (bf16[128,1024]{1,0:T(8,128)(2,1)S(1)}, bf16[128,1024]{1,0:T(8,128)(2,1)S(1)}, u32[]{:S(2)}, u32[]{:S(2)}) collective-permute-start(bf16[128,1024]{1,0:T(8,128)(2,1)S(1)} %get-tuple-element.54), channel_id=1, source_target_pairs={{0,4},{4,0},{8,12},{12,8},{1,5},{5,1},{9,13},{13,9},{2,6},{6,2},{1... | collective-permute-start | bytes 786440 | tf_op jit(solution)/shard_map/ppermute | solution.py:35
  106.9 12.4 %collective-permute-start.21 = (bf16[128,512]{1,0:T(8,128)(2,1)S(1)}, bf16[128,512]{1,0:T(8,128)(2,1)S(1)}, u32[]{:S(2)}, u32[]{:S(2)}) collective-permute-start(bf16[128,512]{1,0:T(8,128)(2,1)S(1)} %get-tuple-element.50), channel_id=1, source_target_pairs={{0,1},{1,2},{2,3},{3,0},{4,5},{5,6},{6,7},{7,4},{8,9},{9,10},{10,1... | collective-permute-start | bytes 393224 | tf_op jit(solution)/shard_map/ppermute | solution.py:31
  110.3 11.0 %collective-permute-start.22 = (bf16[128,512]{1,0:T(8,128)(2,1)S(1)}, bf16[128,512]{1,0:T(8,128)(2,1)S(1)}, u32[]{:S(2)}, u32[]{:S(2)}) collective-permute-start(bf16[128,512]{1,0:T(8,128)(2,1)S(1)} %get-tuple-element.51), channel_id=1, source_target_pairs={{0,3},{1,0},{2,1},{3,2},{4,7},{5,4},{6,5},{7,6},{8,11},{9,8},{10,9... | collective-permute-start | bytes 393224 | tf_op jit(solution)/shard_map/ppermute | solution.py:31
  111.7 16.3 %collective-permute-start.23 = (bf16[128,512]{1,0:T(8,128)(2,1)S(1)}, bf16[128,512]{1,0:T(8,128)(2,1)S(1)}, u32[]{:S(2)}, u32[]{:S(2)}) collective-permute-start(bf16[128,512]{1,0:T(8,128)(2,1)S(1)} %get-tuple-element.52), channel_id=1, source_target_pairs={{0,2},{1,3},{2,0},{3,1},{4,6},{5,7},{6,4},{7,5},{8,10},{9,11},{10,... | collective-permute-start | bytes 393224 | tf_op jit(solution)/shard_map/ppermute | solution.py:31
  122.6 9.3 %collective-permute-start.26 = (bf16[128,512]{1,0:T(8,128)(2,1)S(1)}, bf16[128,512]{1,0:T(8,128)(2,1)S(1)}, u32[]{:S(2)}, u32[]{:S(2)}) collective-permute-start(bf16[128,512]{1,0:T(8,128)(2,1)S(1)} %get-tuple-element.56), channel_id=1, source_target_pairs={{0,1},{1,2},{2,3},{3,0},{4,5},{5,6},{6,7},{7,4},{8,9},{9,10},{10,1... | collective-permute-start | bytes 393224 | tf_op jit(solution)/shard_map/ppermute | solution.py:31
  124.1 13.4 %collective-permute-start.27 = (bf16[128,512]{1,0:T(8,128)(2,1)S(1)}, bf16[128,512]{1,0:T(8,128)(2,1)S(1)}, u32[]{:S(2)}, u32[]{:S(2)}) collective-permute-start(bf16[128,512]{1,0:T(8,128)(2,1)S(1)} %get-tuple-element.57), channel_id=1, source_target_pairs={{0,2},{1,3},{2,0},{3,1},{4,6},{5,7},{6,4},{7,5},{8,10},{9,11},{10,... | collective-permute-start | bytes 393224 | tf_op jit(solution)/shard_map/ppermute | solution.py:31
  126.2 11.3 %collective-permute-start.28 = (bf16[128,512]{1,0:T(8,128)(2,1)S(1)}, bf16[128,512]{1,0:T(8,128)(2,1)S(1)}, u32[]{:S(2)}, u32[]{:S(2)}) collective-permute-start(bf16[128,512]{1,0:T(8,128)(2,1)S(1)} %get-tuple-element.58), channel_id=1, source_target_pairs={{0,3},{1,0},{2,1},{3,2},{4,7},{5,4},{6,5},{7,6},{8,11},{9,8},{10,9... | collective-permute-start | bytes 393224 | tf_op jit(solution)/shard_map/ppermute | solution.py:31
  (5 other events, 4.0 us)

commit v5 on v4

--- a/solution.py
+++ b/solution.py
@@ -711,7 +711,7 @@
     base1 = base_project(table, a1, nears1, own, weights, sent1[0])
 
     gated2, sq2, new_states = ssm(
-        start=HALF, sources=[ssm_states, *along, beside, across], alias=states1, after=[base1]
+        start=HALF, sources=[ssm_states, *along, beside, across], alias=states1, after=[sent1[0]]
     )
     near_sums = trade(sq2, 1)
     z0, r1, r2, r3 = reduce_rest(base1, moved1, [sq2])

time: 140 us -> 142 us (1.014)
    ppermute x15, waiting for transfers between devices: 23.4 us -> 25.8 us  [shift(): lax.ppermute(value, axis, [(i, (i + step) % size) for i in range(size)])]
    ppermute x12, waiting for transfers between devices: 7.95 us -> 6.13 us  [flip(): return lax.ppermute(value, 'x', [(i, i ^ mask) for i in range(4)])]
    ppermute x15, starting transfers between devices: 25.9 us -> 27.3 us  [shift(): lax.ppermute(value, axis, [(i, (i + step) % size) for i in range(size)])]
  transfers between devices with their start and end apart: 29 -> 29, of which waited for: 13 -> 12; matrix products, arithmetic and copies ran while one was open for 0% -> 0% of each run, Pallas kernels for 23% -> 23%
where the time goes in v5:
time: 142 us; the launch traced here: 141 us
  starting transfers between devices  47.1 us (33%)
  Pallas kernels  39.9 us (28%)
  waiting for transfers between devices  32.1 us (23%)
  blocking collectives  14.9 us (10%)
  local copies, waits for them, and re-layouts  5.36 us (4%)
    ppermute x15, starting transfers between devices, shift(): lax.ppermute(value, axis, [(i, (i + step) % size) for i in range(size)])  27.3 us
    ppermute x15, waiting for transfers between devices, shift(): lax.ppermute(value, axis, [(i, (i + step) % size) for i in range(size)])  25.8 us
    psum x1, blocking collectives, local(): sums1 = lax.psum(sq1, 'zh')  14.9 us
    ppermute x12, starting transfers between devices, flip(): return lax.ppermute(value, 'x', [(i, i ^ mask) for i in range(4)])  14.8 us
    pallas_call x2, Pallas kernels, run_ssm(): pl.pallas_call(functools.partial(ssm_kernel, start, len(sources), unused)...  12.7 us
    ppermute x12, waiting for transfers between devices, flip(): return lax.ppermute(value, 'x', [(i, i ^ mask) for i in range(4)])  6.13 us
    unnamed x48, local copies, waits for them, and re-layouts  5.28 us
    ppermute x2, starting transfers between devices, trade(): return lax.ppermute(value, 'zh', [(i, i ^ mask) for i in range(4)])  4.99 us
  transfers between devices with their start and end apart: 29, of which 12 were waited for; matrix products, arithmetic and copies ran while one was open for 0% of the time, Pallas kernels for 23%

profile of v5, /device:TPU:12, one launch (start us, length us, event | category | flops | bytes accessed | tf_op | source)
XLA Modules:
  0.0 140.7 jit_solution(17127780934479958233)
XLA Ops:
  2.0 0.9 route.1
  2.9 1.2 copy-done
  4.2 1.9 %leave.1.refs_1_.refs_0_ = bf16[4,8,64,128]{3,2,1,0:T(8,128)(2,1)} custom-call(s32[128]{0:T(128)S(1)} %bitcast.16, bf16[8,8,64,128]{3,2,1,0:T(8,128)(2,1)S(1)} %copy-done), custom_call_target="tpu_custom_call" | custom-call | tf_op jit(solution)/shard_map/leave/pallas_call | solution.py:605
  6.7 2.6 %collective-permute-start.3 = (bf16[4,8,64,128]{3,2,1,0:T(8,128)(2,1)}, bf16[4,8,64,128]{3,2,1,0:T(8,128)(2,1)S(1)}, u32[]{:S(2)}, u32[]{:S(2)}) collective-permute-start(bf16[4,8,64,128]{3,2,1,0:T(8,128)(2,1)} %leave.1.refs_1_.refs_0_), channel_id=1, source_target_pairs={{0,128},{64,192},{128,0},{192,64},{1,129},{65,193},{129,1},{193,65... | collective-permute-start | bytes 1572872 | tf_op jit(solution)/shard_map/ppermute | solution.py:31
  9.3 1.9 %collective-permute-start.2 = (bf16[4,8,64,128]{3,2,1,0:T(8,128)(2,1)}, bf16[4,8,64,128]{3,2,1,0:T(8,128)(2,1)S(1)}, u32[]{:S(2)}, u32[]{:S(2)}) collective-permute-start(bf16[4,8,64,128]{3,2,1,0:T(8,128)(2,1)} %leave.1.refs_1_.refs_0_), channel_id=1, source_target_pairs={{0,64},{64,128},{128,192},{192,0},{1,65},{65,129},{129,193},{193,1... | collective-permute-start | bytes 1572872 | tf_op jit(solution)/shard_map/ppermute | solution.py:31
  11.2 3.6 %slices.2 = (bf16[512,1024]{1,0:T(8,128)(2,1)}, bf16[512,1024]{1,0:T(8,128)(2,1)}) custom-call(s32[128]{0:T(128)} %bitcast.17, bf16[512,8192]{1,0:T(8,128)(2,1)} %refs_0_.6, bf16[4,8,64,128]{3,2,1,0:T(8,128)(2,1)} %leave.1.refs_1_.refs_0_), custom_call_target="tpu_custom_call" | custom-call | tf_op jit(solution)/shard_map/slices/pallas_call | solution.py:461
  15.4 1.1 collective-permute-start
  16.7 1.2 copy-done.9
  18.5 6.2 %ssm.2 = (f32[4,64,512]{2,1,0:T(8,128)S(1)}, f32[4,1,64]{2,1,0:T(1,128)S(1)}, bf16[8,8,64,128]{3,2,1,0:T(8,128)(2,1)}) custom-call(s32[128]{0:T(128)S(1)} %bitcast.18, bf16[8,64,512]{2,1,0:T(8,128)(2,1)S(1)} %copy-done.2, bf16[8,64,512]{2,1,0:T(8,128)(2,1)S(1)} %copy-done.3, bf16[8,256,128]{2,1,0:T(8,128)(2,1)S(1)} %bitcast.12, ...), custom_call_target="tpu_custom_call" | custom-call | tf_op jit(solution)/shard_map/ssm/pallas_call | solution.py:276
  25.5 14.9 %psum.7.refs_4_.refs_0_ = f32[4,1,64]{2,1,0:T(1,128)S(1)} all-reduce(f32[4,1,64]{2,1,0:T(1,128)S(1)} %get-tuple-element.33), channel_id=1, replica_groups=mesh['y'=4,'zl'=2,'c'=2,'x'=4,'zh'=4] {'zh'}, use_global_device_ids=true, to_apply=%region_0.0 | all-reduce | flops 256 | bytes 2048 | tf_op jit(solution)/shard_map/psum | solution.py:698
  40.4 2.1 %pick.2.after = bf16[8,8,64,128]{3,2,1,0:T(8,128)(2,1)S(1)} custom-call(s32[128]{0:T(128)S(1)} %bitcast.19, bf16[4,8,64,128]{3,2,1,0:T(8,128)(2,1)} %leave.1.refs_1_.refs_0_, bf16[4,8,64,128]{3,2,1,0:T(8,128)(2,1)S(1)} %collective-permute-done.2.refs_1_.refs_2_, bf16[4,8,64,128]{3,2,1,0:T(8,128)(2,1)S(1)} %collective-permute-done.3.refs_2_.refs_3_, ...), custom_call_target="tpu_custom_call" | custom-call | tf_op jit(solution)/shard_map/pick/pallas_call | solution.py:636
  42.7 1.7 %join.1.refs_2_.value = bf16[2,512,1024]{2,1,0:T(8,128)(2,1)S(1)} custom-call(bf16[512,1024]{1,0:T(8,128)(2,1)} %collective-permute-done.first, bf16[512,1024]{1,0:T(8,128)(2,1)} %collective-permute-done.1.second, f32[8,128]{1,0:T(8,128)S(1)} %wait.1.after), custom_call_target="tpu_custom_call" | custom-call | tf_op jit(solution)/shard_map/join/pallas_call | solution.py:521
  45.3 1.9 %pick.3.refs_1_.after = bf16[4,8,64,128]{3,2,1,0:T(8,128)(2,1)S(1)} custom-call(s32[128]{0:T(128)S(1)} %bitcast.20, bf16[4,8,64,128]{3,2,1,0:T(8,128)(2,1)} %leave.1.refs_1_.refs_0_, bf16[4,8,64,128]{3,2,1,0:T(8,128)(2,1)S(1)} %collective-permute-done.2.refs_1_.refs_2_, bf16[4,8,64,128]{3,2,1,0:T(8,128)(2,1)S(1)} %collective-permute-done.3.refs_2_.refs_3_, ...), custom_call_target="tpu_custom_call" | custom-call | tf_op jit(solution)/shard_map/pick/pallas_call | solution.py:636
  47.7 2.1 %collective-permute-start.6 = (bf16[256,512]{1,0:T(8,128)(2,1)S(1)}, bf16[256,512]{1,0:T(8,128)(2,1)S(1)}, u32[]{:S(2)}, u32[]{:S(2)}) collective-permute-start(bf16[256,512]{1,0:T(8,128)(2,1)S(1)} %normalise.2.refs_5_.a), channel_id=1, source_target_pairs={{0,12},{4,8},{8,4},{12,0},{1,13},{5,9},{9,5},{13,1},{2,14},{6,10},... | collective-permute-start | bytes 786440 | tf_op jit(solution)/shard_map/ppermute | solution.py:35
  50.6 0.9 collective-permute-start.11
  51.5 1.0 slices.3
  52.5 4.0 %collective-permute-done.6.near1 = bf16[256,512]{1,0:T(8,128)(2,1)S(1)} collective-permute-done((bf16[256,512]{1,0:T(8,128)(2,1)S(1)}, bf16[256,512]{1,0:T(8,128)(2,1)S(1)}, u32[]{:S(2)}, u32[]{:S(2)}) %collective-permute-start.6) | collective-permute-done | bytes 262176 | tf_op jit(solution)/shard_map/ppermute | solution.py:35
  56.5 1.5 %collective-permute-done.5.near0 = bf16[256,512]{1,0:T(8,128)(2,1)S(1)} collective-permute-done((bf16[256,512]{1,0:T(8,128)(2,1)S(1)}, bf16[256,512]{1,0:T(8,128)(2,1)S(1)}, u32[]{:S(2)}, u32[]{:S(2)}) %collective-permute-start.5) | collective-permute-done | bytes 262176 | tf_op jit(solution)/shard_map/ppermute | solution.py:35
  58.0 2.0 %project.2 = (bf16[256,1024]{1,0:T(8,128)(2,1)S(1)}, bf16[256,1024]{1,0:T(8,128)(2,1)S(1)}) custom-call(s32[128]{0:T(128)S(1)} %bitcast.22, bf16[256,512]{1,0:T(8,128)(2,1)S(1)} %normalise.2.refs_5_.a, bf16[256,512]{1,0:T(8,128)(2,1)S(1)} %collective-permute-done.5.near0, bf16[256,512]{1,0:T(8,128)(2,1)S(1)} %collective-permute-done.6.near1, ...), custom_call_target="tpu_custom_call" | custom-call | tf_op jit(solution)/shard_map/project/pallas_call | solution.py:350
  60.0 0.9 collective-permute-start.10
  60.9 0.9 collective-permute-start.9
  61.8 2.4 %collective-permute-done.11.refs_6_ = bf16[4,8,64,128]{3,2,1,0:T(8,128)(2,1)S(1)} collective-permute-done((bf16[4,8,64,128]{3,2,1,0:T(8,128)(2,1)S(1)}, bf16[4,8,64,128]{3,2,1,0:T(8,128)(2,1)S(1)}, u32[]{:S(2)}, u32[]{:S(2)}) %collective-permute-start.11) | collective-permute-done | bytes 524320 | tf_op jit(solution)/shard_map/ppermute | solution.py:31
  64.1 6.4 %ssm.3 = (f32[4,64,512]{2,1,0:T(8,128)S(1)}, f32[4,1,64]{2,1,0:T(1,128)S(1)}, bf16[8,8,64,128]{3,2,1,0:T(8,128)(2,1)}) custom-call(s32[128]{0:T(128)S(1)} %bitcast.23, bf16[8,64,512]{2,1,0:T(8,128)(2,1)S(1)} %copy-done.2, bf16[8,64,512]{2,1,0:T(8,128)(2,1)S(1)} %copy-done.4, bf16[8,256,128]{2,1,0:T(8,128)(2,1)S(1)} %bitcast.13, ...), custom_call_target="tpu_custom_call", output_to_operand_aliasing={{2}: (17, {})} | custom-call | tf_op jit(solution)/shard_map/ssm/pallas_call | solution.py:276
  71.3 2.0 %base.2 = f32[256,2048]{1,0:T(8,128)S(1)} custom-call(s32[128]{0:T(128)S(1)} %bitcast.24, bf16[256,512]{1,0:T(8,128)(2,1)S(1)} %normalise.2.refs_5_.a, bf16[256,512]{1,0:T(8,128)(2,1)S(1)} %collective-permute-done.5.near0, bf16[256,512]{1,0:T(8,128)(2,1)S(1)} %collective-permute-done.6.near1, bf16[512,2048]{1,0:T(8,128)(2,1)S(1)} %get-tuple-element.35.w, ...), custom_call_target="tpu_custom_call" | custom-call | tf_op jit(solution)/shard_map/base/pallas_call | solution.py:381
  73.5 1.7 %combine.3 = (f32[256,512]{1,0:T(8,128)S(1)}, bf16[256,512]{1,0:T(8,128)(2,1)S(1)}, bf16[256,512]{1,0:T(8,128)(2,1)S(1)}, bf16[256,512]{1,0:T(8,128)(2,1)S(1)}) custom-call(s32[128]{0:T(128)S(1)} %bitcast.25, f32[256,2048]{1,0:T(8,128)S(1)} %base.2, bf16[256,1024]{1,0:T(8,128)(2,1)S(1)} %collective-permute-done.9.e0, ...), custom_call_target="tpu_custom_call" | custom-call | tf_op jit(solution)/shard_map/combine/pallas_call | solution.py:417
  75.3 4.3 %collective-permute-start.16 = (f32[4,1,64]{2,1,0:T(1,128)S(1)}, f32[4,1,64]{2,1,0:T(1,128)S(1)}, u32[]{:S(2)}, u32[]{:S(2)}) collective-permute-start(f32[4,1,64]{2,1,0:T(1,128)S(1)} %add.3.refs_0_), channel_id=1, source_target_pairs={{0,3},{1,2},{2,1},{3,0},{4,7},{5,6},{6,5},{7,4},{8,11},{9,10},{10,... | collective-permute-start | bytes 3080 | tf_op jit(solution)/shard_map/ppermute | solution.py:145
  79.6 1.5 %collective-permute-start.12 = (bf16[256,512]{1,0:T(8,128)(2,1)S(1)}, bf16[256,512]{1,0:T(8,128)(2,1)S(1)}, u32[]{:S(2)}, u32[]{:S(2)}) collective-permute-start(bf16[256,512]{1,0:T(8,128)(2,1)S(1)} %get-tuple-element.43), channel_id=1, source_target_pairs={{0,1},{1,2},{2,3},{3,0},{4,5},{5,6},{6,7},{7,4},{8,9},{9,10},{10,1... | collective-permute-start | bytes 786440 | tf_op jit(solution)/shard_map/ppermute | solution.py:31
  81.1 2.6 %collective-permute-start.13 = (bf16[256,512]{1,0:T(8,128)(2,1)S(1)}, bf16[256,512]{1,0:T(8,128)(2,1)S(1)}, u32[]{:S(2)}, u32[]{:S(2)}) collective-permute-start(bf16[256,512]{1,0:T(8,128)(2,1)S(1)} %get-tuple-element.44), channel_id=1, source_target_pairs={{0,3},{1,0},{2,1},{3,2},{4,7},{5,4},{6,5},{7,6},{8,11},{9,8},{10,9... | collective-permute-start | bytes 786440 | tf_op jit(solution)/shard_map/ppermute | solution.py:31
  83.9 1.0 collective-permute-start.18
  84.8 2.0 %collective-permute-start.17 = (bf16[256,512]{1,0:T(8,128)(2,1)S(1)}, bf16[256,512]{1,0:T(8,128)(2,1)S(1)}, u32[]{:S(2)}, u32[]{:S(2)}) collective-permute-start(bf16[256,512]{1,0:T(8,128)(2,1)S(1)} %normalise.3.a), channel_id=1, source_target_pairs={{0,4},{4,0},{8,12},{12,8},{1,5},{5,1},{9,13},{13,9},{2,6},{6,2},{1... | collective-permute-start | bytes 786440 | tf_op jit(solution)/shard_map/ppermute | solution.py:35
  86.8 6.2 %collective-permute-done.12.refs_1_ = bf16[256,512]{1,0:T(8,128)(2,1)S(1)} collective-permute-done((bf16[256,512]{1,0:T(8,128)(2,1)S(1)}, bf16[256,512]{1,0:T(8,128)(2,1)S(1)}, u32[]{:S(2)}, u32[]{:S(2)}) %collective-permute-start.12) | collective-permute-done | bytes 262176 | tf_op jit(solution)/shard_map/ppermute | solution.py:31
  94.0 2.0 %project.3 = (bf16[128,1024]{1,0:T(8,128)(2,1)S(1)}, bf16[128,1024]{1,0:T(8,128)(2,1)S(1)}, bf16[128,1024]{1,0:T(8,128)(2,1)S(1)}, bf16[128,1024]{1,0:T(8,128)(2,1)S(1)}) custom-call(s32[128]{0:T(128)S(1)} %bitcast.26, bf16[256,512]{1,0:T(8,128)(2,1)S(1)} %normalise.3.a, bf16[256,512]{1,0:T(8,128)(2,1)S(1)} %collective-permute-done.17.near0, ...), custom_call_target="tpu_custom_call" | custom-call | tf_op jit(solution)/shard_map/project/pallas_call | solution.py:350
  96.0 1.0 collective-permute-start.20
  97.0 1.1 collective-permute-start.19
  98.1 2.3 %collective-permute-start.14 = (bf16[256,512]{1,0:T(8,128)(2,1)S(1)}, bf16[256,512]{1,0:T(8,128)(2,1)S(1)}, u32[]{:S(2)}, u32[]{:S(2)}) collective-permute-start(bf16[256,512]{1,0:T(8,128)(2,1)S(1)} %get-tuple-element.45), channel_id=1, source_target_pairs={{0,2},{1,3},{2,0},{3,1},{4,6},{5,7},{6,4},{7,5},{8,10},{9,11},{10,... | collective-permute-start | bytes 786440 | tf_op jit(solution)/shard_map/ppermute | solution.py:31
  100.4 0.9 collective-permute-start.24
  101.3 2.2 %collective-permute-start.25 = (bf16[128,1024]{1,0:T(8,128)(2,1)S(1)}, bf16[128,1024]{1,0:T(8,128)(2,1)S(1)}, u32[]{:S(2)}, u32[]{:S(2)}) collective-permute-start(bf16[128,1024]{1,0:T(8,128)(2,1)S(1)} %get-tuple-element.54), channel_id=1, source_target_pairs={{0,4},{4,0},{8,12},{12,8},{1,5},{5,1},{9,13},{13,9},{2,6},{6,2},{1... | collective-permute-start | bytes 786440 | tf_op jit(solution)/shard_map/ppermute | solution.py:35
  103.6 2.2 %base.3.refs_0_ = f32[256,2048]{1,0:T(8,128)S(1)} custom-call(s32[128]{0:T(128)S(1)} %bitcast.27, bf16[256,512]{1,0:T(8,128)(2,1)S(1)} %normalise.3.a, bf16[256,512]{1,0:T(8,128)(2,1)S(1)} %collective-permute-done.17.near0, bf16[256,512]{1,0:T(8,128)(2,1)S(1)} %collective-permute-done.18.near1, bf16[512,2048]{1,0:T(8,128)(2,1)S(1)} %get-tuple-element.35.w, ...), custom_call_target="tpu_custom_call" | custom-call | tf_op jit(solution)/shard_map/base/pallas_call | solution.py:381
  106.2 1.2 combine.4
  107.5 3.4 %collective-permute-start.21 = (bf16[128,512]{1,0:T(8,128)(2,1)S(1)}, bf16[128,512]{1,0:T(8,128)(2,1)S(1)}, u32[]{:S(2)}, u32[]{:S(2)}) collective-permute-start(bf16[128,512]{1,0:T(8,128)(2,1)S(1)} %get-tuple-element.50), channel_id=1, source_target_pairs={{0,1},{1,2},{2,3},{3,0},{4,5},{5,6},{6,7},{7,4},{8,9},{9,10},{10,1... | collective-permute-start | bytes 393224 | tf_op jit(solution)/shard_map/ppermute | solution.py:31
  111.8 3.4 %collective-permute-start.23 = (bf16[128,512]{1,0:T(8,128)(2,1)S(1)}, bf16[128,512]{1,0:T(8,128)(2,1)S(1)}, u32[]{:S(2)}, u32[]{:S(2)}) collective-permute-start(bf16[128,512]{1,0:T(8,128)(2,1)S(1)} %get-tuple-element.52), channel_id=1, source_target_pairs={{0,2},{1,3},{2,0},{3,1},{4,6},{5,7},{6,4},{7,5},{8,10},{9,11},{10,... | collective-permute-start | bytes 393224 | tf_op jit(solution)/shard_map/ppermute | solution.py:31
  115.1 5.2 %collective-permute-done.21.refs_1_ = bf16[128,512]{1,0:T(8,128)(2,1)S(1)} collective-permute-done((bf16[128,512]{1,0:T(8,128)(2,1)S(1)}, bf16[128,512]{1,0:T(8,128)(2,1)S(1)}, u32[]{:S(2)}, u32[]{:S(2)}) %collective-permute-start.21) | collective-permute-done | bytes 131104 | tf_op jit(solution)/shard_map/ppermute | solution.py:31
  120.4 1.2 combine.5
  121.6 2.8 %collective-permute-start.26 = (bf16[128,512]{1,0:T(8,128)(2,1)S(1)}, bf16[128,512]{1,0:T(8,128)(2,1)S(1)}, u32[]{:S(2)}, u32[]{:S(2)}) collective-permute-start(bf16[128,512]{1,0:T(8,128)(2,1)S(1)} %get-tuple-element.56), channel_id=1, source_target_pairs={{0,1},{1,2},{2,3},{3,0},{4,5},{5,6},{6,7},{7,4},{8,9},{9,10},{10,1... | collective-permute-start | bytes 393224 | tf_op jit(solution)/shard_map/ppermute | solution.py:31
  124.4 4.2 %collective-permute-start.27 = (bf16[128,512]{1,0:T(8,128)(2,1)S(1)}, bf16[128,512]{1,0:T(8,128)(2,1)S(1)}, u32[]{:S(2)}, u32[]{:S(2)}) collective-permute-start(bf16[128,512]{1,0:T(8,128)(2,1)S(1)} %get-tuple-element.57), channel_id=1, source_target_pairs={{0,2},{1,3},{2,0},{3,1},{4,6},{5,7},{6,4},{7,5},{8,10},{9,11},{10,... | collective-permute-start | bytes 393224 | tf_op jit(solution)/shard_map/ppermute | solution.py:31
  128.6 4.8 %collective-permute-done.26.refs_3_ = bf16[128,512]{1,0:T(8,128)(2,1)S(1)} collective-permute-done((bf16[128,512]{1,0:T(8,128)(2,1)S(1)}, bf16[128,512]{1,0:T(8,128)(2,1)S(1)}, u32[]{:S(2)}, u32[]{:S(2)}) %collective-permute-start.26) | collective-permute-done | bytes 131104 | tf_op jit(solution)/shard_map/ppermute | solution.py:31
  133.4 5.7 %collective-permute-done.27.refs_4_ = bf16[128,512]{1,0:T(8,128)(2,1)S(1)} collective-permute-done((bf16[128,512]{1,0:T(8,128)(2,1)S(1)}, bf16[128,512]{1,0:T(8,128)(2,1)S(1)}, u32[]{:S(2)}, u32[]{:S(2)}) %collective-permute-start.27) | collective-permute-done | bytes 131104 | tf_op jit(solution)/shard_map/ppermute | solution.py:31
  139.1 1.4 finish.1
  (86 shorter events, 9.8 us)
Async XLA Ops:
  2.9 8.3 %copy-start.13 = (s32[1,128]{1,0:T(1,128)}, s32[1,128]{1,0:T(1,128)S(1)}, u32[]{:S(2)}) copy-start(s32[1,128]{1,0:T(1,128)S(1)} %route.1) | copy-start | bytes 1540
  2.9 1.2 copy-start
  6.1 10.5 %copy-start.1 = (bf16[8,8,64,128]{3,2,1,0:T(8,128)(2,1)S(1)}, bf16[8,8,64,128]{3,2,1,0:T(8,128)(2,1)}, u32[]{:S(2)}) copy-start(bf16[8,8,64,128]{3,2,1,0:T(8,128)(2,1)} %refs_0_.7) | copy-start | bytes 3145732
  6.1 10.5 %copy-start.2 = (bf16[8,64,512]{2,1,0:T(8,128)(2,1)S(1)}, bf16[8,64,512]{2,1,0:T(8,128)(2,1)}, u32[]{:S(2)}) copy-start(bf16[8,64,512]{2,1,0:T(8,128)(2,1)} %x_ref.3) | copy-start | bytes 1572868
  6.1 10.5 %copy-start.3 = (bf16[8,64,512]{2,1,0:T(8,128)(2,1)S(1)}, bf16[8,64,512]{2,1,0:T(8,128)(2,1)}, u32[]{:S(2)}) copy-start(bf16[8,64,512]{2,1,0:T(8,128)(2,1)} %g_ref.3) | copy-start | bytes 1572868
  6.1 10.5 %copy-start.5 = (bf16[8,64,4,128]{3,2,1,0:T(4,128)(2,1)S(1)}, bf16[8,64,4,128]{3,2,1,0:T(4,128)(2,1)}, u32[]{:S(2)}) copy-start(bf16[8,64,4,128]{3,2,1,0:T(4,128)(2,1)} %param.15) | copy-start | bytes 1572868
  6.1 10.5 %copy-start.7 = (bf16[8,64,4,128]{3,2,1,0:T(4,128)(2,1)S(1)}, bf16[8,64,4,128]{3,2,1,0:T(4,128)(2,1)}, u32[]{:S(2)}) copy-start(bf16[8,64,4,128]{3,2,1,0:T(4,128)(2,1)} %param.16) | copy-start | bytes 1572868
  6.1 10.5 %copy-start.12 = (f32[8,8,64]{2,1,0:T(8,128)S(1)}, f32[8,8,64]{2,1,0:T(8,128)}, u32[]{:S(2)}) copy-start(f32[8,8,64]{2,1,0:T(8,128)} %dt_ref.3) | copy-start | bytes 49156
  6.2 10.5 %copy-start.17 = (f32[8]{0:T(128)S(1)}, f32[8]{0:T(128)}, u32[]{:S(2)}) copy-start(f32[8]{0:T(128)} %bias.3) | copy-start | bytes 100
  6.2 10.5 %copy-start.18 = (f32[8]{0:T(128)S(1)}, f32[8]{0:T(128)}, u32[]{:S(2)}) copy-start(f32[8]{0:T(128)} %rate.3) | copy-start | bytes 100
  6.2 10.5 %copy-start.19 = (f32[8]{0:T(128)S(1)}, f32[8]{0:T(128)}, u32[]{:S(2)}) copy-start(f32[8]{0:T(128)} %skip.3) | copy-start | bytes 100
  6.2 34.2 %collective-permute-start.4 = (bf16[4,8,64,128]{3,2,1,0:T(8,128)(2,1)}, bf16[4,8,64,128]{3,2,1,0:T(8,128)(2,1)S(1)}, u32[]{:S(2)}, u32[]{:S(2)}) collective-permute-start(bf16[4,8,64,128]{3,2,1,0:T(8,128)(2,1)} %leave.1.refs_1_.refs_0_), channel_id=1, source_target_pairs={{0,192},{64,0},{128,64},{192,128},{1,193},{65,1},{129,65},{193,129... | collective-permute-start | bytes 1572872 | tf_op jit(solution)/shard_map/ppermute | solution.py:31
  6.7 33.7 %collective-permute-start.3 = (bf16[4,8,64,128]{3,2,1,0:T(8,128)(2,1)}, bf16[4,8,64,128]{3,2,1,0:T(8,128)(2,1)S(1)}, u32[]{:S(2)}, u32[]{:S(2)}) collective-permute-start(bf16[4,8,64,128]{3,2,1,0:T(8,128)(2,1)} %leave.1.refs_1_.refs_0_), channel_id=1, source_target_pairs={{0,128},{64,192},{128,0},{192,64},{1,129},{65,193},{129,1},{193,65... | collective-permute-start | bytes 1572872 | tf_op jit(solution)/shard_map/ppermute | solution.py:31
  9.3 31.1 %collective-permute-start.2 = (bf16[4,8,64,128]{3,2,1,0:T(8,128)(2,1)}, bf16[4,8,64,128]{3,2,1,0:T(8,128)(2,1)S(1)}, u32[]{:S(2)}, u32[]{:S(2)}) collective-permute-start(bf16[4,8,64,128]{3,2,1,0:T(8,128)(2,1)} %leave.1.refs_1_.refs_0_), channel_id=1, source_target_pairs={{0,64},{64,128},{128,192},{192,0},{1,65},{65,129},{129,193},{193,1... | collective-permute-start | bytes 1572872 | tf_op jit(solution)/shard_map/ppermute | solution.py:31
  14.8 27.9 %collective-permute-start.1 = (bf16[512,1024]{1,0:T(8,128)(2,1)}, bf16[512,1024]{1,0:T(8,128)(2,1)}, u32[]{:S(2)}, u32[]{:S(2)}) collective-permute-start(bf16[512,1024]{1,0:T(8,128)(2,1)} %get-tuple-element.34), channel_id=1, source_target_pairs={{0,12},{4,8},{8,4},{12,0},{1,13},{5,9},{9,5},{13,1},{2,14},{6,10},... | collective-permute-start | bytes 3145736 | tf_op jit(solution)/shard_map/ppermute | solution.py:35
  15.4 27.3 %collective-permute-start = (bf16[512,1024]{1,0:T(8,128)(2,1)}, bf16[512,1024]{1,0:T(8,128)(2,1)}, u32[]{:S(2)}, u32[]{:S(2)}) collective-permute-start(bf16[512,1024]{1,0:T(8,128)(2,1)} %get-tuple-element.31.refs_1_), channel_id=1, source_target_pairs={{0,4},{4,0},{8,12},{12,8},{1,5},{5,1},{9,13},{13,9},{2,6},{6,2},{1... | collective-permute-start | bytes 3145736 | tf_op jit(solution)/shard_map/ppermute | solution.py:35
  18.5 22.0 %copy-start.15 = (s32[1,128]{1,0:T(1,128)S(1)}, s32[1,128]{1,0:T(1,128)}, u32[]{:S(2)}) copy-start(s32[1,128]{1,0:T(1,128)} %copy-done.13) | copy-start | bytes 1540
  42.6 2.7 %collective-permute-start.7 = (bf16[8,8,64,128]{3,2,1,0:T(8,128)(2,1)S(1)}, bf16[8,8,64,128]{3,2,1,0:T(8,128)(2,1)S(1)}, u32[]{:S(2)}, u32[]{:S(2)}) collective-permute-start(bf16[8,8,64,128]{3,2,1,0:T(8,128)(2,1)S(1)} %pick.2.after), channel_id=1, source_target_pairs={{0,16},{16,0},{1,17},{17,1},{2,18},{18,2},{3,19},{19,3},{4,20},{20... | collective-permute-start | bytes 3145736 | tf_op jit(solution)/shard_map/ppermute | solution.py:31
  42.7 1.8 %copy-start.11 = (f32[4,64,512]{2,1,0:T(8,128)S(1)}, f32[4,64,512]{2,1,0:T(8,128)}, u32[]{:S(2)}) copy-start(f32[4,64,512]{2,1,0:T(8,128)} %copy-done.10) | copy-start | bytes 1572868
  42.7 1.8 %copy-start.16 = (f32[512]{0:T(512)S(1)}, f32[512]{0:T(512)}, u32[]{:S(2)}) copy-start(f32[512]{0:T(512)} %param.21) | copy-start | bytes 6148
  42.7 8.8 %slice-start = ((s8[8388608]{0:T(1024)(128)(4,1)}), s8[4194304]{0:T(1024)(128)(4,1)S(1)}, s32[]{:S(2)}) async-start(s8[8388608]{0:T(1024)(128)(4,1)} %bitcast.10), calls=%async_computation | async-start | bytes 8388608
  44.6 6.9 %slice-start.1 = ((s8[8388608]{0:T(1024)(128)(4,1)}), s8[4194304]{0:T(1024)(128)(4,1)S(1)}, s32[]{:S(2)}) async-start(s8[8388608]{0:T(1024)(128)(4,1)} %bitcast.10), calls=%async_computation.1 | async-start | bytes 8388608
  47.3 10.7 %collective-permute-start.8 = (bf16[2,512,1024]{2,1,0:T(8,128)(2,1)S(1)}, bf16[2,512,1024]{2,1,0:T(8,128)(2,1)S(1)}, u32[]{:S(2)}, u32[]{:S(2)}) collective-permute-start(bf16[2,512,1024]{2,1,0:T(8,128)(2,1)S(1)} %hold.1.got), channel_id=1, source_target_pairs={{0,16},{16,0},{1,17},{17,1},{2,18},{18,2},{3,19},{19,3},{4,20},{20... | collective-permute-start | bytes 6291464 | tf_op jit(solution)/shard_map/ppermute | solution.py:31
  47.7 8.8 %collective-permute-start.6 = (bf16[256,512]{1,0:T(8,128)(2,1)S(1)}, bf16[256,512]{1,0:T(8,128)(2,1)S(1)}, u32[]{:S(2)}, u32[]{:S(2)}) collective-permute-start(bf16[256,512]{1,0:T(8,128)(2,1)S(1)} %normalise.2.refs_5_.a), channel_id=1, source_target_pairs={{0,12},{4,8},{8,4},{12,0},{1,13},{5,9},{9,5},{13,1},{2,14},{6,10},... | collective-permute-start | bytes 786440 | tf_op jit(solution)/shard_map/ppermute | solution.py:35
  49.8 8.1 %collective-permute-start.5 = (bf16[256,512]{1,0:T(8,128)(2,1)S(1)}, bf16[256,512]{1,0:T(8,128)(2,1)S(1)}, u32[]{:S(2)}, u32[]{:S(2)}) collective-permute-start(bf16[256,512]{1,0:T(8,128)(2,1)S(1)} %normalise.2.refs_5_.a), channel_id=1, source_target_pairs={{0,4},{4,0},{8,12},{12,8},{1,5},{5,1},{9,13},{13,9},{2,6},{6,2},{1... | collective-permute-start | bytes 786440 | tf_op jit(solution)/shard_map/ppermute | solution.py:35
  50.6 13.5 %collective-permute-start.11 = (bf16[4,8,64,128]{3,2,1,0:T(8,128)(2,1)S(1)}, bf16[4,8,64,128]{3,2,1,0:T(8,128)(2,1)S(1)}, u32[]{:S(2)}, u32[]{:S(2)}) collective-permute-start(bf16[4,8,64,128]{3,2,1,0:T(8,128)(2,1)S(1)} %pick.3.refs_1_.after), channel_id=1, source_target_pairs={{0,32},{32,0},{1,33},{33,1},{2,34},{34,2},{3,35},{35,3},{4,36},{36... | collective-permute-start | bytes 1572872 | tf_op jit(solution)/shard_map/ppermute | solution.py:31
  58.0 6.2 %copy-start.4 = (bf16[8,64,512]{2,1,0:T(8,128)(2,1)S(1)}, bf16[8,64,512]{2,1,0:T(8,128)(2,1)}, u32[]{:S(2)}) copy-start(bf16[8,64,512]{2,1,0:T(8,128)(2,1)} %g_ref.3) | copy-start | bytes 1572868
  58.0 6.2 %copy-start.6 = (bf16[8,64,4,128]{3,2,1,0:T(4,128)(2,1)S(1)}, bf16[8,64,4,128]{3,2,1,0:T(4,128)(2,1)}, u32[]{:S(2)}) copy-start(bf16[8,64,4,128]{3,2,1,0:T(4,128)(2,1)} %param.15) | copy-start | bytes 1572868
  58.0 6.2 %copy-start.8 = (bf16[8,64,4,128]{3,2,1,0:T(4,128)(2,1)S(1)}, bf16[8,64,4,128]{3,2,1,0:T(4,128)(2,1)}, u32[]{:S(2)}) copy-start(bf16[8,64,4,128]{3,2,1,0:T(4,128)(2,1)} %param.16) | copy-start | bytes 1572868
  60.0 13.3 %collective-permute-start.10 = (bf16[256,1024]{1,0:T(8,128)(2,1)S(1)}, bf16[256,1024]{1,0:T(8,128)(2,1)S(1)}, u32[]{:S(2)}, u32[]{:S(2)}) collective-permute-start(bf16[256,1024]{1,0:T(8,128)(2,1)S(1)} %get-tuple-element.39), channel_id=1, source_target_pairs={{0,4},{4,0},{8,12},{12,8},{1,5},{5,1},{9,13},{13,9},{2,6},{6,2},{1... | collective-permute-start | bytes 1572872 | tf_op jit(solution)/shard_map/ppermute | solution.py:35
  60.9 12.6 %collective-permute-start.9 = (bf16[256,1024]{1,0:T(8,128)(2,1)S(1)}, bf16[256,1024]{1,0:T(8,128)(2,1)S(1)}, u32[]{:S(2)}, u32[]{:S(2)}) collective-permute-start(bf16[256,1024]{1,0:T(8,128)(2,1)S(1)} %get-tuple-element.38.after.refs_7_), channel_id=1, source_target_pairs={{0,12},{4,8},{8,4},{12,0},{1,13},{5,9},{9,5},{13,1},{2,14},{6,10},... | collective-permute-start | bytes 1572872 | tf_op jit(solution)/shard_map/ppermute | solution.py:35
  70.6 4.8 %collective-permute-start.15 = (f32[4,1,64]{2,1,0:T(1,128)S(1)}, f32[4,1,64]{2,1,0:T(1,128)S(1)}, u32[]{:S(2)}, u32[]{:S(2)}) collective-permute-start(f32[4,1,64]{2,1,0:T(1,128)S(1)} %get-tuple-element.41.refs_0_.first), channel_id=1, source_target_pairs={{0,1},{1,0},{2,3},{3,2},{4,5},{5,4},{6,7},{7,6},{8,9},{9,8},{10,11... | collective-permute-start | bytes 3080 | tf_op jit(solution)/shard_map/ppermute | solution.py:145
  75.3 8.4 %collective-permute-start.16 = (f32[4,1,64]{2,1,0:T(1,128)S(1)}, f32[4,1,64]{2,1,0:T(1,128)S(1)}, u32[]{:S(2)}, u32[]{:S(2)}) collective-permute-start(f32[4,1,64]{2,1,0:T(1,128)S(1)} %add.3.refs_0_), channel_id=1, source_target_pairs={{0,3},{1,2},{2,1},{3,0},{4,7},{5,6},{6,5},{7,4},{8,11},{9,10},{10,... | collective-permute-start | bytes 3080 | tf_op jit(solution)/shard_map/ppermute | solution.py:145
  79.6 13.4 %collective-permute-start.12 = (bf16[256,512]{1,0:T(8,128)(2,1)S(1)}, bf16[256,512]{1,0:T(8,128)(2,1)S(1)}, u32[]{:S(2)}, u32[]{:S(2)}) collective-permute-start(bf16[256,512]{1,0:T(8,128)(2,1)S(1)} %get-tuple-element.43), channel_id=1, source_target_pairs={{0,1},{1,2},{2,3},{3,0},{4,5},{5,6},{6,7},{7,4},{8,9},{9,10},{10,1... | collective-permute-start | bytes 786440 | tf_op jit(solution)/shard_map/ppermute | solution.py:31
  81.1 12.8 %collective-permute-start.13 = (bf16[256,512]{1,0:T(8,128)(2,1)S(1)}, bf16[256,512]{1,0:T(8,128)(2,1)S(1)}, u32[]{:S(2)}, u32[]{:S(2)}) collective-permute-start(bf16[256,512]{1,0:T(8,128)(2,1)S(1)} %get-tuple-element.44), channel_id=1, source_target_pairs={{0,3},{1,0},{2,1},{3,2},{4,7},{5,4},{6,5},{7,6},{8,11},{9,8},{10,9... | collective-permute-start | bytes 786440 | tf_op jit(solution)/shard_map/ppermute | solution.py:31
  83.9 10.1 %collective-permute-start.18 = (bf16[256,512]{1,0:T(8,128)(2,1)S(1)}, bf16[256,512]{1,0:T(8,128)(2,1)S(1)}, u32[]{:S(2)}, u32[]{:S(2)}) collective-permute-start(bf16[256,512]{1,0:T(8,128)(2,1)S(1)} %normalise.3.a), channel_id=1, source_target_pairs={{0,12},{4,8},{8,4},{12,0},{1,13},{5,9},{9,5},{13,1},{2,14},{6,10},... | collective-permute-start | bytes 786440 | tf_op jit(solution)/shard_map/ppermute | solution.py:35
  84.8 9.1 %collective-permute-start.17 = (bf16[256,512]{1,0:T(8,128)(2,1)S(1)}, bf16[256,512]{1,0:T(8,128)(2,1)S(1)}, u32[]{:S(2)}, u32[]{:S(2)}) collective-permute-start(bf16[256,512]{1,0:T(8,128)(2,1)S(1)} %normalise.3.a), channel_id=1, source_target_pairs={{0,4},{4,0},{8,12},{12,8},{1,5},{5,1},{9,13},{13,9},{2,6},{6,2},{1... | collective-permute-start | bytes 786440 | tf_op jit(solution)/shard_map/ppermute | solution.py:35
  96.0 9.8 %collective-permute-start.20 = (bf16[128,1024]{1,0:T(8,128)(2,1)S(1)}, bf16[128,1024]{1,0:T(8,128)(2,1)S(1)}, u32[]{:S(2)}, u32[]{:S(2)}) collective-permute-start(bf16[128,1024]{1,0:T(8,128)(2,1)S(1)} %get-tuple-element.48), channel_id=1, source_target_pairs={{0,4},{4,0},{8,12},{12,8},{1,5},{5,1},{9,13},{13,9},{2,6},{6,2},{1... | collective-permute-start | bytes 786440 | tf_op jit(solution)/shard_map/ppermute | solution.py:35
  97.0 9.2 %collective-permute-start.19 = (bf16[128,1024]{1,0:T(8,128)(2,1)S(1)}, bf16[128,1024]{1,0:T(8,128)(2,1)S(1)}, u32[]{:S(2)}, u32[]{:S(2)}) collective-permute-start(bf16[128,1024]{1,0:T(8,128)(2,1)S(1)} %get-tuple-element.47.after), channel_id=1, source_target_pairs={{0,12},{4,8},{8,4},{12,0},{1,13},{5,9},{9,5},{13,1},{2,14},{6,10},... | collective-permute-start | bytes 786440 | tf_op jit(solution)/shard_map/ppermute | solution.py:35
  98.1 13.6 %collective-permute-start.14 = (bf16[256,512]{1,0:T(8,128)(2,1)S(1)}, bf16[256,512]{1,0:T(8,128)(2,1)S(1)}, u32[]{:S(2)}, u32[]{:S(2)}) collective-permute-start(bf16[256,512]{1,0:T(8,128)(2,1)S(1)} %get-tuple-element.45), channel_id=1, source_target_pairs={{0,2},{1,3},{2,0},{3,1},{4,6},{5,7},{6,4},{7,5},{8,10},{9,11},{10,... | collective-permute-start | bytes 786440 | tf_op jit(solution)/shard_map/ppermute | solution.py:31
  100.4 20.0 %collective-permute-start.24 = (bf16[128,1024]{1,0:T(8,128)(2,1)S(1)}, bf16[128,1024]{1,0:T(8,128)(2,1)S(1)}, u32[]{:S(2)}, u32[]{:S(2)}) collective-permute-start(bf16[128,1024]{1,0:T(8,128)(2,1)S(1)} %get-tuple-element.53), channel_id=1, source_target_pairs={{0,12},{4,8},{8,4},{12,0},{1,13},{5,9},{9,5},{13,1},{2,14},{6,10},... | collective-permute-start | bytes 786440 | tf_op jit(solution)/shard_map/ppermute | solution.py:35
  101.3 19.1 %collective-permute-start.25 = (bf16[128,1024]{1,0:T(8,128)(2,1)S(1)}, bf16[128,1024]{1,0:T(8,128)(2,1)S(1)}, u32[]{:S(2)}, u32[]{:S(2)}) collective-permute-start(bf16[128,1024]{1,0:T(8,128)(2,1)S(1)} %get-tuple-element.54), channel_id=1, source_target_pairs={{0,4},{4,0},{8,12},{12,8},{1,5},{5,1},{9,13},{13,9},{2,6},{6,2},{1... | collective-permute-start | bytes 786440 | tf_op jit(solution)/shard_map/ppermute | solution.py:35
  107.5 12.9 %collective-permute-start.21 = (bf16[128,512]{1,0:T(8,128)(2,1)S(1)}, bf16[128,512]{1,0:T(8,128)(2,1)S(1)}, u32[]{:S(2)}, u32[]{:S(2)}) collective-permute-start(bf16[128,512]{1,0:T(8,128)(2,1)S(1)} %get-tuple-element.50), channel_id=1, source_target_pairs={{0,1},{1,2},{2,3},{3,0},{4,5},{5,6},{6,7},{7,4},{8,9},{9,10},{10,1... | collective-permute-start | bytes 393224 | tf_op jit(solution)/shard_map/ppermute | solution.py:31
  110.8 9.5 %collective-permute-start.22 = (bf16[128,512]{1,0:T(8,128)(2,1)S(1)}, bf16[128,512]{1,0:T(8,128)(2,1)S(1)}, u32[]{:S(2)}, u32[]{:S(2)}) collective-permute-start(bf16[128,512]{1,0:T(8,128)(2,1)S(1)} %get-tuple-element.51), channel_id=1, source_target_pairs={{0,3},{1,0},{2,1},{3,2},{4,7},{5,4},{6,5},{7,6},{8,11},{9,8},{10,9... | collective-permute-start | bytes 393224 | tf_op jit(solution)/shard_map/ppermute | solution.py:31
  111.8 16.8 %collective-permute-start.23 = (bf16[128,512]{1,0:T(8,128)(2,1)S(1)}, bf16[128,512]{1,0:T(8,128)(2,1)S(1)}, u32[]{:S(2)}, u32[]{:S(2)}) collective-permute-start(bf16[128,512]{1,0:T(8,128)(2,1)S(1)} %get-tuple-element.52), channel_id=1, source_target_pairs={{0,2},{1,3},{2,0},{3,1},{4,6},{5,7},{6,4},{7,5},{8,10},{9,11},{10,... | collective-permute-start | bytes 393224 | tf_op jit(solution)/shard_map/ppermute | solution.py:31
  121.6 11.8 %collective-permute-start.26 = (bf16[128,512]{1,0:T(8,128)(2,1)S(1)}, bf16[128,512]{1,0:T(8,128)(2,1)S(1)}, u32[]{:S(2)}, u32[]{:S(2)}) collective-permute-start(bf16[128,512]{1,0:T(8,128)(2,1)S(1)} %get-tuple-element.56), channel_id=1, source_target_pairs={{0,1},{1,2},{2,3},{3,0},{4,5},{5,6},{6,7},{7,4},{8,9},{9,10},{10,1... | collective-permute-start | bytes 393224 | tf_op jit(solution)/shard_map/ppermute | solution.py:31
  124.4 14.7 %collective-permute-start.27 = (bf16[128,512]{1,0:T(8,128)(2,1)S(1)}, bf16[128,512]{1,0:T(8,128)(2,1)S(1)}, u32[]{:S(2)}, u32[]{:S(2)}) collective-permute-start(bf16[128,512]{1,0:T(8,128)(2,1)S(1)} %get-tuple-element.57), channel_id=1, source_target_pairs={{0,2},{1,3},{2,0},{3,1},{4,6},{5,7},{6,4},{7,5},{8,10},{9,11},{10,... | collective-permute-start | bytes 393224 | tf_op jit(solution)/shard_map/ppermute | solution.py:31
  128.6 10.5 %collective-permute-start.28 = (bf16[128,512]{1,0:T(8,128)(2,1)S(1)}, bf16[128,512]{1,0:T(8,128)(2,1)S(1)}, u32[]{:S(2)}, u32[]{:S(2)}) collective-permute-start(bf16[128,512]{1,0:T(8,128)(2,1)S(1)} %get-tuple-element.58), channel_id=1, source_target_pairs={{0,3},{1,0},{2,1},{3,2},{4,7},{5,4},{6,5},{7,6},{8,11},{9,8},{10,9... | collective-permute-start | bytes 393224 | tf_op jit(solution)/shard_map/ppermute | solution.py:31
  (5 other events, 4.0 us)
